TPU v7x, 256 devices: a whole 4x4x8 slice. The times are simulated.
256 devices in a mesh: group: 16 (over z, x_hi), fsdp: 16 (over y, x_lo, core).
Axes of the slice: x: 4 (x_hi: 2, x_lo: 2; x = x_hi * 2 + x_lo), y: 4, z: 8, core: 2. Of those that a mesh axis runs over, the one named last changes fastest.
Arguments:
- mol_qkv: bfloat16 [128, 128, 3, 4096], P('group', None, None, 'fsdp'), may hold values from -12 to 12
- pair_list: int32 [256, 3], replicated, may hold values from 0 to 15, as said below
- head_proj: bfloat16 [32, 128, 256], P('fsdp'), may hold values from -0.5 to 0.5
- head_out: float32 [32, 256], P('fsdp'), may hold values from -0.375 to 0.375
- labels: int32 [256], P('group'), may hold values 0 or 1
Outputs:
- mol_grad: bfloat16 [128, 128, 3, 4096], P('group', None, None, 'fsdp')
- pair_logits: float32 [256], P('group')
- mean_loss: float32 [], replicated
Inputs may be any that keep to these rules, and one draw needn't show every extreme that they name: `pair_list`: pair p belongs to owner p // 16; column 0 is the first molecule's index among the owner's 8 molecules, column 1 the group index that holds the second molecule, column 2 its index among that holder's 8 molecules; molecule m is held by group m // 8. `pair_list`: among one owner's pairs, at most 2 take their second molecule from any one holder, and those name at most 1 different molecules; every owner reaches both bounds.
All inputs are finite; a program needn't handle non-finite values. No bound on the sum of `labels` on one device may be relied on, other than what follows from the above.
Results may differ from a plain program's by a relative error of at most 0.0075.
Values may be sent and summed in bfloat16 or wider, within the bound.
No kernel may reach another device: no remote copies, remote signals or barrier semaphores. Data moves between devices by JAX's collectives and lax.ppermute only.
A program may use at most 128 MiB of HBM per device.

v0:
```python
import jax
import jax.numpy as jnp
from jax import lax
from jax.sharding import PartitionSpec as P

loss_scale = 8192.0


def split_heads(rows_in, component, heads, head_dim):
    return rows_in[:, :, component].reshape(rows_in.shape[0], rows_in.shape[1], heads, head_dim)


def forward(query_rows, key_rows, value_rows, head_proj, head_out, inv_root, length):
    scores = (
        jnp.einsum("plhd,pmhd->phlm", query_rows, key_rows, preferred_element_type=jnp.float32)
        * inv_root
    )
    row_max = jnp.max(scores, axis=-1, keepdims=True)
    lifted = jnp.exp(scores - row_max)
    attn_weights = lifted / jnp.sum(lifted, axis=-1, keepdims=True)
    weights_bf = attn_weights.astype(jnp.bfloat16)
    context = jnp.einsum(
        "phlm,pmhd->plhd", weights_bf, value_rows, preferred_element_type=jnp.float32
    ).astype(jnp.bfloat16)
    hidden = jnp.einsum("plhd,hdr->plhr", context, head_proj, preferred_element_type=jnp.float32)
    partial_value = jnp.sum(jax.nn.silu(hidden) * head_out[None, None], axis=(1, 2, 3)) / length
    return (partial_value, (attn_weights, weights_bf, hidden))


def backward(
    query_rows, key_rows, value_rows, head_proj, head_out, saved, grad_out, inv_root, length
):
    attn_weights, weights_bf, hidden = saved
    sigmoid_h = jax.nn.sigmoid(hidden)
    silu_slope = sigmoid_h * (1.0 + hidden * (1.0 - sigmoid_h))
    dhidden = (grad_out[:, None, None, None] / length * head_out[None, None] * silu_slope).astype(
        jnp.bfloat16
    )
    dcontext = jnp.einsum(
        "plhr,hdr->plhd", dhidden, head_proj, preferred_element_type=jnp.float32
    ).astype(jnp.bfloat16)
    dvalues = jnp.einsum(
        "phlm,plhd->pmhd", weights_bf, dcontext, preferred_element_type=jnp.float32
    )
    dweights = jnp.einsum(
        "plhd,pmhd->phlm", dcontext, value_rows, preferred_element_type=jnp.float32
    )
    dscores = (
        attn_weights
        * (dweights - jnp.sum(dweights * attn_weights, axis=-1, keepdims=True))
        * inv_root
    ).astype(jnp.bfloat16)
    dqueries = jnp.einsum("phlm,pmhd->plhd", dscores, key_rows, preferred_element_type=jnp.float32)
    dkey_rows = jnp.einsum(
        "phlm,plhd->pmhd", dscores, query_rows, preferred_element_type=jnp.float32
    )
    return (dqueries, dkey_rows, dvalues)


def routing(blocks, mol_count, capacity, device):
    groups, per_owner, _ = blocks.shape
    holder = blocks[:, :, 1]
    member = blocks[:, :, 2]
    position = jnp.arange(per_owner, dtype=jnp.int32)
    mol_key = holder * mol_count + member
    matches = mol_key[:, :, None] == mol_key[:, None, :]
    earlier = matches & (position[None, None, :] < position[None, :, None])
    leading = jnp.logical_not(jnp.any(earlier, axis=2))
    leader = jnp.argmax(matches, axis=2)
    owns_slot = jnp.ones_like(leading)
    per_holder = (
        (holder[:, :, None] == jnp.arange(groups, dtype=jnp.int32)[None, None, :])
        & owns_slot[:, :, None]
    ).astype(jnp.int32)
    rank_all = jnp.cumsum(per_holder, axis=1) - per_holder
    rank_in = jnp.take_along_axis(rank_all, holder[:, :, None], axis=2)[:, :, 0]
    slot_index = holder * capacity + rank_in
    return_slot = jnp.take_along_axis(slot_index, leader, axis=1)
    to_device = owns_slot & (holder == device)
    picked = to_device[:, :, None] & (
        rank_in[:, :, None] == jnp.arange(capacity, dtype=jnp.int32)[None, None, :]
    )
    send_member = jnp.sum(picked.astype(jnp.int32) * member[:, :, None], axis=1)
    send_valid = jnp.any(picked, axis=1)
    return (slot_index, return_slot, send_member, send_valid)


def local(mol_qkv, pair_list, head_proj, head_out, labels):
    groups = lax.axis_size("group")
    device = lax.axis_index("group")
    mol_count, length, _, row_width = mol_qkv.shape
    heads_here, head_dim, inner_width = head_proj.shape
    total_pairs = pair_list.shape[0]
    per_owner = total_pairs // groups
    inv_root = head_dim ** (-0.5)
    blocks = pair_list.reshape(groups, per_owner, 3)
    capacity = 2 * per_owner // groups
    fetch_slot, return_slot, send_member, send_valid = routing(blocks, mol_count, capacity, device)
    slots_all = groups * capacity
    flat_member = send_member.reshape(slots_all)
    flat_valid = send_valid.reshape(slots_all)
    outgoing = jnp.take(mol_qkv, flat_member, axis=0)
    outgoing = jnp.where(flat_valid[:, None, None, None], outgoing, jnp.zeros_like(outgoing))
    incoming = lax.all_to_all(outgoing, "group", split_axis=0, concat_axis=0, tiled=True)
    my_pairs = lax.dynamic_index_in_dim(blocks, device, 0, keepdims=False)
    my_fetch = lax.dynamic_index_in_dim(fetch_slot, device, 0, keepdims=False)
    my_return = lax.dynamic_index_in_dim(return_slot, device, 0, keepdims=False)
    partner_rows = jnp.take(incoming, my_fetch, axis=0)
    own_rows = jnp.take(mol_qkv, my_pairs[:, 0], axis=0)
    qa, ka, va = [split_heads(own_rows, c, heads_here, head_dim) for c in range(3)]
    qb, kb, vb = [split_heads(partner_rows, c, heads_here, head_dim) for c in range(3)]
    part_ab, saved_ab = forward(qa, kb, vb, head_proj, head_out, inv_root, length)
    part_ba, saved_ba = forward(qb, ka, va, head_proj, head_out, inv_root, length)
    logits = lax.psum(part_ab + part_ba, "fsdp")
    targets = labels.astype(jnp.float32)
    loss_terms = jax.nn.softplus(logits) - targets * logits
    loss_sum = lax.psum(jnp.sum(loss_terms), "group")
    mean_loss = loss_sum / total_pairs
    grad_out = (jax.nn.sigmoid(logits) - targets) * loss_scale
    dq_a, dk_b, dv_b = backward(
        qa, kb, vb, head_proj, head_out, saved_ab, grad_out, inv_root, length
    )
    dq_b, dk_a, dv_a = backward(
        qb, ka, va, head_proj, head_out, saved_ba, grad_out, inv_root, length
    )
    grad_first = jnp.stack([dq_a, dk_a, dv_a], axis=2).reshape(per_owner, -1)
    grad_second = jnp.stack([dq_b, dk_b, dv_b], axis=2).reshape(per_owner, -1)
    own_pick = (my_pairs[:, 0][None, :] == jnp.arange(mol_count, dtype=jnp.int32)[:, None]).astype(
        jnp.float32
    )
    own_sum = jnp.dot(
        own_pick, grad_first, precision=lax.Precision.HIGHEST, preferred_element_type=jnp.float32
    )
    back_pick = (my_return[None, :] == jnp.arange(slots_all, dtype=jnp.int32)[:, None]).astype(
        jnp.float32
    )
    outgoing_grad = jnp.dot(
        back_pick, grad_second, precision=lax.Precision.HIGHEST, preferred_element_type=jnp.float32
    )
    outgoing_grad = outgoing_grad.astype(jnp.bfloat16).reshape(slots_all, length, 3, row_width)
    returned = lax.all_to_all(outgoing_grad, "group", split_axis=0, concat_axis=0, tiled=True)
    land_pick = (
        (flat_member[None, :] == jnp.arange(mol_count, dtype=jnp.int32)[:, None])
        & flat_valid[None, :]
    ).astype(jnp.bfloat16)
    partner_sum = jnp.dot(
        land_pick, returned.reshape(slots_all, -1), preferred_element_type=jnp.float32
    )
    mol_grad = (own_sum + partner_sum).astype(jnp.bfloat16).reshape(mol_qkv.shape)
    return (mol_grad, logits, mean_loss)


def solution(mesh):
    placed = (
        P("group", None, None, "fsdp"),
        P(),
        P("fsdp", None, None),
        P("fsdp", None),
        P("group"),
    )
    return jax.shard_map(
        local,
        mesh=mesh,
        in_specs=placed,
        out_specs=(P("group", None, None, "fsdp"), P("group"), P()),
        check_vma=False,
    )
```

profile of v0, /device:TPU:8, one launch (start us, length us, event | category | flops | bytes accessed | tf_op | source)
XLA Modules:
  0.0 569.2 jit_solution(3673725026989699490)
XLA Ops:
  1.9 2.4 gather_fusion.3
  5.1 3.6 gather_fusion
  8.7 6.2 %select_select_fusion = bf16[32,128,3,256]{3,1,2,0:T(8,128)(2,1)} fusion(bf16[32,128,3,256]{3,1,2,0:T(8,128)(2,1)} %gather_fusion, pred[32]{0:T(512)(128)(4,1)S(1)} %compare_and_fusion, pred[32]{0:T(512)(128)(4,1)S(1)} %broadcast_in_dim.72), kind=kLoop, calls=%fused_computation.14 | loop fusion | flops 6291456 | bytes 12582976 | tf_op jit(solution)/shard_map/jit(_where)/select_n | solution.py:103
  14.9 11.1 %all-to-all-start = ((bf16[32,128,3,256]{3,1,2,0:T(8,128)(2,1)}), bf16[32,128,3,256]{3,1,2,0:T(8,128)(2,1)}, u32[]{:S(2)}, u32[]{:S(2)}) async-start(bf16[32,128,3,256]{3,1,2,0:T(8,128)(2,1)} %select_select_fusion), calls=%async_computation | async-start | bytes 12582912 | tf_op jit(solution)/shard_map/all_to_all | solution.py:104
  26.0 1.5 iota_reduce_fusion
  27.6 1.9 gather_fusion.4
  29.7 2.4 gather_fusion.2
  32.1 2.2 broadcast_select_fusion
  34.4 1.7 fusion.142
  36.7 1.6 copy.124
  38.3 2.3 copy.122
  40.7 132.1 %all-to-all-done = bf16[32,128,3,256]{3,1,2,0:T(8,128)(2,1)} async-done(((bf16[32,128,3,256]{3,1,2,0:T(8,128)(2,1)}), bf16[32,128,3,256]{3,1,2,0:T(8,128)(2,1)}, u32[]{:S(2)}, u32[]{:S(2)}) %all-to-all-start) | async-done | bytes 6291488 | tf_op jit(solution)/shard_map/all_to_all | solution.py:104
  172.8 5.2 gather_fusion.1
  178.0 2.2 broadcast_select_fusion.1
  180.3 1.8 fusion.141
  182.1 2.3 copy.118
  184.4 2.3 copy.123
  186.7 2.3 copy.114
  189.0 3.5 fusion.144
  192.4 3.5 fusion.143
  195.9 5.0 fusion.66
  200.9 7.8 %fusion.9 = (f32[16]{0:T(128)S(1)}, f32[16]{0:T(128)S(1)}, f32[2,16,128,256]{3,2,1,0:T(8,128)}) fusion(f32[2,256]{1,0:T(2,128)S(1)} %copy-done.11, f32[2,16,128,256]{3,2,1,0:T(8,128)} %fusion.66, bf16[2,128,256]{2,1,0:T(8,128)(2,1)S(1)} %copy-done.14, bf16[16,128,2,128]{1,3,2,0:T(8,128)(2,1)} %bitcast.188, f32[16,2,128,128]{2,3,1,0:T(8,128)} %get-tuple-element.40, ...), kind=kOutput, calls=%fused_computation.22 | convolution fusion | flops 416808960 | bytes 11683968 | tf_op jit(solution)/shard_map/plhd,hdr->plhr/dot_general | solution.py:25
  208.7 22.6 %psum.14 = f32[16]{0:T(128)S(1)} all-reduce(f32[16]{0:T(128)S(1)} %add_multiply_fusion), channel_id=1, replica_groups=mesh['group'=16,'fsdp'=16] {'fsdp'}, use_global_device_ids=true, to_apply=%region_9.10 | all-reduce | flops 16 | bytes 128 | tf_op jit(solution)/shard_map/psum | solution.py:114
  231.9 3.9 fusion.69
  235.9 2.3 fusion.93
  238.2 2.2 convolution_bitcast_fusion
  241.1 1.6 fusion.72
  243.7 2.2 fusion.90
  245.9 5.6 fusion.50
  251.5 5.7 %fusion.56 = f32[16,128,1,2,128]{1,4,3,0,2:T(8,128)} fusion(bf16[16,128,2,128]{1,3,2,0:T(8,128)(2,1)S(1)} %bitcast.185, f32[16,2,128,128]{2,3,1,0:T(8,128)} %fusion.93, f32[16,2,128,128]{2,3,1,0:T(8,128)} %get-tuple-element.42, f32[16,2,128]{2,1,0:T(2,128)S(1)} %get-tuple-element.41), kind=kOutput, calls=%fused_computation.62 | convolution fusion | flops 137891968 | bytes 7356416 | tf_op jit(solution)/shard_map/phlm,plhd->pmhd/dot_general | solution.py:54
  257.3 6.3 %pad_maximum_fusion.1 = f32[16,128,3,2,128]{1,4,3,0,2:T(8,128)} fusion(f32[16,128,1,2,128]{1,4,3,0,2:T(8,128)} %convolution_bitcast_fusion, f32[16,128,1,2,128]{1,4,3,0,2:T(8,128)} %fusion.56, f32[16,128,1,2,128]{1,4,3,0,2:T(8,128)} %fusion.50), kind=kLoop, calls=%fused_computation.13 | loop fusion | flops 3145728 | bytes 12582912 | tf_op jit(solution)/shard_map/stack | solution.py:127
  263.6 10.3 %copy.143 = f32[16,128,3,2,128]{4,3,2,1,0:T(2,128)} copy(f32[16,128,3,2,128]{1,4,3,0,2:T(8,128)} %pad_maximum_fusion.1) | data formatting | bytes 12582912 | tf_op jit(solution)/shard_map/stack | solution.py:127
  273.9 8.6 %reshape.161 = f32[16,98304]{1,0:T(8,128)} reshape(f32[16,128,3,2,128]{4,3,2,1,0:T(2,128)} %copy.143) | data formatting | bytes 12582912 | tf_op jit(solution)/shard_map/reshape | solution.py:127
  282.6 11.3 %convolution_convert_fusion = bf16[32,98304]{1,0:T(8,128)(2,1)} fusion(f32[16,98304]{1,0:T(8,128)} %reshape.161, s32[16]{0:T(128)S(1)} %fusion.125), kind=kOutput, calls=%fused_computation.9 | convolution fusion | flops 607126016 | bytes 12582976 | tf_op jit(solution)/shard_map/dot_general | solution.py:137
  293.8 11.7 %reshape.162 = bf16[32,128,3,256]{3,2,1,0:T(4,128)(2,1)} reshape(bf16[32,98304]{1,0:T(8,128)(2,1)} %convolution_convert_fusion) | data formatting | bytes 12582912 | tf_op jit(solution)/shard_map/reshape | solution.py:140
  305.5 7.5 %copy.144 = bf16[32,128,3,256]{3,1,2,0:T(8,128)(2,1)} copy(bf16[32,128,3,256]{3,2,1,0:T(4,128)(2,1)} %reshape.162) | data formatting | bytes 12582912 | tf_op jit(solution)/shard_map/reshape | solution.py:140
  313.0 6.1 %all-to-all-start.1 = ((bf16[32,128,3,256]{3,1,2,0:T(8,128)(2,1)}), bf16[32,128,3,256]{3,1,2,0:T(8,128)(2,1)}, u32[]{:S(2)}, u32[]{:S(2)}) async-start(bf16[32,128,3,256]{3,1,2,0:T(8,128)(2,1)} %copy.144), calls=%async_computation.1 | async-start | bytes 12582912 | tf_op jit(solution)/shard_map/all_to_all | solution.py:141
  319.0 176.0 %psum.15 = f32[]{:T(128)} all-reduce(f32[]{:T(128)} %get-tuple-element.37), channel_id=1, replica_groups=mesh['group'=16,'fsdp'=16] {'group'}, use_global_device_ids=true, to_apply=%region_14.15 | all-reduce | flops 1 | bytes 8 | tf_op jit(solution)/shard_map/psum | solution.py:117
  495.1 5.8 %fusion.47 = f32[16,128,1,2,128]{1,4,3,0,2:T(8,128)} fusion(bf16[16,128,2,128]{1,3,2,0:T(8,128)(2,1)S(1)} %bitcast.191, f32[16,2,128,128]{2,3,1,0:T(8,128)} %fusion.90, f32[16,2,128,128]{2,3,1,0:T(8,128)} %get-tuple-element.40, f32[16,2,128]{2,1,0:T(2,128)S(1)} %get-tuple-element.39), kind=kOutput, calls=%fused_computation.59 | convolution fusion | flops 137891968 | bytes 7356416 | tf_op jit(solution)/shard_map/phlm,plhd->pmhd/dot_general | solution.py:54
  500.9 5.7 fusion.53
  506.6 2.6 convolution_bitcast_fusion.1
  509.4 3.1 pad_maximum_fusion
  512.5 10.3 %copy.138 = f32[16,128,3,2,128]{4,3,2,1,0:T(2,128)} copy(f32[16,128,3,2,128]{1,4,3,0,2:T(8,128)} %pad_maximum_fusion) | data formatting | bytes 12582912 | tf_op jit(solution)/shard_map/stack | solution.py:126
  522.8 8.8 %reshape.159 = f32[16,98304]{1,0:T(8,128)} reshape(f32[16,128,3,2,128]{4,3,2,1,0:T(2,128)} %copy.138) | data formatting | bytes 12582912 | tf_op jit(solution)/shard_map/reshape | solution.py:126
  532.3 6.8 %fusion.110 = f32[8,98304]{1,0:T(8,128)} fusion(f32[16,98304]{1,0:T(8,128)} %reshape.159, s32[16]{0:T(128)S(1)} %get-tuple-element.35), kind=kOutput, calls=%fused_computation.134 | convolution fusion | flops 150995072 | bytes 9437248 | tf_op jit(solution)/shard_map/dot_general | solution.py:131
  539.1 12.0 %copy.145 = bf16[32,128,3,256]{3,2,1,0:T(4,128)(2,1)} copy(bf16[32,128,3,256]{3,1,2,0:T(8,128)(2,1)} %all-to-all-done.1) | data formatting | bytes 12582912 | tf_op jit(solution)/shard_map/all_to_all | solution.py:141
  551.1 10.5 %reshape.163 = bf16[32,98304]{1,0:T(8,128)(2,1)} reshape(bf16[32,128,3,256]{3,2,1,0:T(4,128)(2,1)} %copy.145) | data formatting | bytes 12582912 | tf_op jit(solution)/shard_map/reshape | solution.py:147
  561.6 4.8 fusion.4
  (73 shorter events, 7.1 us)
Async XLA Ops:
  0.6 4.5 copy-start
  14.9 157.9 %all-to-all-start = ((bf16[32,128,3,256]{3,1,2,0:T(8,128)(2,1)}), bf16[32,128,3,256]{3,1,2,0:T(8,128)(2,1)}, u32[]{:S(2)}, u32[]{:S(2)}) async-start(bf16[32,128,3,256]{3,1,2,0:T(8,128)(2,1)} %select_select_fusion), calls=%async_computation | async-start | bytes 12582912 | tf_op jit(solution)/shard_map/all_to_all | solution.py:104
  192.4 3.5 copy-start.14
  195.9 5.0 copy-start.11
  200.9 30.4 %copy-start.12 = (s32[16]{0:T(128)S(1)}, s32[16]{0:T(128)}, u32[]{:S(2)}) copy-start(s32[16]{0:T(128)} %param.9) | copy-start | bytes 196
  231.3 4.6 copy-start.13
  231.9 3.9 copy-start.5
  235.9 2.3 copy-start.6
  238.2 2.9 copy-start.15
  241.1 2.6 copy-start.2
  242.7 1.0 copy-start.9
  313.0 182.1 %copy-start.3 = (bf16[16,128,1,256]{1,3,0,2:T(8,128)(2,1)S(1)}, bf16[16,128,1,256]{1,3,0,2:T(8,128)(2,1)}, u32[]{:S(2)}) copy-start(bf16[16,128,1,256]{1,3,0,2:T(8,128)(2,1)} %copy.123) | copy-start | bytes 3145732
  313.0 226.1 %all-to-all-start.1 = ((bf16[32,128,3,256]{3,1,2,0:T(8,128)(2,1)}), bf16[32,128,3,256]{3,1,2,0:T(8,128)(2,1)}, u32[]{:S(2)}, u32[]{:S(2)}) async-start(bf16[32,128,3,256]{3,1,2,0:T(8,128)(2,1)} %copy.144), calls=%async_computation.1 | async-start | bytes 12582912 | tf_op jit(solution)/shard_map/all_to_all | solution.py:141
  495.1 5.8 %copy-start.4 = (bf16[16,128,1,256]{1,3,0,2:T(8,128)(2,1)S(1)}, bf16[16,128,1,256]{1,3,0,2:T(8,128)(2,1)}, u32[]{:S(2)}) copy-start(bf16[16,128,1,256]{1,3,0,2:T(8,128)(2,1)} %copy.114) | copy-start | bytes 3145732
  500.9 5.7 %copy-start.10 = (bf16[16,128,2,128]{3,1,0,2:T(8,128)(2,1)S(1)}, bf16[16,128,2,128]{3,1,0,2:T(8,128)(2,1)}, u32[]{:S(2)}) copy-start(bf16[16,128,2,128]{3,1,0,2:T(8,128)(2,1)} %copy-done.9) | copy-start | bytes 3145732
  506.6 2.6 copy-start.7
  506.6 2.9 copy-start.8
  561.6 6.3 %copy-start.1 = (bf16[8,128,3,256]{3,1,2,0:T(8,128)(2,1)S(1)}, bf16[8,128,3,256]{3,1,2,0:T(8,128)(2,1)}, u32[]{:S(2)}) copy-start(bf16[8,128,3,256]{3,1,2,0:T(8,128)(2,1)} %param.5) | copy-start | bytes 4718596
where the time goes:
time: 574 us; the launch traced here: 569 us
  blocking collectives  199 us (35%)
  waiting for transfers between devices  132 us (23%)
  local copies, waits for them, and re-layouts  115 us (20%)
  matrix products  80.2 us (14%)
  other arithmetic  22.8 us (4%)
  starting transfers between devices  17.1 us (3%)
    psum x1, blocking collectives, local(): loss_sum = lax.psum(jnp.sum(loss_terms), 'group')  176 us
    all_to_all x1, waiting for transfers between devices, local(): lax.all_to_all(outgoing, 'group', split_axis=0, concat_axis=0, tiled=True)  132 us
    psum x1, blocking collectives, local(): logits = lax.psum(part_ab + part_ba, 'fsdp')  22.6 us
    reshape x2, local copies, waits for them, and re-layouts, local(): outgoing_grad.astype(jnp.bfloat16).reshape(slots_all, length, 3, row_width)  19.2 us
    slice x8, local copies, waits for them, and re-layouts, split_heads(): rows_in[:, :, component]  14.9 us
    dot_general x2, matrix products, forward(): jnp.einsum('plhd,hdr->plhr', context, head_proj, preferred_element_type=j...  12.7 us
    all_to_all x1, local copies, waits for them, and re-layouts, local(): lax.all_to_all(outgoing_grad, 'group', split_axis=0, concat_axis=0, tiled...  12 us
    dot_general x2, matrix products, backward(): jnp.einsum('phlm,plhd->pmhd', dscores, query_rows, preferred_element_type...  11.5 us
  transfers between devices with their start and end apart: 2, of which 1 were waited for; matrix products, arithmetic and copies ran while one was open for 10% of the time, Pallas kernels for 0%

commit v1 on v0

v1 whole, which is shorter than its diff:
```python
import functools

import jax
import jax.numpy as jnp
from jax import lax
from jax.experimental import pallas as pl
from jax.experimental.pallas import tpu as pltpu
from jax.sharding import PartitionSpec as P

loss_scale = 8192.0
VMEM_BYTES = 48 * 1024 * 1024
F32 = jnp.float32
BF16 = jnp.bfloat16
SMEM_SPEC = pl.BlockSpec(memory_space=pltpu.SMEM)
VMEM_SPEC = pl.BlockSpec(memory_space=pltpu.VMEM)
ANY_SPEC = pl.BlockSpec(memory_space=pl.ANY)


def params():
    return pltpu.CompilerParams(vmem_limit_bytes=VMEM_BYTES)


def mm(a, b, ca, cb):
    return lax.dot_general(a, b, (((ca,), (cb,)), ((), ())), preferred_element_type=F32)


def pick_kernel(head, hd, member_ref, mol_ref, out_ref, sems):
    slots = out_ref.shape[0]
    copies = []
    for s in range(slots):
        copies.append(
            pltpu.make_async_copy(
                mol_ref.at[member_ref[s], :, :, pl.ds(head * hd, hd)], out_ref.at[s], sems.at[s]
            )
        )
    for c in copies:
        c.start()
    for c in copies:
        c.wait()


def pick(member, mol, head, hd):
    slots = member.shape[0]
    _, parts, length, _ = mol.shape
    return pl.pallas_call(
        functools.partial(pick_kernel, head, hd),
        out_shape=jax.ShapeDtypeStruct((slots, parts, length, hd), mol.dtype),
        in_specs=[SMEM_SPEC, ANY_SPEC],
        out_specs=ANY_SPEC,
        scratch_shapes=[pltpu.SemaphoreType.DMA((slots,))],
        compiler_params=params(),
        name="pick_rows",
    )(member, mol)


def pair_kernel(group, inv_root, first_ref, slot_ref, mol_ref, inc_ref, proj_ref, out_w_ref, prev_ref, gf_ref, gs_ref, lp_ref):
    pairs = gf_ref.shape[0]
    length = gf_ref.shape[2]
    proj = proj_ref[0]
    readout = out_w_ref[...] * (1.0 / length)

    def step(i, carry):
        units = []
        ids = []
        for j in range(group):
            p = i * group + j
            a = first_ref[p]
            s = slot_ref[p]
            ids.append(p)
            units.append((mol_ref[a, 0], inc_ref[s, 1], inc_ref[s, 2]))
            units.append((inc_ref[s, 0], mol_ref[a, 1], mol_ref[a, 2]))
        scores = [mm(q, k, 1, 1) for q, k, _ in units]
        weights = []
        for sc in scores:
            top = jnp.max(sc, axis=1, keepdims=True)
            lifted = jnp.exp((sc - top) * inv_root)
            weights.append(lifted * (1.0 / jnp.sum(lifted, axis=1, keepdims=True)))
        weights_bf = [w.astype(BF16) for w in weights]
        context = jnp.concatenate(
            [mm(w, u[2], 1, 0).astype(BF16) for w, u in zip(weights_bf, units)], axis=0
        )
        hidden = mm(context, proj, 1, 0)
        sig = 0.5 + 0.5 * jnp.tanh(0.5 * hidden)
        act = hidden * sig
        slope = sig + act * (1.0 - sig)
        dhidden = (slope * readout).astype(BF16)
        for j, p in enumerate(ids):
            rows = jnp.sum(act[2 * j * length : (2 * j + 2) * length], axis=0, keepdims=True)
            total = jnp.sum(rows * readout, axis=1, keepdims=True)
            lp_ref[pl.ds(p, 1), :] = prev_ref[pl.ds(p, 1), :] + jnp.broadcast_to(total, (1, lp_ref.shape[1]))
        dcontext_all = mm(dhidden, proj, 1, 1).astype(BF16)
        dcontext = [dcontext_all[n * length : (n + 1) * length] for n in range(len(units))]
        dvalues = [mm(w, d, 0, 0) for w, d in zip(weights_bf, dcontext)]
        dweights = [mm(d, u[2], 1, 1) for d, u in zip(dcontext, units)]
        dscores = []
        for w, dw in zip(weights, dweights):
            inner = jnp.sum(dw * w, axis=1, keepdims=True)
            dscores.append((w * (dw - inner) * inv_root).astype(BF16))
        dqueries = [mm(d, u[1], 1, 0) for d, u in zip(dscores, units)]
        dkeys = [mm(d, u[0], 0, 0) for d, u in zip(dscores, units)]
        for j, p in enumerate(ids):
            ab, ba = 2 * j, 2 * j + 1
            gf_ref[p, 0] = dqueries[ab].astype(BF16)
            gf_ref[p, 1] = dkeys[ba].astype(BF16)
            gf_ref[p, 2] = dvalues[ba].astype(BF16)
            gs_ref[p, 0] = dqueries[ba].astype(BF16)
            gs_ref[p, 1] = dkeys[ab].astype(BF16)
            gs_ref[p, 2] = dvalues[ab].astype(BF16)
        return carry

    lax.fori_loop(0, pairs // group, step, 0)


def pair_grads(first, slot, mol, inc, proj, readout, prev, head, hd):
    pairs = first.shape[0]
    mols, parts, length, _ = mol.shape
    grad_shape = jax.ShapeDtypeStruct((pairs, parts, length, hd), BF16)
    width = proj.shape[2]
    return pl.pallas_call(
        functools.partial(pair_kernel, 2, hd ** (-0.5)),
        grid=(1,),
        out_shape=(grad_shape, grad_shape, jax.ShapeDtypeStruct((pairs, 128), F32)),
        in_specs=[
            SMEM_SPEC,
            SMEM_SPEC,
            pl.BlockSpec((mols, parts, length, hd), lambda i: (0, 0, 0, head)),
            VMEM_SPEC,
            pl.BlockSpec((1, hd, width), lambda i: (head, 0, 0)),
            VMEM_SPEC,
            VMEM_SPEC,
        ],
        out_specs=(VMEM_SPEC, VMEM_SPEC, VMEM_SPEC),
        compiler_params=params(),
        name="pair_grads",
    )(first, slot, mol, inc, proj, readout, prev)


def grad_scale(logits, target):
    return (0.5 + 0.5 * jnp.tanh(0.5 * logits) - target) * loss_scale


def second_kernel(slot_ref, lead_ref, mate_ref, logits_ref, target_ref, gs_ref, out_ref, scale_ref):
    pairs, parts = gs_ref.shape[:2]
    scale_ref[...] = grad_scale(logits_ref[...], target_ref[...])

    def step(p, carry):
        slot = slot_ref[p]
        mate = mate_ref[p]
        own = scale_ref[pl.ds(p, 1), :]

        @pl.when((lead_ref[p] == 1) & (mate < 0))
        def single():
            for c in range(parts):
                out_ref[slot, c] = (own * gs_ref[p, c].astype(F32)).astype(BF16)

        @pl.when((lead_ref[p] == 1) & (mate >= 0))
        def double():
            other_at = jnp.maximum(mate, 0)
            other = scale_ref[pl.ds(other_at, 1), :]
            for c in range(parts):
                out_ref[slot, c] = (
                    own * gs_ref[p, c].astype(F32) + other * gs_ref[other_at, c].astype(F32)
                ).astype(BF16)

        return carry

    lax.fori_loop(0, pairs, step, 0)


def second_terms(slot, lead, mate, logits, target, gs, slots):
    pairs, parts, length, hd = gs.shape
    return pl.pallas_call(
        second_kernel,
        out_shape=jax.ShapeDtypeStruct((slots, parts, length, hd), BF16),
        in_specs=[SMEM_SPEC] * 3 + [VMEM_SPEC] * 3,
        out_specs=VMEM_SPEC,
        scratch_shapes=[pltpu.VMEM(logits.shape, F32)],
        compiler_params=params(),
        name="second_terms",
    )(slot, lead, mate, logits, target, gs)


def first_kernel(first_ref, logits_ref, target_ref, gf_ref, own_ref, scale_ref):
    pairs, parts = gf_ref.shape[:2]
    scale_ref[...] = grad_scale(logits_ref[...], target_ref[...])
    own_ref[...] = jnp.zeros_like(own_ref)

    def step(p, carry):
        a = first_ref[p]
        own = scale_ref[pl.ds(p, 1), :]
        for c in range(parts):
            own_ref[a, c] += own * gf_ref[p, c].astype(F32)
        return carry

    lax.fori_loop(0, pairs, step, 0)


def first_terms(first, logits, target, gf, mols):
    pairs, parts, length, hd = gf.shape
    return pl.pallas_call(
        first_kernel,
        out_shape=jax.ShapeDtypeStruct((mols, parts, length, hd), F32),
        in_specs=[SMEM_SPEC] + [VMEM_SPEC] * 3,
        out_specs=VMEM_SPEC,
        scratch_shapes=[pltpu.VMEM(logits.shape, F32)],
        compiler_params=params(),
        name="first_terms",
    )(first, logits, target, gf)


def add_returned(code_ref, back_ref, sum_ref):
    slots, parts = back_ref.shape[:2]

    def step(s, carry):
        m = code_ref[s]

        @pl.when(m >= 0)
        def add():
            at = jnp.maximum(m, 0)
            for c in range(parts):
                sum_ref[at, c] += back_ref[s, c].astype(F32)

        return carry

    lax.fori_loop(0, slots, step, 0)


def finish_kernel(code_ref, back_ref, own_ref, out_ref, sum_ref):
    sum_ref[...] = own_ref[...]
    add_returned(code_ref, back_ref, sum_ref)
    out_ref[...] = sum_ref[...].astype(BF16)


def finish(code, back, own):
    mols, parts, length, hd = own.shape
    return pl.pallas_call(
        finish_kernel,
        out_shape=jax.ShapeDtypeStruct((mols, parts, length, hd), BF16),
        in_specs=[SMEM_SPEC, VMEM_SPEC, VMEM_SPEC],
        out_specs=VMEM_SPEC,
        scratch_shapes=[pltpu.VMEM(own.shape, F32)],
        compiler_params=params(),
        name="finish_head",
    )(code, back, own)


def finish_last_kernel(code_ref, back_ref, own_ref, earlier_ref, out_ref, sum_ref):
    hd = own_ref.shape[3]
    sum_ref[...] = own_ref[...]
    add_returned(code_ref, back_ref, sum_ref)
    out_ref[:, :, :, :hd] = earlier_ref[...]
    out_ref[:, :, :, hd:] = sum_ref[...].astype(BF16)


def finish_last(code, back, own, earlier):
    mols, parts, length, hd = own.shape
    return pl.pallas_call(
        finish_last_kernel,
        out_shape=jax.ShapeDtypeStruct((mols, parts, length, 2 * hd), BF16),
        in_specs=[SMEM_SPEC, VMEM_SPEC, VMEM_SPEC, VMEM_SPEC],
        out_specs=VMEM_SPEC,
        scratch_shapes=[pltpu.VMEM(own.shape, F32)],
        compiler_params=params(),
        name="finish_last_head",
    )(code, back, own, earlier)


def butterfly(value, axis, size):
    hop = 1
    while hop < size:
        value = value + lax.ppermute(value, axis, [(i, i ^ hop) for i in range(size)])
        hop *= 2
    return value


def exchange(value):
    return lax.all_to_all(value, "group", split_axis=0, concat_axis=0, tiled=True)


def local(mol_qkv, pair_list, head_proj, head_out, labels):
    groups = lax.axis_size("group")
    shards = lax.axis_size("fsdp")
    device = lax.axis_index("group")
    mols = mol_qkv.shape[0]
    hd = head_proj.shape[1]
    total_pairs = pair_list.shape[0]
    pairs = total_pairs // groups
    mol = jnp.transpose(mol_qkv, (0, 2, 1, 3))

    blocks = pair_list.T.reshape(3, groups, pairs)
    code = jnp.max(jnp.where(blocks[1] == device, blocks[2], -1), axis=1)
    member = jnp.maximum(code, 0)
    mine = lax.dynamic_index_in_dim(blocks, device, 1, keepdims=False)
    first, slot = mine[0], mine[1]
    place = jnp.arange(pairs, dtype=jnp.int32)
    same = slot[:, None] == slot[None, :]
    lead = jnp.logical_not(jnp.any(same & (place[None, :] < place[:, None]), axis=1)).astype(jnp.int32)
    mate = jnp.max(jnp.where(same & (place[None, :] > place[:, None]), place[None, :], -1), axis=1)

    inc0 = exchange(pick(member, mol, 0, hd))
    inc1 = exchange(pick(member, mol, 1, hd))
    none = jnp.zeros((pairs, 128), F32)
    gf0, gs0, part0 = pair_grads(first, slot, mol, inc0, head_proj, head_out[0:1], none, 0, hd)
    gf1, gs1, part1 = pair_grads(first, slot, mol, inc1, head_proj, head_out[1:2], part0, 1, hd)
    logits_wide = butterfly(part1, "fsdp", shards)
    targets = labels.astype(F32)
    target_wide = jnp.broadcast_to(targets[:, None], logits_wide.shape)

    out0 = second_terms(slot, lead, mate, logits_wide, target_wide, gs0, groups)
    out1 = second_terms(slot, lead, mate, logits_wide, target_wide, gs1, groups)
    back0 = exchange(out0)
    back1 = exchange(out1)
    own0 = first_terms(first, logits_wide, target_wide, gf0, mols)
    own1 = first_terms(first, logits_wide, target_wide, gf1, mols)

    logits = logits_wide[:, 0]
    loss_terms = jax.nn.softplus(logits) - targets * logits
    mean_loss = butterfly(jnp.sum(loss_terms), "group", groups) / total_pairs

    half = finish(code, back0, own0)
    grads = finish_last(code, back1, own1, half)
    mol_grad = jnp.transpose(grads, (0, 2, 1, 3))
    return (mol_grad, logits, mean_loss)


def solution(mesh):
    placed = (
        P("group", None, None, "fsdp"),
        P(),
        P("fsdp", None, None),
        P("fsdp", None),
        P("group"),
    )
    return jax.shard_map(
        local,
        mesh=mesh,
        in_specs=placed,
        out_specs=(P("group", None, None, "fsdp"), P("group"), P()),
        check_vma=False,
    )
```

time: 574 us -> 238 us (0.41)
  blocking collectives: 199 us -> 0 us
  local copies, waits for them, and re-layouts: 115 us -> 13.7 us
  matrix products: 80.2 us -> 0 us
  Pallas kernels: 0 us -> 39.9 us
  starting transfers between devices: 17.1 us -> 56.2 us
  other arithmetic: 22.8 us -> 1.91 us
  waiting for transfers between devices: 132 us -> 120 us
    psum x2 -> x0, blocking collectives: 199 us -> none  [the longest x1 176 us: local(): loss_sum = lax.psum(jnp.sum(loss_terms), 'group')]
    dot_general x15 -> x0, matrix products: 73.3 us -> none  [the longest x2 12.7 us: forward(): jnp.einsum('plhd,hdr->plhr', context, head_proj, preferred_element_type=j...]
    reshape x8 -> x1, local copies, waits for them, and re-layouts: 48.2 us -> 0.08 us  [local(): blocks = pair_list.T.reshape(3, groups, pairs)]
    pallas_call x0 -> x10, Pallas kernels: none -> 39.9 us  [the longest x2 25.8 us: pair_grads(): pl.pallas_call(functools.partial(pair_kernel, 2, hd ** (-0.5)), grid=(1,)...]
    ppermute x0 -> x8, starting transfers between devices: none -> 33 us  [butterfly(): lax.ppermute(value, axis, [(i, i ^ hop) for i in range(size)])]
    all_to_all x2 -> x4, waiting for transfers between devices: 132 us -> 101 us  [exchange(): lax.all_to_all(value, 'group', split_axis=0, concat_axis=0, tiled=True)]
    another operation x2 -> x0, local copies, waits for them, and re-layouts: 20.6 us -> none  [the longest x1 10.3 us: local(): grad_second = jnp.stack([dq_b, dk_b, dv_b], axis=2).reshape(per_owner, -1)]
    ppermute x0 -> x8, waiting for transfers between devices: none -> 19.6 us  [butterfly(): lax.ppermute(value, axis, [(i, i ^ hop) for i in range(size)])]
  transfers between devices with their start and end apart: 2 -> 12, of which waited for: 1 -> 11; matrix products, arithmetic and copies ran while one was open for 10% -> 1% of each run, Pallas kernels for 0% -> 9%
where the time goes in v1:
time: 238 us; the launch traced here: 237 us
  waiting for transfers between devices  120 us (50%)
  starting transfers between devices  56.2 us (24%)
  Pallas kernels  39.9 us (17%)
  local copies, waits for them, and re-layouts  13.7 us (6%)
  between operations  5.27 us (2%)
    all_to_all x4, waiting for transfers between devices, exchange(): lax.all_to_all(value, 'group', split_axis=0, concat_axis=0, tiled=True)  101 us
    ppermute x8, starting transfers between devices, butterfly(): lax.ppermute(value, axis, [(i, i ^ hop) for i in range(size)])  33 us
    pallas_call x2, Pallas kernels, pair_grads(): pl.pallas_call(functools.partial(pair_kernel, 2, hd ** (-0.5)), grid=(1,)...  25.8 us
    all_to_all x4, starting transfers between devices, exchange(): lax.all_to_all(value, 'group', split_axis=0, concat_axis=0, tiled=True)  23.2 us
    ppermute x8, waiting for transfers between devices, butterfly(): lax.ppermute(value, axis, [(i, i ^ hop) for i in range(size)])  19.6 us
    unnamed x38, local copies, waits for them, and re-layouts  13.4 us
  transfers between devices with their start and end apart: 12, of which 11 were waited for; matrix products, arithmetic and copies ran while one was open for 1% of the time, Pallas kernels for 9%

profile of v1, /device:TPU:8, one launch (start us, length us, event | category | flops | bytes accessed | tf_op | source)
XLA Modules:
  0.0 237.4 jit_solution(10638926961599711239)
XLA Ops:
  0.6 0.8 fusion.1
  1.5 0.1 reduce_max.18.code_ref
  1.6 1.4 copy-done
  3.0 1.9 pick_rows.3
  4.9 11.2 %all-to-all-start.1 = ((bf16[16,3,128,128]{3,2,1,0:T(8,128)(2,1)}), bf16[16,3,128,128]{3,2,1,0:T(8,128)(2,1)}, u32[]{:S(2)}, u32[]{:S(2)}) async-start(bf16[16,3,128,128]{3,2,1,0:T(8,128)(2,1)} %pick_rows.3), calls=%async_computation.1 | async-start | bytes 3145728 | tf_op jit(solution)/shard_map/all_to_all | solution.py:277
  16.2 1.8 pick_rows.2
  18.0 39.3 %all-to-all-done.1.inc_ref = bf16[16,3,128,128]{3,2,1,0:T(8,128)(2,1)} async-done(((bf16[16,3,128,128]{3,2,1,0:T(8,128)(2,1)}), bf16[16,3,128,128]{3,2,1,0:T(8,128)(2,1)}, u32[]{:S(2)}, u32[]{:S(2)}) %all-to-all-start.1) | async-done | bytes 1572896 | tf_op jit(solution)/shard_map/all_to_all | solution.py:277
  57.3 4.4 %all-to-all-start = ((bf16[16,3,128,128]{3,2,1,0:T(8,128)(2,1)}), bf16[16,3,128,128]{3,2,1,0:T(8,128)(2,1)}, u32[]{:S(2)}, u32[]{:S(2)}) async-start(bf16[16,3,128,128]{3,2,1,0:T(8,128)(2,1)} %pick_rows.2), calls=%async_computation | async-start | bytes 3145728 | tf_op jit(solution)/shard_map/all_to_all | solution.py:277
  61.9 12.9 %pair_grads.2 = (bf16[16,3,128,128]{3,2,1,0:T(8,128)(2,1)S(1)}, bf16[16,3,128,128]{3,2,1,0:T(8,128)(2,1)S(1)}, f32[16,128]{1,0:T(8,128)S(1)}) custom-call(s32[16]{0:T(128)S(1)} %get-tuple-element.15.first_ref, s32[16]{0:T(128)S(1)} %get-tuple-element.16.slot_ref, bf16[8,3,128,256]{3,2,1,0:T(8,128)(2,1)S(1)} %bitcast.9, ...), custom_call_target="tpu_custom_call" | custom-call | tf_op jit(solution)/shard_map/pair_grads/pallas_call | solution.py:119
  74.8 1.1 copy-done.10
  75.9 25.5 %all-to-all-done.inc_ref = bf16[16,3,128,128]{3,2,1,0:T(8,128)(2,1)} async-done(((bf16[16,3,128,128]{3,2,1,0:T(8,128)(2,1)}), bf16[16,3,128,128]{3,2,1,0:T(8,128)(2,1)}, u32[]{:S(2)}, u32[]{:S(2)}) %all-to-all-start) | async-done | bytes 1572896 | tf_op jit(solution)/shard_map/all_to_all | solution.py:277
  101.4 12.9 %pair_grads.3 = (bf16[16,3,128,128]{3,2,1,0:T(8,128)(2,1)S(1)}, bf16[16,3,128,128]{3,2,1,0:T(8,128)(2,1)S(1)}, f32[16,128]{1,0:T(8,128)S(1)}) custom-call(s32[16]{0:T(128)S(1)} %get-tuple-element.15.first_ref, s32[16]{0:T(128)S(1)} %get-tuple-element.16.slot_ref, bf16[8,3,128,256]{3,2,1,0:T(8,128)(2,1)S(1)} %bitcast.10, ...), custom_call_target="tpu_custom_call" | custom-call | tf_op jit(solution)/shard_map/pair_grads/pallas_call | solution.py:119
  114.4 1.1 copy-done.8
  115.5 1.2 copy-done.12
  116.7 1.2 collective-permute-done
  117.8 0.6 collective-permute-start.1
  118.4 0.2 fusion
  118.6 2.9 %collective-permute-done.1 = f32[16,128]{1,0:T(8,128)S(1)} collective-permute-done((f32[16,128]{1,0:T(8,128)S(1)}, f32[16,128]{1,0:T(8,128)S(1)}, u32[]{:S(2)}, u32[]{:S(2)}) %collective-permute-start.1) | collective-permute-done | bytes 8224 | tf_op jit(solution)/shard_map/ppermute | solution.py:271
  121.5 0.5 collective-permute-start.2
  122.0 3.2 %collective-permute-done.2 = f32[16,128]{1,0:T(8,128)S(1)} collective-permute-done((f32[16,128]{1,0:T(8,128)S(1)}, f32[16,128]{1,0:T(8,128)S(1)}, u32[]{:S(2)}, u32[]{:S(2)}) %collective-permute-start.2) | collective-permute-done | bytes 8224 | tf_op jit(solution)/shard_map/ppermute | solution.py:271
  125.2 2.3 collective-permute-start.3
  127.4 0.2 select_reduce_fusion.mate_ref
  127.7 2.7 %collective-permute-done.3 = f32[16,128]{1,0:T(8,128)S(1)} collective-permute-done((f32[16,128]{1,0:T(8,128)S(1)}, f32[16,128]{1,0:T(8,128)S(1)}, u32[]{:S(2)}, u32[]{:S(2)}) %collective-permute-start.3) | collective-permute-done | bytes 8224 | tf_op jit(solution)/shard_map/ppermute | solution.py:271
  130.4 2.4 second_terms.3
  132.8 3.8 %all-to-all-start.3 = ((bf16[16,3,128,128]{3,2,1,0:T(8,128)(2,1)}), bf16[16,3,128,128]{3,2,1,0:T(8,128)(2,1)S(1)}, u32[]{:S(2)}, u32[]{:S(2)}) async-start(bf16[16,3,128,128]{3,2,1,0:T(8,128)(2,1)} %second_terms.3), calls=%async_computation.3 | async-start | bytes 3145728 | tf_op jit(solution)/shard_map/all_to_all | solution.py:277
  136.6 2.4 second_terms.2
  139.0 36.0 %all-to-all-done.3.back_ref = bf16[16,3,128,128]{3,2,1,0:T(8,128)(2,1)S(1)} async-done(((bf16[16,3,128,128]{3,2,1,0:T(8,128)(2,1)}), bf16[16,3,128,128]{3,2,1,0:T(8,128)(2,1)S(1)}, u32[]{:S(2)}, u32[]{:S(2)}) %all-to-all-start.3) | async-done | bytes 1572896 | tf_op jit(solution)/shard_map/all_to_all | solution.py:277
  174.9 3.7 %all-to-all-start.2 = ((bf16[16,3,128,128]{3,2,1,0:T(8,128)(2,1)}), bf16[16,3,128,128]{3,2,1,0:T(8,128)(2,1)S(1)}, u32[]{:S(2)}, u32[]{:S(2)}) async-start(bf16[16,3,128,128]{3,2,1,0:T(8,128)(2,1)} %second_terms.2), calls=%async_computation.2 | async-start | bytes 3145728 | tf_op jit(solution)/shard_map/all_to_all | solution.py:277
  178.7 1.4 copy-done.13
  180.1 1.0 first_terms.2.own_ref
  181.1 1.2 copy-done.2
  182.3 1.0 first_terms.3.own_ref
  183.3 1.1 copy-done.4
  184.6 0.6 fusion.3
  185.2 3.3 %collective-permute-start.4 = (f32[]{:T(128)}, f32[]{:T(128)}, u32[]{:S(2)}, u32[]{:S(2)}) collective-permute-start(f32[]{:T(128)} %fusion.3), channel_id=1, source_target_pairs={{0,16},{16,0},{32,48},{48,32},{64,80},{80,64},{96,112},{112,96},{1... | collective-permute-start | bytes 20 | tf_op jit(solution)/shard_map/ppermute | solution.py:271
  188.5 1.8 collective-permute-done.4
  191.6 18.1 %collective-permute-start.5 = (f32[]{:T(128)}, f32[]{:T(128)}, u32[]{:S(2)}, u32[]{:S(2)}) collective-permute-start(f32[]{:T(128)} %add.38), channel_id=1, source_target_pairs={{0,32},{16,48},{32,0},{48,16},{64,96},{80,112},{96,64},{112,80},{1... | collective-permute-start | bytes 20 | tf_op jit(solution)/shard_map/ppermute | solution.py:271
  209.7 4.1 %collective-permute-done.5 = f32[]{:T(128)} collective-permute-done((f32[]{:T(128)}, f32[]{:T(128)}, u32[]{:S(2)}, u32[]{:S(2)}) %collective-permute-start.5) | collective-permute-done | bytes 36 | tf_op jit(solution)/shard_map/ppermute | solution.py:271
  214.5 3.1 %collective-permute-start.6 = (f32[]{:T(128)}, f32[]{:T(128)}, u32[]{:S(2)}, u32[]{:S(2)}) collective-permute-start(f32[]{:T(128)} %add.39), channel_id=1, source_target_pairs={{0,64},{16,80},{32,96},{48,112},{64,0},{80,16},{96,32},{112,48},{1... | collective-permute-start | bytes 20 | tf_op jit(solution)/shard_map/ppermute | solution.py:271
  217.6 1.4 collective-permute-done.6
  219.6 5.1 %collective-permute-start.7 = (f32[]{:T(128)}, f32[]{:T(128)}, u32[]{:S(2)}, u32[]{:S(2)}) collective-permute-start(f32[]{:T(128)} %add.40), channel_id=1, source_target_pairs={{0,128},{16,144},{32,160},{48,176},{64,192},{80,208},{96,224},{112... | collective-permute-start | bytes 20 | tf_op jit(solution)/shard_map/ppermute | solution.py:271
  224.7 2.4 collective-permute-done.7
  227.8 1.4 copy-done.5
  229.2 1.2 finish_head.1.earlier_ref
  230.4 0.9 copy-done.6
  231.2 1.4 copy-done.3
  232.6 1.1 copy-done.7
  233.8 2.5 %finish_last_head.1 = bf16[8,3,128,256]{3,2,1,0:T(8,128)(2,1)} custom-call(s32[16]{0:T(128)S(1)} %reduce_max.18.code_ref, bf16[16,3,128,128]{3,2,1,0:T(8,128)(2,1)S(1)} %all-to-all-done.2.back_ref, f32[8,3,128,128]{3,2,1,0:T(8,128)S(1)} %copy-done.3, bf16[8,3,128,128]{3,2,1,0:T(8,128)(2,1)S(1)} %copy-done.7), custom_call_target="tpu_custom_call" | custom-call | tf_op jit(solution)/shard_map/finish_last_head/pallas_call | solution.py:257
  (43 shorter events, 0.5 us)
Async XLA Ops:
  1.6 1.4 copy-start
  4.9 11.2 %copy-start.1 = (bf16[8,128,3,256]{3,1,2,0:T(8,128)(2,1)S(1)}, bf16[8,128,3,256]{3,1,2,0:T(8,128)(2,1)}, u32[]{:S(2)}) copy-start(bf16[8,128,3,256]{3,1,2,0:T(8,128)(2,1)} %param.5) | copy-start | bytes 4718596
  4.9 52.4 %all-to-all-start.1 = ((bf16[16,3,128,128]{3,2,1,0:T(8,128)(2,1)}), bf16[16,3,128,128]{3,2,1,0:T(8,128)(2,1)}, u32[]{:S(2)}, u32[]{:S(2)}) async-start(bf16[16,3,128,128]{3,2,1,0:T(8,128)(2,1)} %pick_rows.3), calls=%async_computation.1 | async-start | bytes 3145728 | tf_op jit(solution)/shard_map/all_to_all | solution.py:277
  18.0 43.8 %copy-start.15 = (s32[256,3]{0,1:T(4,128)S(1)}, s32[256,3]{0,1:T(4,128)}, u32[]{:S(2)}) copy-start(s32[256,3]{0,1:T(4,128)} %param.6) | copy-start | bytes 9220
  18.0 43.8 %copy-start.16 = (f32[2,256]{1,0:T(2,128)S(1)}, f32[2,256]{1,0:T(2,128)}, u32[]{:S(2)}) copy-start(f32[2,256]{1,0:T(2,128)} %param.8) | copy-start | bytes 6148
  18.0 43.9 %copy-start.14 = (bf16[2,128,256]{2,1,0:T(8,128)(2,1)S(1)}, bf16[2,128,256]{2,1,0:T(8,128)(2,1)}, u32[]{:S(2)}) copy-start(bf16[2,128,256]{2,1,0:T(8,128)(2,1)} %proj_ref.3) | copy-start | bytes 393220
  57.3 44.1 %all-to-all-start = ((bf16[16,3,128,128]{3,2,1,0:T(8,128)(2,1)}), bf16[16,3,128,128]{3,2,1,0:T(8,128)(2,1)}, u32[]{:S(2)}, u32[]{:S(2)}) async-start(bf16[16,3,128,128]{3,2,1,0:T(8,128)(2,1)} %pick_rows.2), calls=%async_computation | async-start | bytes 3145728 | tf_op jit(solution)/shard_map/all_to_all | solution.py:277
  74.8 1.1 copy-start.10
  101.4 26.2 %copy-start.18 = (s32[16]{0:T(128)S(1)}, s32[16]{0:T(128)}, u32[]{:S(2)}) copy-start(s32[16]{0:T(128)} %param.9) | copy-start | bytes 196
  114.3 1.1 copy-start.8
  115.5 1.2 copy-start.12
  116.7 1.2 collective-permute-start
  117.8 3.7 %collective-permute-start.1 = (f32[16,128]{1,0:T(8,128)S(1)}, f32[16,128]{1,0:T(8,128)S(1)}, u32[]{:S(2)}, u32[]{:S(2)}) collective-permute-start(f32[16,128]{1,0:T(8,128)S(1)} %add.33), channel_id=1, source_target_pairs={{0,2},{1,3},{2,0},{3,1},{4,6},{5,7},{6,4},{7,5},{8,10},{9,11},{10,... | collective-permute-start | bytes 24584 | tf_op jit(solution)/shard_map/ppermute | solution.py:271
  121.5 3.7 %collective-permute-start.2 = (f32[16,128]{1,0:T(8,128)S(1)}, f32[16,128]{1,0:T(8,128)S(1)}, u32[]{:S(2)}, u32[]{:S(2)}) collective-permute-start(f32[16,128]{1,0:T(8,128)S(1)} %add.34), channel_id=1, source_target_pairs={{0,4},{1,5},{2,6},{3,7},{4,0},{5,1},{6,2},{7,3},{8,12},{9,13},{10,... | collective-permute-start | bytes 24584 | tf_op jit(solution)/shard_map/ppermute | solution.py:271
  125.2 5.2 %collective-permute-start.3 = (f32[16,128]{1,0:T(8,128)S(1)}, f32[16,128]{1,0:T(8,128)S(1)}, u32[]{:S(2)}, u32[]{:S(2)}) collective-permute-start(f32[16,128]{1,0:T(8,128)S(1)} %add.35), channel_id=1, source_target_pairs={{0,8},{1,9},{2,10},{3,11},{4,12},{5,13},{6,14},{7,15},{8,0},{9,1},... | collective-permute-start | bytes 24584 | tf_op jit(solution)/shard_map/ppermute | solution.py:271
  132.7 3.9 %copy-start.9 = (bf16[16,3,128,128]{3,2,1,0:T(8,128)(2,1)S(1)}, bf16[16,3,128,128]{3,2,1,0:T(8,128)(2,1)}, u32[]{:S(2)}) copy-start(bf16[16,3,128,128]{3,2,1,0:T(8,128)(2,1)} %copy-done.8) | copy-start | bytes 4718596
  132.8 42.2 %all-to-all-start.3 = ((bf16[16,3,128,128]{3,2,1,0:T(8,128)(2,1)}), bf16[16,3,128,128]{3,2,1,0:T(8,128)(2,1)S(1)}, u32[]{:S(2)}, u32[]{:S(2)}) async-start(bf16[16,3,128,128]{3,2,1,0:T(8,128)(2,1)} %second_terms.3), calls=%async_computation.3 | async-start | bytes 3145728 | tf_op jit(solution)/shard_map/all_to_all | solution.py:277
  174.9 56.3 %all-to-all-start.2 = ((bf16[16,3,128,128]{3,2,1,0:T(8,128)(2,1)}), bf16[16,3,128,128]{3,2,1,0:T(8,128)(2,1)S(1)}, u32[]{:S(2)}, u32[]{:S(2)}) async-start(bf16[16,3,128,128]{3,2,1,0:T(8,128)(2,1)} %second_terms.2), calls=%async_computation.2 | async-start | bytes 3145728 | tf_op jit(solution)/shard_map/all_to_all | solution.py:277
  178.7 1.4 copy-start.13
  180.1 2.2 copy-start.11
  181.1 1.2 copy-start.2
  183.3 1.1 copy-start.4
  184.5 45.8 %copy-start.17 = (f32[16]{0:T(128)}, f32[16]{0:T(128)S(1)}, u32[]{:S(2)}) copy-start(f32[16]{0:T(128)S(1)} %slice_reduce_fusion) | copy-start | bytes 196
  185.2 5.1 %collective-permute-start.4 = (f32[]{:T(128)}, f32[]{:T(128)}, u32[]{:S(2)}, u32[]{:S(2)}) collective-permute-start(f32[]{:T(128)} %fusion.3), channel_id=1, source_target_pairs={{0,16},{16,0},{32,48},{48,32},{64,80},{80,64},{96,112},{112,96},{1... | collective-permute-start | bytes 20 | tf_op jit(solution)/shard_map/ppermute | solution.py:271
  191.6 22.3 %collective-permute-start.5 = (f32[]{:T(128)}, f32[]{:T(128)}, u32[]{:S(2)}, u32[]{:S(2)}) collective-permute-start(f32[]{:T(128)} %add.38), channel_id=1, source_target_pairs={{0,32},{16,48},{32,0},{48,16},{64,96},{80,112},{96,64},{112,80},{1... | collective-permute-start | bytes 20 | tf_op jit(solution)/shard_map/ppermute | solution.py:271
  214.5 4.5 %collective-permute-start.6 = (f32[]{:T(128)}, f32[]{:T(128)}, u32[]{:S(2)}, u32[]{:S(2)}) collective-permute-start(f32[]{:T(128)} %add.39), channel_id=1, source_target_pairs={{0,64},{16,80},{32,96},{48,112},{64,0},{80,16},{96,32},{112,48},{1... | collective-permute-start | bytes 20 | tf_op jit(solution)/shard_map/ppermute | solution.py:271
  219.6 7.5 %collective-permute-start.7 = (f32[]{:T(128)}, f32[]{:T(128)}, u32[]{:S(2)}, u32[]{:S(2)}) collective-permute-start(f32[]{:T(128)} %add.40), channel_id=1, source_target_pairs={{0,128},{16,144},{32,160},{48,176},{64,192},{80,208},{96,224},{112... | collective-permute-start | bytes 20 | tf_op jit(solution)/shard_map/ppermute | solution.py:271
  227.7 1.4 copy-start.5
  230.4 0.9 copy-start.6
  231.2 1.4 copy-start.3
  232.6 1.1 copy-start.7

commit v2 on v1

v2 whole, which is shorter than its diff:
```python
import functools

import jax
import jax.numpy as jnp
from jax import lax
from jax.experimental import pallas as pl
from jax.experimental.pallas import tpu as pltpu
from jax.sharding import PartitionSpec as P

loss_scale = 8192.0
VMEM_BYTES = 24 * 1024 * 1024
SECOND_BYTES = 54 * 1024 * 1024
VMEM_ALL = 60 * 1024 * 1024
F32 = jnp.float32
BF16 = jnp.bfloat16
SMEM_SPEC = pl.BlockSpec(memory_space=pltpu.SMEM)
VMEM_SPEC = pl.BlockSpec(memory_space=pltpu.VMEM)
ANY_SPEC = pl.BlockSpec(memory_space=pl.ANY)


def params(limit=VMEM_BYTES):
    return pltpu.CompilerParams(vmem_limit_bytes=limit)


def mm(a, b, ca, cb):
    return lax.dot_general(a, b, (((ca,), (cb,)), ((), ())), preferred_element_type=F32)

HBM_SPEC = pl.BlockSpec(memory_space=pltpu.HBM)


def pick_kernel(start, parts, member_ref, mol_ref, out_ref, sems):
    slots = out_ref.shape[0]
    copies = []
    for s in range(slots):
        copies.append(
            pltpu.make_async_copy(
                mol_ref.at[member_ref[s], pl.ds(start, parts)], out_ref.at[s], sems.at[s]
            )
        )
    for c in copies:
        c.start()
    for c in copies:
        c.wait()


def pick(member, mol, start, parts):
    slots = member.shape[0]
    _, _, length, width = mol.shape
    return pl.pallas_call(
        functools.partial(pick_kernel, start, parts),
        out_shape=jax.ShapeDtypeStruct((slots, parts, length, width), mol.dtype),
        in_specs=[SMEM_SPEC, HBM_SPEC],
        out_specs=HBM_SPEC,
        scratch_shapes=[pltpu.SemaphoreType.DMA((slots,))],
        compiler_params=params(VMEM_ALL),
        name="pick_rows",
    )(member, mol)


def lanes(ref_value, head, hd):
    return ref_value[:, head * hd : (head + 1) * hd]


def weights_of(query, key, inv_root):
    scores = mm(query, key, 1, 1)
    top = jnp.max(scores, axis=1, keepdims=True)
    lifted = jnp.exp((scores - top) * inv_root)
    return lifted * (1.0 / jnp.sum(lifted, axis=1, keepdims=True))


def hidden_of(weights_bf, units, proj):
    context = jnp.concatenate([mm(w, u[2], 1, 0).astype(BF16) for w, u in zip(weights_bf, units)], axis=0)
    hidden = mm(context, proj, 1, 0)
    sig = 0.5 + 0.5 * jnp.tanh(0.5 * hidden)
    return sig, hidden * sig


def add_logits(ids, acts, readouts, length, prev_ref, lp_ref):
    for j, p in enumerate(ids):
        rows = [
            jnp.sum(act[j * length : (j + 1) * length], axis=0, keepdims=True) * readout
            for act, readout in zip(acts, readouts)
        ]
        total = jnp.sum(sum(rows[1:], rows[0]), axis=1, keepdims=True)
        total = jnp.broadcast_to(total, (1, lp_ref.shape[1]))
        if prev_ref is not None:
            total = total + prev_ref[pl.ds(p, 1), :]
        lp_ref[pl.ds(p, 1), :] = total


def forward_units(units, proj_ref, inv_root):
    heads = proj_ref.shape[0]
    weights = [[weights_of(u[0], u[1], inv_root) for u in units[h]] for h in range(heads)]
    weights_bf = [[w.astype(BF16) for w in weights[h]] for h in range(heads)]
    sigs, acts = zip(*[hidden_of(weights_bf[h], units[h], proj_ref[h]) for h in range(heads)])
    return weights, weights_bf, sigs, acts


def direction_units(ids, refs, heads, hd):
    return [[tuple(r(p)[:, h * hd : (h + 1) * hd] for r in refs) for p in ids] for h in range(heads)]


def backward_units(units, weights, weights_bf, sigs, acts, proj_ref, readouts, inv_root, store):
    heads = len(units)
    length = units[0][0][0].shape[0]
    count = len(units[0])
    dcontext = []
    for h in range(heads):
        slope = sigs[h] + acts[h] * (1.0 - sigs[h])
        dhidden = (slope * readouts[h]).astype(BF16)
        whole = mm(dhidden, proj_ref[h], 1, 1).astype(BF16)
        dcontext.append([whole[j * length : (j + 1) * length] for j in range(count)])
    for h in range(heads):
        for j in range(count):
            store(j, h, 2, mm(weights_bf[h][j], dcontext[h][j], 0, 0))
    dweights = [[mm(dcontext[h][j], units[h][j][2], 1, 1) for j in range(count)] for h in range(heads)]
    dscores = []
    for h in range(heads):
        row = []
        for j in range(count):
            w, dw = weights[h][j], dweights[h][j]
            inner = jnp.sum(dw * w, axis=1, keepdims=True)
            row.append((w * (dw - inner) * inv_root).astype(BF16))
        dscores.append(row)
    for h in range(heads):
        for j in range(count):
            store(j, h, 0, mm(dscores[h][j], units[h][j][1], 1, 0))
            store(j, h, 1, mm(dscores[h][j], units[h][j][0], 0, 0))


def outward_kernel(group, first_ref, slot_ref, mol_ref, kv_ref, proj_ref, readout_ref, dq_ref, dkv_ref, lp_ref):
    pairs, length, _ = dq_ref.shape
    heads, hd, _ = proj_ref.shape
    inv_root = hd ** (-0.5)
    readouts = [readout_ref[h : h + 1, :] * (1.0 / length) for h in range(heads)]

    def step(i, carry):
        ids = [i * group + j for j in range(group)]
        units = direction_units(
            ids,
            (lambda p: mol_ref[first_ref[p], 0], lambda p: kv_ref[slot_ref[p], 0], lambda p: kv_ref[slot_ref[p], 1]),
            heads,
            hd,
        )
        weights, weights_bf, sigs, acts = forward_units(units, proj_ref, inv_root)
        add_logits(ids, acts, readouts, length, None, lp_ref)

        def store(j, h, part, value):
            value = value.astype(BF16)
            if part == 0:
                dq_ref[ids[j], :, h * hd : (h + 1) * hd] = value
            else:
                dkv_ref[ids[j], part - 1, :, h * hd : (h + 1) * hd] = value

        backward_units(units, weights, weights_bf, sigs, acts, proj_ref, readouts, inv_root, store)
        return carry

    lax.fori_loop(0, pairs // group, step, 0)


def inward_logits_kernel(group, first_ref, slot_ref, mol_ref, q_ref, proj_ref, readout_ref, prev_ref, lp_ref):
    pairs = lp_ref.shape[0]
    length = mol_ref.shape[2]
    heads, hd, _ = proj_ref.shape
    inv_root = hd ** (-0.5)
    readouts = [readout_ref[h : h + 1, :] * (1.0 / length) for h in range(heads)]

    def step(i, carry):
        ids = [i * group + j for j in range(group)]
        units = direction_units(
            ids,
            (lambda p: q_ref[slot_ref[p], 0], lambda p: mol_ref[first_ref[p], 1], lambda p: mol_ref[first_ref[p], 2]),
            heads,
            hd,
        )
        acts = forward_units(units, proj_ref, inv_root)[3]
        add_logits(ids, acts, readouts, length, prev_ref, lp_ref)
        return carry

    lax.fori_loop(0, pairs // group, step, 0)


def inward_kernel(group, first_ref, slot_ref, mol_ref, q_ref, proj_ref, readout_ref, dq_ref, dkv_ref):
    pairs, length, _ = dq_ref.shape
    heads, hd, _ = proj_ref.shape
    inv_root = hd ** (-0.5)
    readouts = [readout_ref[h : h + 1, :] * (1.0 / length) for h in range(heads)]

    def step(i, carry):
        ids = [i * group + j for j in range(group)]
        units = direction_units(
            ids,
            (lambda p: q_ref[slot_ref[p], 0], lambda p: mol_ref[first_ref[p], 1], lambda p: mol_ref[first_ref[p], 2]),
            heads,
            hd,
        )
        weights, weights_bf, sigs, acts = forward_units(units, proj_ref, inv_root)

        def store(j, h, part, value):
            value = value.astype(BF16)
            if part == 0:
                dq_ref[ids[j], :, h * hd : (h + 1) * hd] = value
            else:
                dkv_ref[ids[j], part - 1, :, h * hd : (h + 1) * hd] = value

        backward_units(units, weights, weights_bf, sigs, acts, proj_ref, readouts, inv_root, store)
        return carry

    lax.fori_loop(0, pairs // group, step, 0)


def wide(pairs):
    return jax.ShapeDtypeStruct((pairs, 128), F32)


def grads_shape(pairs, mol):
    _, parts, length, width = mol.shape
    return (
        jax.ShapeDtypeStruct((pairs, length, width), BF16),
        jax.ShapeDtypeStruct((pairs, parts - 1, length, width), BF16),
    )


def pair_cost(share, terms):
    return pl.CostEstimate(flops=int(2.7e9 * share), bytes_accessed=terms, transcendentals=0)


def outward(first, slot, mol, kv, proj, readout):
    pairs = first.shape[0]
    return pl.pallas_call(
        functools.partial(outward_kernel, 2),
        out_shape=grads_shape(pairs, mol) + (wide(pairs),),
        in_specs=[SMEM_SPEC] * 2 + [VMEM_SPEC] * 4,
        out_specs=(VMEM_SPEC,) * 3,
        compiler_params=params(),
        name="outward_grads",
    )(first, slot, mol, kv, proj, readout)


def inward_logits(first, slot, mol, q, proj, readout, prev):
    return pl.pallas_call(
        functools.partial(inward_logits_kernel, 2),
        out_shape=jax.ShapeDtypeStruct(prev.shape, F32),
        in_specs=[SMEM_SPEC] * 2 + [VMEM_SPEC] * 5,
        out_specs=VMEM_SPEC,
        compiler_params=params(),
        name="inward_logits",
    )(first, slot, mol, q, proj, readout, prev)


def inward(first, slot, mol, q, proj, readout):
    pairs = first.shape[0]
    return pl.pallas_call(
        functools.partial(inward_kernel, 2),
        out_shape=grads_shape(pairs, mol),
        in_specs=[SMEM_SPEC] * 2 + [VMEM_SPEC] * 4,
        out_specs=(VMEM_SPEC,) * 2,
        compiler_params=params(),
        name="inward_grads",
    )(first, slot, mol, q, proj, readout)


def grad_scale(logits, target):
    scale = (0.5 + 0.5 * jnp.tanh(0.5 * logits) - target) * loss_scale
    return jnp.concatenate([scale, scale], axis=1)


def second_kernel(slot_ref, lead_ref, mate_ref, logits_ref, target_ref, gs_ref, out_ref, scale_ref, hold_ref, sems):
    pairs, parts = gs_ref.shape[:2]
    scale_ref[...] = grad_scale(logits_ref[...], target_ref[...])

    def send(p):
        return pltpu.make_async_copy(hold_ref.at[p], out_ref.at[slot_ref[p]], sems.at[p])

    def step(p, carry):
        mate = mate_ref[p]
        own = scale_ref[pl.ds(p, 1), :]

        @pl.when((lead_ref[p] == 1) & (mate < 0))
        def single():
            for c in range(parts):
                hold_ref[p, c] = (own * gs_ref[p, c].astype(F32)).astype(BF16)
            send(p).start()

        @pl.when((lead_ref[p] == 1) & (mate >= 0))
        def double():
            other_at = jnp.maximum(mate, 0)
            other = scale_ref[pl.ds(other_at, 1), :]
            for c in range(parts):
                hold_ref[p, c] = (
                    own * gs_ref[p, c].astype(F32) + other * gs_ref[other_at, c].astype(F32)
                ).astype(BF16)
            send(p).start()

        return carry

    lax.fori_loop(0, pairs, step, 0)

    def land(p, carry):
        @pl.when(lead_ref[p] == 1)
        def wait():
            send(p).wait()

        return carry

    lax.fori_loop(0, pairs, land, 0)


def second_terms(slot, lead, mate, logits, target, gs, slots):
    pairs, parts, length, width = gs.shape
    return pl.pallas_call(
        second_kernel,
        out_shape=jax.ShapeDtypeStruct((slots, parts, length, width), BF16),
        in_specs=[SMEM_SPEC] * 3 + [VMEM_SPEC] * 3,
        out_specs=HBM_SPEC,
        scratch_shapes=[
            pltpu.VMEM((pairs, width), F32),
            pltpu.VMEM((pairs, parts, length, width), BF16),
            pltpu.SemaphoreType.DMA((pairs,)),
        ],
        compiler_params=params(SECOND_BYTES),
        name="second_terms",
    )(slot, lead, mate, logits, target, gs)


def finish_kernel(first_ref, code_ref, logits_ref, target_ref, own_ref, back_ref, *rest):
    out_ref, sum_ref, scale_ref = rest[-3:]
    pairs = own_ref.shape[0]
    slots = back_ref.shape[0]
    scale_ref[...] = grad_scale(logits_ref[...], target_ref[...])
    sum_ref[...] = jnp.zeros_like(sum_ref)

    def own_step(p, carry):
        sum_ref[first_ref[p]] += scale_ref[pl.ds(p, 1), :] * own_ref[p, 0].astype(F32)
        return carry

    def back_step(s, carry):
        m = code_ref[s]

        @pl.when(m >= 0)
        def add():
            sum_ref[jnp.maximum(m, 0)] += back_ref[s, 0].astype(F32)

        return carry

    lax.fori_loop(0, pairs, own_step, 0)
    lax.fori_loop(0, slots, back_step, 0)
    out_ref[:, 0] = sum_ref[...].astype(BF16)


def finish(first, code, logits, target, own, back, mols, start, whole):
    pairs, parts, length, width = own.shape
    slots = back.shape[0]
    part = lambda i: (0, i, 0, 0)
    operands = (first, code, logits, target, own, back)
    in_specs = [SMEM_SPEC] * 2 + [VMEM_SPEC] * 2
    in_specs += [pl.BlockSpec((pairs, 1, length, width), part), pl.BlockSpec((slots, 1, length, width), part)]
    aliases = {}
    if whole is not None:
        operands += (whole,)
        in_specs += [HBM_SPEC]
        aliases = {len(operands) - 1: 0}
    return pl.pallas_call(
        finish_kernel,
        grid=(parts,),
        out_shape=jax.ShapeDtypeStruct((mols, 3, length, width), BF16),
        in_specs=in_specs,
        out_specs=pl.BlockSpec((mols, 1, length, width), lambda i: (0, start + i, 0, 0)),
        scratch_shapes=[pltpu.VMEM((mols, length, width), F32), pltpu.VMEM((pairs, width), F32)],
        input_output_aliases=aliases,
        compiler_params=params(),
        name="finish_parts",
    )(*operands)


def hop(value, axis, size, change):
    return lax.ppermute(value, axis, [(i, change(i)) for i in range(size)])


def butterfly(value, axis, size):
    step = 1
    while step < size:
        value = value + hop(value, axis, size, lambda i: i ^ step)
        step *= 2
    return value


def sum_shards(value, size):
    quarter = size // 4
    step = 1
    while step < quarter:
        value = value + hop(value, "fsdp", size, lambda i: i ^ step)
        step *= 2
    near, far, last = [
        hop(value, "fsdp", size, lambda i: (i + k * quarter) % size) for k in (1, 2, 3)
    ]
    return (value + far) + (near + last)


def exchange(value):
    return lax.all_to_all(value, "group", split_axis=0, concat_axis=0, tiled=True)


def local(mol_qkv, pair_list, head_proj, head_out, labels):
    groups = lax.axis_size("group")
    shards = lax.axis_size("fsdp")
    device = lax.axis_index("group")
    mols = mol_qkv.shape[0]
    total_pairs = pair_list.shape[0]
    pairs = total_pairs // groups
    mol = jnp.transpose(mol_qkv, (0, 2, 1, 3))

    blocks = pair_list.T.reshape(3, groups, pairs)
    code = jnp.max(jnp.where(blocks[1] == device, blocks[2], -1), axis=1)
    member = jnp.maximum(code, 0)
    mine = lax.dynamic_index_in_dim(blocks, device, 1, keepdims=False)
    first, slot = mine[0], mine[1]
    place = jnp.arange(pairs, dtype=jnp.int32)
    same = slot[:, None] == slot[None, :]
    lead = jnp.logical_not(jnp.any(same & (place[None, :] < place[:, None]), axis=1)).astype(jnp.int32)
    mate = jnp.max(jnp.where(same & (place[None, :] > place[:, None]), place[None, :], -1), axis=1)

    kv = exchange(pick(member, mol, 1, 2))
    q = exchange(pick(member, mol, 0, 1))
    out_dq, out_dkv, part = outward(first, slot, mol, kv, head_proj, head_out)
    part = inward_logits(first, slot, mol, q, head_proj, head_out, part)
    logits_wide = sum_shards(part, shards)
    targets = labels.astype(F32)
    target_wide = jnp.broadcast_to(targets[:, None], logits_wide.shape)

    back_kv = exchange(second_terms(slot, lead, mate, logits_wide, target_wide, out_dkv, groups))
    in_dq, in_dkv = inward(first, slot, mol, q, head_proj, head_out)
    logits = logits_wide[:, 0]
    loss_terms = jax.nn.softplus(logits) - targets * logits
    mean_loss = butterfly(jnp.sum(loss_terms), "group", groups) / total_pairs
    in_dq, mean_loss = lax.optimization_barrier((in_dq, mean_loss))
    back_q = exchange(second_terms(slot, lead, mate, logits_wide, target_wide, in_dq[:, None], groups))

    grads = finish(first, code, logits_wide, target_wide, in_dkv, back_kv, mols, 1, None)
    grads = finish(first, code, logits_wide, target_wide, out_dq[:, None], back_q, mols, 0, grads)
    mol_grad = jnp.transpose(grads, (0, 2, 1, 3))
    return (mol_grad, logits, mean_loss)


def solution(mesh):
    placed = (
        P("group", None, None, "fsdp"),
        P(),
        P("fsdp", None, None),
        P("fsdp", None),
        P("group"),
    )
    return jax.shard_map(
        local,
        mesh=mesh,
        in_specs=placed,
        out_specs=(P("group", None, None, "fsdp"), P("group"), P()),
        check_vma=False,
    )
```

time: 238 us -> 294 us (1.24)
  Pallas kernels: 39.9 us -> 142 us
  waiting for transfers between devices: 120 us -> 70.6 us
  local copies, waits for them, and re-layouts: 13.7 us -> 6.85 us
  starting transfers between devices: 56.2 us -> 62 us
    pallas_call x8 -> x7, Pallas kernels: 35.2 us -> 136 us  [the longest x2 99.3 us: pick(): pl.pallas_call(functools.partial(pick_kernel, start, parts), out_shape=ja...]
    all_to_all x4, waiting for transfers between devices: 101 us -> 54.5 us  [exchange(): lax.all_to_all(value, 'group', split_axis=0, concat_axis=0, tiled=True)]
    unnamed x38 -> x34, local copies, waits for them, and re-layouts: 13.4 us -> 5.92 us
    ppermute x8 -> x9, waiting for transfers between devices: 19.6 us -> 16.2 us  [hop(): return lax.ppermute(value, axis, [(i, change(i)) for i in range(size)])]
    all_to_all x4, starting transfers between devices: 23.2 us -> 26.2 us  [exchange(): lax.all_to_all(value, 'group', split_axis=0, concat_axis=0, tiled=True)]
    ppermute x8 -> x9, starting transfers between devices: 33 us -> 35.9 us  [hop(): return lax.ppermute(value, axis, [(i, change(i)) for i in range(size)])]
  transfers between devices with their start and end apart: 12 -> 13, of which waited for: 11 -> 11; matrix products, arithmetic and copies ran while one was open for 1% -> 1% of each run, Pallas kernels for 9% -> 22%
where the time goes in v2:
time: 294 us; the launch traced here: 291 us
  Pallas kernels  142 us (48%)
  waiting for transfers between devices  70.6 us (24%)
  starting transfers between devices  62 us (21%)
  local copies, waits for them, and re-layouts  6.85 us (2%)
  between operations  5.21 us (2%)
  other arithmetic  4.05 us (1%)
    pallas_call x2, Pallas kernels, pick(): pl.pallas_call(functools.partial(pick_kernel, start, parts), out_shape=ja...  99.3 us
    all_to_all x4, waiting for transfers between devices, exchange(): lax.all_to_all(value, 'group', split_axis=0, concat_axis=0, tiled=True)  54.5 us
    ppermute x9, starting transfers between devices, hop(): return lax.ppermute(value, axis, [(i, change(i)) for i in range(size)])  35.9 us
    all_to_all x4, starting transfers between devices, exchange(): lax.all_to_all(value, 'group', split_axis=0, concat_axis=0, tiled=True)  26.2 us
    ppermute x9, waiting for transfers between devices, hop(): return lax.ppermute(value, axis, [(i, change(i)) for i in range(size)])  16.2 us
    pallas_call x1, Pallas kernels, outward(): pl.pallas_call(functools.partial(outward_kernel, 2), out_shape=grads_shap...  12.8 us
    pallas_call x1, Pallas kernels, inward(): pl.pallas_call(functools.partial(inward_kernel, 2), out_shape=grads_shape...  11.5 us
    pallas_call x1, Pallas kernels, inward_logits(): pl.pallas_call(functools.partial(inward_logits_kernel, 2), out_shape=jax....  6.96 us
  transfers between devices with their start and end apart: 13, of which 11 were waited for; matrix products, arithmetic and copies ran while one was open for 1% of the time, Pallas kernels for 22%

profile of v2, /device:TPU:8, one launch (start us, length us, event | category | flops | bytes accessed | tf_op | source)
XLA Modules:
  0.0 291.0 jit_solution(3327182634497808609)
XLA Ops:
  0.6 0.8 fusion.1
  1.4 0.1 select_n.25
  1.5 0.1 reduce_max.18.code_ref
  1.6 0.5 broadcast_maximum_fusion.member_ref
  2.1 65.4 %pick_rows.3 = bf16[16,2,128,256]{3,2,1,0:T(8,128)(2,1)} custom-call(s32[16]{0:T(128)} %broadcast_maximum_fusion.member_ref, bf16[8,3,128,256]{3,2,1,0:T(8,128)(2,1)} %bitcast.9), custom_call_target="tpu_custom_call" | custom-call | tf_op jit(solution)/shard_map/pick_rows/pallas_call | solution.py:49
  67.6 11.1 %all-to-all-start.1 = ((bf16[16,2,128,256]{3,2,1,0:T(8,128)(2,1)}), bf16[16,2,128,256]{3,2,1,0:T(8,128)(2,1)}, u32[]{:S(2)}, u32[]{:S(2)}) async-start(bf16[16,2,128,256]{3,2,1,0:T(8,128)(2,1)} %pick_rows.3), calls=%async_computation.1 | async-start | bytes 4194304 | tf_op jit(solution)/shard_map/all_to_all | solution.py:401
  78.7 33.8 %pick_rows.2 = bf16[16,1,128,256]{3,2,1,0:T(8,128)(2,1)} custom-call(s32[16]{0:T(128)} %broadcast_maximum_fusion.member_ref, bf16[8,3,128,256]{3,2,1,0:T(8,128)(2,1)} %bitcast.10), custom_call_target="tpu_custom_call" | custom-call | tf_op jit(solution)/shard_map/pick_rows/pallas_call | solution.py:49
  112.6 18.2 %all-to-all-done.1.kv_ref = bf16[16,2,128,256]{3,2,1,0:T(8,128)(2,1)} async-done(((bf16[16,2,128,256]{3,2,1,0:T(8,128)(2,1)}), bf16[16,2,128,256]{3,2,1,0:T(8,128)(2,1)}, u32[]{:S(2)}, u32[]{:S(2)}) %all-to-all-start.1) | async-done | bytes 2097184 | tf_op jit(solution)/shard_map/all_to_all | solution.py:401
  130.8 3.7 %all-to-all-start = ((bf16[16,1,128,256]{3,2,1,0:T(8,128)(2,1)}), bf16[16,1,128,256]{3,2,1,0:T(8,128)(2,1)S(1)}, u32[]{:S(2)}, u32[]{:S(2)}) async-start(bf16[16,1,128,256]{3,2,1,0:T(8,128)(2,1)} %pick_rows.2), calls=%async_computation | async-start | bytes 2097152 | tf_op jit(solution)/shard_map/all_to_all | solution.py:401
  134.5 0.1 reshape.25
  134.6 12.8 %outward_grads.1 = (bf16[16,128,256]{2,1,0:T(8,128)(2,1)S(1)}, bf16[16,2,128,256]{3,2,1,0:T(8,128)(2,1)S(1)}, f32[16,128]{1,0:T(8,128)S(1)}) custom-call(s32[16]{0:T(128)S(1)} %get-tuple-element.18.first_ref, s32[16]{0:T(128)S(1)} %get-tuple-element.17.slot_ref, bf16[8,3,128,256]{3,2,1,0:T(8,128)(2,1)S(1)} %bitcast.11, ...), custom_call_target="tpu_custom_call" | custom-call | tf_op jit(solution)/shard_map/outward_grads/pallas_call | solution.py:230
  147.4 1.3 copy-done.3
  148.7 1.0 copy-done.6
  149.7 14.8 %all-to-all-done.q_ref = bf16[16,1,128,256]{3,2,1,0:T(8,128)(2,1)S(1)} async-done(((bf16[16,1,128,256]{3,2,1,0:T(8,128)(2,1)}), bf16[16,1,128,256]{3,2,1,0:T(8,128)(2,1)S(1)}, u32[]{:S(2)}, u32[]{:S(2)}) %all-to-all-start) | async-done | bytes 1048608 | tf_op jit(solution)/shard_map/all_to_all | solution.py:401
  164.6 7.0 %inward_logits.1 = f32[16,128]{1,0:T(8,128)S(1)} custom-call(s32[16]{0:T(128)S(1)} %get-tuple-element.18.first_ref, s32[16]{0:T(128)S(1)} %get-tuple-element.17.slot_ref, bf16[8,3,128,256]{3,2,1,0:T(8,128)(2,1)S(1)} %bitcast.12, bf16[16,1,128,256]{3,2,1,0:T(8,128)(2,1)S(1)} %all-to-all-done.q_ref, bf16[2,128,256]{2,1,0:T(8,128)(2,1)S(1)} %copy-done.4, ...), custom_call_target="tpu_custom_call" | custom-call | tf_op jit(solution)/shard_map/inward_logits/pallas_call | solution.py:241
  171.6 0.2 fusion
  171.7 1.0 collective-permute-done
  172.7 0.6 collective-permute-start.1
  173.3 0.5 not_convert_fusion.lead_ref
  173.8 2.5 collective-permute-done.1
  176.4 2.3 collective-permute-start.2
  178.7 2.0 collective-permute-start.4
  180.7 0.7 select_reduce_fusion.mate_ref
  181.4 0.1 collective-permute-done.2
  181.6 0.8 collective-permute-done.3
  182.3 0.6 add_add_fusion.logits_ref
  182.9 0.7 broadcast_in_dim.32.target_ref
  183.6 3.1 %second_terms.3 = bf16[16,2,128,256]{3,2,1,0:T(8,128)(2,1)} custom-call(s32[16]{0:T(128)} %copy-done.12, s32[16]{0:T(128)} %not_convert_fusion.lead_ref, s32[16]{0:T(128)} %select_reduce_fusion.mate_ref, f32[16,128]{1,0:T(8,128)} %add_add_fusion.logits_ref, f32[16,128]{1,0:T(8,128)} %broadcast_in_dim.32.target_ref, bf16[16,2,128,256]{3,2,1,0:T(8,128)(2,1)} %copy-done.3), custom_call_target="tpu_custom_call" | custom-call | tf_op jit(solution)/shard_map/second_terms/pallas_call | solution.py:311
  186.8 4.5 %all-to-all-start.3 = ((bf16[16,2,128,256]{3,2,1,0:T(8,128)(2,1)}), bf16[16,2,128,256]{3,2,1,0:T(8,128)(2,1)}, u32[]{:S(2)}, u32[]{:S(2)}) async-start(bf16[16,2,128,256]{3,2,1,0:T(8,128)(2,1)} %second_terms.3), calls=%async_computation.3 | async-start | bytes 4194304 | tf_op jit(solution)/shard_map/all_to_all | solution.py:401
  191.2 11.5 %inward_grads.1 = (bf16[16,128,256]{2,1,0:T(8,128)(2,1)S(1)}, bf16[16,2,128,256]{3,2,1,0:T(8,128)(2,1)S(1)}) custom-call(s32[16]{0:T(128)S(1)} %get-tuple-element.18.first_ref, s32[16]{0:T(128)S(1)} %copy-done.13, bf16[8,3,128,256]{3,2,1,0:T(8,128)(2,1)S(1)} %bitcast.13, bf16[16,1,128,256]{3,2,1,0:T(8,128)(2,1)S(1)} %all-to-all-done.q_ref, ...), custom_call_target="tpu_custom_call" | custom-call | tf_op jit(solution)/shard_map/inward_grads/pallas_call | solution.py:253
  202.7 1.3 copy-done.1
  204.1 1.0 copy-done.5
  205.1 0.1 slice_reduce_fusion
  205.2 0.6 fusion.3
  205.8 3.2 %collective-permute-start.5 = (f32[]{:T(128)}, f32[]{:T(128)}, u32[]{:S(2)}, u32[]{:S(2)}) collective-permute-start(f32[]{:T(128)} %fusion.3), channel_id=1, source_target_pairs={{0,16},{16,0},{32,48},{48,32},{64,80},{80,64},{96,112},{112,96},{1... | collective-permute-start | bytes 20 | tf_op jit(solution)/shard_map/ppermute | solution.py:377
  209.0 1.9 collective-permute-done.5
  212.2 20.8 %collective-permute-start.6 = (f32[]{:T(128)}, f32[]{:T(128)}, u32[]{:S(2)}, u32[]{:S(2)}) collective-permute-start(f32[]{:T(128)} %add.42), channel_id=1, source_target_pairs={{0,32},{16,48},{32,0},{48,16},{64,96},{80,112},{96,64},{112,80},{1... | collective-permute-start | bytes 20 | tf_op jit(solution)/shard_map/ppermute | solution.py:377
  233.0 4.7 %collective-permute-done.6 = f32[]{:T(128)} collective-permute-done((f32[]{:T(128)}, f32[]{:T(128)}, u32[]{:S(2)}, u32[]{:S(2)}) %collective-permute-start.6) | collective-permute-done | bytes 36 | tf_op jit(solution)/shard_map/ppermute | solution.py:377
  238.4 2.4 collective-permute-start.7
  240.8 2.0 collective-permute-done.7
  243.5 4.4 %collective-permute-start.8 = (f32[]{:T(128)}, f32[]{:T(128)}, u32[]{:S(2)}, u32[]{:S(2)}) collective-permute-start(f32[]{:T(128)} %add.44), channel_id=1, source_target_pairs={{0,128},{16,144},{32,160},{48,176},{64,192},{80,208},{96,224},{112... | collective-permute-start | bytes 20 | tf_op jit(solution)/shard_map/ppermute | solution.py:377
  247.9 3.1 %collective-permute-done.8 = f32[]{:T(128)} collective-permute-done((f32[]{:T(128)}, f32[]{:T(128)}, u32[]{:S(2)}, u32[]{:S(2)}) %collective-permute-start.8) | collective-permute-done | bytes 36 | tf_op jit(solution)/shard_map/ppermute | solution.py:377
  251.6 2.7 second_terms.2
  254.4 7.0 %all-to-all-start.2 = ((bf16[16,1,128,256]{3,2,1,0:T(8,128)(2,1)}), bf16[16,1,128,256]{3,2,1,0:T(8,128)(2,1)S(1)}, u32[]{:S(2)}, u32[]{:S(2)}) async-start(bf16[16,1,128,256]{3,2,1,0:T(8,128)(2,1)} %second_terms.2), calls=%async_computation.2 | async-start | bytes 2097152 | tf_op jit(solution)/shard_map/all_to_all | solution.py:401
  261.4 3.8 %finish_parts.2.rest_0_ = bf16[8,3,128,256]{3,2,1,0:T(8,128)(2,1)} custom-call(s32[16]{0:T(128)S(1)} %get-tuple-element.18.first_ref, s32[16]{0:T(128)S(1)} %reduce_max.18.code_ref, f32[16,128]{1,0:T(8,128)S(1)} %copy-done.9, f32[16,128]{1,0:T(8,128)S(1)} %copy-done.10, bf16[16,2,128,256]{3,2,1,0:T(8,128)(2,1)S(1)} %copy-done.2, ...), custom_call_target="tpu_custom_call" | custom-call | tf_op jit(solution)/shard_map/finish_parts/pallas_call | solution.py:363
  265.2 21.4 %all-to-all-done.2.back_ref = bf16[16,1,128,256]{3,2,1,0:T(8,128)(2,1)S(1)} async-done(((bf16[16,1,128,256]{3,2,1,0:T(8,128)(2,1)}), bf16[16,1,128,256]{3,2,1,0:T(8,128)(2,1)S(1)}, u32[]{:S(2)}, u32[]{:S(2)}) %all-to-all-start.2) | async-done | bytes 1048608 | tf_op jit(solution)/shard_map/all_to_all | solution.py:401
  286.5 1.2 copy-done.7
  287.7 2.1 finish_parts.3
  (37 shorter events, 0.1 us)
Async XLA Ops:
  67.6 63.2 %all-to-all-start.1 = ((bf16[16,2,128,256]{3,2,1,0:T(8,128)(2,1)}), bf16[16,2,128,256]{3,2,1,0:T(8,128)(2,1)}, u32[]{:S(2)}, u32[]{:S(2)}) async-start(bf16[16,2,128,256]{3,2,1,0:T(8,128)(2,1)} %pick_rows.3), calls=%async_computation.1 | async-start | bytes 4194304 | tf_op jit(solution)/shard_map/all_to_all | solution.py:401
  78.7 55.8 %copy-start.14 = (s32[256,3]{0,1:T(4,128)S(1)}, s32[256,3]{0,1:T(4,128)}, u32[]{:S(2)}) copy-start(s32[256,3]{0,1:T(4,128)} %param.6) | copy-start | bytes 9220
  78.7 55.9 %copy-start = (bf16[8,128,3,256]{3,1,2,0:T(8,128)(2,1)S(1)}, bf16[8,128,3,256]{3,1,2,0:T(8,128)(2,1)}, u32[]{:S(2)}) copy-start(bf16[8,128,3,256]{3,1,2,0:T(8,128)(2,1)} %param.5) | copy-start | bytes 4718596
  78.7 55.9 %copy-start.4 = (bf16[2,128,256]{2,1,0:T(8,128)(2,1)S(1)}, bf16[2,128,256]{2,1,0:T(8,128)(2,1)}, u32[]{:S(2)}) copy-start(bf16[2,128,256]{2,1,0:T(8,128)(2,1)} %proj_ref.5) | copy-start | bytes 393220
  78.7 55.9 %copy-start.11 = (f32[2,256]{1,0:T(2,128)S(1)}, f32[2,256]{1,0:T(2,128)}, u32[]{:S(2)}) copy-start(f32[2,256]{1,0:T(2,128)} %readout_ref.5) | copy-start | bytes 6148
  130.8 33.8 %all-to-all-start = ((bf16[16,1,128,256]{3,2,1,0:T(8,128)(2,1)}), bf16[16,1,128,256]{3,2,1,0:T(8,128)(2,1)S(1)}, u32[]{:S(2)}, u32[]{:S(2)}) async-start(bf16[16,1,128,256]{3,2,1,0:T(8,128)(2,1)} %pick_rows.2), calls=%async_computation | async-start | bytes 2097152 | tf_op jit(solution)/shard_map/all_to_all | solution.py:401
  134.6 46.1 %copy-start.12 = (s32[16]{0:T(128)}, s32[16]{0:T(128)S(1)}, u32[]{:S(2)}) copy-start(s32[16]{0:T(128)S(1)} %get-tuple-element.17.slot_ref) | copy-start | bytes 196
  147.4 1.3 copy-start.3
  148.7 1.0 copy-start.6
  149.7 31.7 %copy-start.16 = (s32[16]{0:T(128)S(1)}, s32[16]{0:T(128)}, u32[]{:S(2)}) copy-start(s32[16]{0:T(128)} %param.9) | copy-start | bytes 196
  171.5 1.2 collective-permute-start
  172.7 3.7 %collective-permute-start.1 = (f32[16,128]{1,0:T(8,128)S(1)}, f32[16,128]{1,0:T(8,128)S(1)}, u32[]{:S(2)}, u32[]{:S(2)}) collective-permute-start(f32[16,128]{1,0:T(8,128)S(1)} %add.36), channel_id=1, source_target_pairs={{0,2},{1,3},{2,0},{3,1},{4,6},{5,7},{6,4},{7,5},{8,10},{9,11},{10,... | collective-permute-start | bytes 24584 | tf_op jit(solution)/shard_map/ppermute | solution.py:377
  176.4 5.2 %collective-permute-start.2 = (f32[16,128]{1,0:T(8,128)S(1)}, f32[16,128]{1,0:T(8,128)S(1)}, u32[]{:S(2)}, u32[]{:S(2)}) collective-permute-start(f32[16,128]{1,0:T(8,128)S(1)} %add.37), channel_id=1, source_target_pairs={{0,8},{1,9},{2,10},{3,11},{4,12},{5,13},{6,14},{7,15},{8,0},{9,1},... | collective-permute-start | bytes 24584 | tf_op jit(solution)/shard_map/ppermute | solution.py:377
  178.7 3.7 %collective-permute-start.3 = (f32[16,128]{1,0:T(8,128)S(1)}, f32[16,128]{1,0:T(8,128)S(1)}, u32[]{:S(2)}, u32[]{:S(2)}) collective-permute-start(f32[16,128]{1,0:T(8,128)S(1)} %add.37), channel_id=1, source_target_pairs={{0,4},{1,5},{2,6},{3,7},{4,8},{5,9},{6,10},{7,11},{8,12},{9,13},{1... | collective-permute-start | bytes 24584 | tf_op jit(solution)/shard_map/ppermute | solution.py:377
  178.7 3.7 %collective-permute-start.4 = (f32[16,128]{1,0:T(8,128)S(1)}, f32[16,128]{1,0:T(8,128)S(1)}, u32[]{:S(2)}, u32[]{:S(2)}) collective-permute-start(f32[16,128]{1,0:T(8,128)S(1)} %add.37), channel_id=1, source_target_pairs={{0,12},{1,13},{2,14},{3,15},{4,0},{5,1},{6,2},{7,3},{8,4},{9,5},{1... | collective-permute-start | bytes 24584 | tf_op jit(solution)/shard_map/ppermute | solution.py:377
  186.7 4.5 %copy-start.13 = (s32[16]{0:T(128)S(1)}, s32[16]{0:T(128)}, u32[]{:S(2)}) copy-start(s32[16]{0:T(128)} %copy-done.12) | copy-start | bytes 196
  186.8 67.6 %all-to-all-start.3 = ((bf16[16,2,128,256]{3,2,1,0:T(8,128)(2,1)}), bf16[16,2,128,256]{3,2,1,0:T(8,128)(2,1)}, u32[]{:S(2)}, u32[]{:S(2)}) async-start(bf16[16,2,128,256]{3,2,1,0:T(8,128)(2,1)} %second_terms.3), calls=%async_computation.3 | async-start | bytes 4194304 | tf_op jit(solution)/shard_map/all_to_all | solution.py:401
  191.2 13.8 %copy-start.8 = (f32[16,128]{1,0:T(8,128)S(1)}, f32[16,128]{1,0:T(8,128)}, u32[]{:S(2)}) copy-start(f32[16,128]{1,0:T(8,128)} %add_add_fusion.logits_ref) | copy-start | bytes 24580
  202.7 1.4 copy-start.1
  204.1 1.0 copy-start.5
  205.2 49.2 %copy-start.15 = (f32[16]{0:T(128)}, f32[16]{0:T(128)S(1)}, u32[]{:S(2)}) copy-start(f32[16]{0:T(128)S(1)} %slice_reduce_fusion) | copy-start | bytes 196
  205.8 5.1 %collective-permute-start.5 = (f32[]{:T(128)}, f32[]{:T(128)}, u32[]{:S(2)}, u32[]{:S(2)}) collective-permute-start(f32[]{:T(128)} %fusion.3), channel_id=1, source_target_pairs={{0,16},{16,0},{32,48},{48,32},{64,80},{80,64},{96,112},{112,96},{1... | collective-permute-start | bytes 20 | tf_op jit(solution)/shard_map/ppermute | solution.py:377
  212.2 25.5 %collective-permute-start.6 = (f32[]{:T(128)}, f32[]{:T(128)}, u32[]{:S(2)}, u32[]{:S(2)}) collective-permute-start(f32[]{:T(128)} %add.42), channel_id=1, source_target_pairs={{0,32},{16,48},{32,0},{48,16},{64,96},{80,112},{96,64},{112,80},{1... | collective-permute-start | bytes 20 | tf_op jit(solution)/shard_map/ppermute | solution.py:377
  238.4 4.5 %collective-permute-start.7 = (f32[]{:T(128)}, f32[]{:T(128)}, u32[]{:S(2)}, u32[]{:S(2)}) collective-permute-start(f32[]{:T(128)} %add.43), channel_id=1, source_target_pairs={{0,64},{16,80},{32,96},{48,112},{64,0},{80,16},{96,32},{112,48},{1... | collective-permute-start | bytes 20 | tf_op jit(solution)/shard_map/ppermute | solution.py:377
  243.5 7.5 %collective-permute-start.8 = (f32[]{:T(128)}, f32[]{:T(128)}, u32[]{:S(2)}, u32[]{:S(2)}) collective-permute-start(f32[]{:T(128)} %add.44), channel_id=1, source_target_pairs={{0,128},{16,144},{32,160},{48,176},{64,192},{80,208},{96,224},{112... | collective-permute-start | bytes 20 | tf_op jit(solution)/shard_map/ppermute | solution.py:377
  251.6 9.8 %copy-start.2 = (bf16[16,2,128,256]{3,2,1,0:T(8,128)(2,1)S(1)}, bf16[16,2,128,256]{3,2,1,0:T(8,128)(2,1)}, u32[]{:S(2)}) copy-start(bf16[16,2,128,256]{3,2,1,0:T(8,128)(2,1)} %copy-done.1) | copy-start | bytes 6291460
  251.6 9.8 %copy-start.9 = (f32[16,128]{1,0:T(8,128)S(1)}, f32[16,128]{1,0:T(8,128)}, u32[]{:S(2)}) copy-start(f32[16,128]{1,0:T(8,128)} %add_add_fusion.logits_ref) | copy-start | bytes 24580
  251.6 9.8 %copy-start.10 = (f32[16,128]{1,0:T(8,128)S(1)}, f32[16,128]{1,0:T(8,128)}, u32[]{:S(2)}) copy-start(f32[16,128]{1,0:T(8,128)} %broadcast_in_dim.32.target_ref) | copy-start | bytes 24580
  254.4 32.2 %all-to-all-start.2 = ((bf16[16,1,128,256]{3,2,1,0:T(8,128)(2,1)}), bf16[16,1,128,256]{3,2,1,0:T(8,128)(2,1)S(1)}, u32[]{:S(2)}, u32[]{:S(2)}) async-start(bf16[16,1,128,256]{3,2,1,0:T(8,128)(2,1)} %second_terms.2), calls=%async_computation.2 | async-start | bytes 2097152 | tf_op jit(solution)/shard_map/all_to_all | solution.py:401
  286.5 1.2 copy-start.7

commit v3 on v1

v3 whole, which is shorter than its diff:
```python
import functools

import jax
import jax.numpy as jnp
from jax import lax
from jax.experimental import pallas as pl
from jax.experimental.pallas import tpu as pltpu
from jax.sharding import PartitionSpec as P

loss_scale = 8192.0
VMEM_BYTES = 24 * 1024 * 1024
SECOND_BYTES = 54 * 1024 * 1024
VMEM_ALL = 60 * 1024 * 1024
F32 = jnp.float32
BF16 = jnp.bfloat16
SMEM_SPEC = pl.BlockSpec(memory_space=pltpu.SMEM)
VMEM_SPEC = pl.BlockSpec(memory_space=pltpu.VMEM)
ANY_SPEC = pl.BlockSpec(memory_space=pl.ANY)


def params(limit=VMEM_BYTES):
    return pltpu.CompilerParams(vmem_limit_bytes=limit)


def mm(a, b, ca, cb):
    return lax.dot_general(a, b, (((ca,), (cb,)), ((), ())), preferred_element_type=F32)

HBM_SPEC = pl.BlockSpec(memory_space=pltpu.HBM)


def pick_kernel(member_ref, mol_ref, out_ref, hold_ref, in_sems, out_sems):
    slots = out_ref.shape[0]
    mols = mol_ref.shape[0]
    loads = [pltpu.make_async_copy(mol_ref.at[m], hold_ref.at[m], in_sems.at[m]) for m in range(mols)]
    for c in loads:
        c.start()
    for c in loads:
        c.wait()
    copies = [
        pltpu.make_async_copy(hold_ref.at[member_ref[s]], out_ref.at[s], out_sems.at[s]) for s in range(slots)
    ]
    for c in copies:
        c.start()
    for c in copies:
        c.wait()


def pick(member, mol):
    slots = member.shape[0]
    return pl.pallas_call(
        pick_kernel,
        out_shape=jax.ShapeDtypeStruct((slots,) + mol.shape[1:], mol.dtype),
        in_specs=[SMEM_SPEC, HBM_SPEC],
        out_specs=HBM_SPEC,
        scratch_shapes=[
            pltpu.VMEM(mol.shape, mol.dtype),
            pltpu.SemaphoreType.DMA((mol.shape[0],)),
            pltpu.SemaphoreType.DMA((slots,)),
        ],
        compiler_params=params(VMEM_ALL),
        name="pick_rows",
    )(member, mol)


def load_units(ids, first_ref, slot_ref, mol_ref, inc_ref, heads, hd, directions):
    units = []
    for h in range(heads):
        cols = slice(h * hd, (h + 1) * hd)
        for j, p in enumerate(ids):
            a, s = first_ref[p], slot_ref[p]
            for d in directions:
                if d == 0:
                    rows = (mol_ref[a, 0, :, cols], inc_ref[s, 1, :, cols], inc_ref[s, 2, :, cols])
                else:
                    rows = (inc_ref[s, 0, :, cols], mol_ref[a, 1, :, cols], mol_ref[a, 2, :, cols])
                units.append((j, d, h) + rows)
    return units


def forward_kernel(group, first_ref, slot_ref, mol_ref, inc_ref, proj_ref, readout_ref, lp_ref, w_ref, dh_ref):
    pairs = lp_ref.shape[0]
    length = mol_ref.shape[2]
    heads, hd, _ = proj_ref.shape
    inv_root = hd ** (-0.5)
    readouts = [readout_ref[h : h + 1, :] * (1.0 / length) for h in range(heads)]

    def step(i, carry):
        ids = [i * group + j for j in range(group)]
        units = load_units(ids, first_ref, slot_ref, mol_ref, inc_ref, heads, hd, (0, 1))
        scores = [mm(u[4], u[3], 1, 1) for u in units]
        weights = []
        for sc in scores:
            lifted = jnp.exp((sc - jnp.max(sc, axis=0, keepdims=True)) * inv_root)
            weights.append(lifted * (1.0 / jnp.sum(lifted, axis=0, keepdims=True)))
        context = [mm(w.astype(BF16), u[5], 0, 0).astype(BF16) for w, u in zip(weights, units)]
        count = len(units) // heads
        totals = [None] * group
        dhidden = []
        for h in range(heads):
            hidden = mm(jnp.concatenate(context[h * count : (h + 1) * count], axis=0), proj_ref[h], 1, 0)
            sig = 0.5 + 0.5 * jnp.tanh(0.5 * hidden)
            act = hidden * sig
            for j in range(group):
                rows = jnp.sum(act[2 * j * length : (2 * j + 2) * length], axis=0, keepdims=True) * readouts[h]
                totals[j] = rows if totals[j] is None else totals[j] + rows
            dhidden.append(((sig + act * (1.0 - sig)) * readouts[h]).astype(BF16))
        for j, p in enumerate(ids):
            total = jnp.sum(totals[j], axis=1, keepdims=True)
            lp_ref[pl.ds(p, 1), :] = jnp.broadcast_to(total, (1, lp_ref.shape[1]))
        for n, (j, d, h, *_) in enumerate(units):
            at = n - h * count
            w_ref[d, ids[j], h] = weights[n]
            dh_ref[d, ids[j], h] = dhidden[h][at * length : (at + 1) * length]
        return carry

    lax.fori_loop(0, pairs // group, step, 0)


def forward(first, slot, mol, inc, proj, readout):
    pairs = first.shape[0]
    length = mol.shape[2]
    heads, _, width = proj.shape
    return pl.pallas_call(
        functools.partial(forward_kernel, min(8, pairs)),
        out_shape=(
            jax.ShapeDtypeStruct((pairs, 128), F32),
            jax.ShapeDtypeStruct((2, pairs, heads, length, length), F32),
            jax.ShapeDtypeStruct((2, pairs, heads, length, width), BF16),
        ),
        in_specs=[SMEM_SPEC] * 2 + [VMEM_SPEC] * 4,
        out_specs=(VMEM_SPEC,) * 3,
        compiler_params=params(),
        name="pair_forward",
    )(first, slot, mol, inc, proj, readout)


def backward_kernel(direction, group, first_ref, slot_ref, mol_ref, inc_ref, proj_ref, w_ref, dh_ref, dq_ref, dkv_ref):
    pairs, length, _ = dq_ref.shape
    heads, hd, _ = proj_ref.shape
    inv_root = hd ** (-0.5)

    def step(i, carry):
        ids = [i * group + j for j in range(group)]
        units = load_units(ids, first_ref, slot_ref, mol_ref, inc_ref, heads, hd, (direction,))
        weights = [w_ref[0, ids[u[0]], u[2]] for u in units]
        dcontext = []
        for h in range(heads):
            dhidden = jnp.concatenate([dh_ref[0, p, h] for p in ids], axis=0)
            whole = mm(dhidden, proj_ref[h], 1, 1).astype(BF16)
            dcontext += [whole[j * length : (j + 1) * length] for j in range(group)]
        dvalues = [mm(w.astype(BF16), dc, 1, 0).astype(BF16) for w, dc in zip(weights, dcontext)]
        dweights = [mm(u[5], dc, 1, 1) for u, dc in zip(units, dcontext)]
        dscores = []
        for w, dw in zip(weights, dweights):
            inner = jnp.sum(dw * w, axis=0, keepdims=True)
            dscores.append((w * (dw - inner) * inv_root).astype(BF16))
        dqueries = [mm(ds, u[4], 0, 0).astype(BF16) for ds, u in zip(dscores, units)]
        dkeys = [mm(ds, u[3], 1, 0).astype(BF16) for ds, u in zip(dscores, units)]
        for n, (j, _, h, *_) in enumerate(units):
            cols = slice(h * hd, (h + 1) * hd)
            dq_ref[ids[j], :, cols] = dqueries[n]
            dkv_ref[ids[j], 0, :, cols] = dkeys[n]
            dkv_ref[ids[j], 1, :, cols] = dvalues[n]
        return carry

    lax.fori_loop(0, pairs // group, step, 0)


def backward(direction, first, slot, mol, inc, proj, weights, dhidden):
    pairs = first.shape[0]
    _, parts, length, width = mol.shape
    here = lambda i: (direction, 0, 0, 0, 0)
    return pl.pallas_call(
        functools.partial(backward_kernel, direction, min(16, pairs)),
        grid=(1,),
        out_shape=(
            jax.ShapeDtypeStruct((pairs, length, width), BF16),
            jax.ShapeDtypeStruct((pairs, parts - 1, length, width), BF16),
        ),
        in_specs=[SMEM_SPEC] * 2
        + [VMEM_SPEC] * 3
        + [pl.BlockSpec((1,) + weights.shape[1:], here), pl.BlockSpec((1,) + dhidden.shape[1:], here)],
        out_specs=(VMEM_SPEC,) * 2,
        compiler_params=params(),
        name="pair_backward",
    )(first, slot, mol, inc, proj, weights, dhidden)


def grad_scale(logits, target):
    scale = (0.5 + 0.5 * jnp.tanh(0.5 * logits) - target) * loss_scale
    return jnp.concatenate([scale, scale], axis=1)


def second_kernel(slot_ref, lead_ref, mate_ref, logits_ref, target_ref, dq_ref, dkv_ref, out_ref, scale_ref, hold_ref, sems):
    pairs = dq_ref.shape[0]
    scale_ref[...] = grad_scale(logits_ref[...], target_ref[...])

    def send(p):
        return pltpu.make_async_copy(hold_ref.at[p], out_ref.at[slot_ref[p]], sems.at[p])

    def part(p, c):
        return (dq_ref[p] if c == 0 else dkv_ref[p, c - 1]).astype(F32)

    def step(p, carry):
        mate = mate_ref[p]
        own = scale_ref[pl.ds(p, 1), :]

        @pl.when((lead_ref[p] == 1) & (mate < 0))
        def single():
            for c in range(3):
                hold_ref[p, c] = (own * part(p, c)).astype(BF16)
            send(p).start()

        @pl.when((lead_ref[p] == 1) & (mate >= 0))
        def double():
            at = jnp.maximum(mate, 0)
            other = scale_ref[pl.ds(at, 1), :]
            for c in range(3):
                hold_ref[p, c] = (own * part(p, c) + other * part(at, c)).astype(BF16)
            send(p).start()

        return carry

    lax.fori_loop(0, pairs, step, 0)

    def land(p, carry):
        @pl.when(lead_ref[p] == 1)
        def wait():
            send(p).wait()

        return carry

    lax.fori_loop(0, pairs, land, 0)


def second_terms(slot, lead, mate, logits, target, dq, dkv, slots):
    pairs, length, width = dq.shape
    return pl.pallas_call(
        second_kernel,
        out_shape=jax.ShapeDtypeStruct((slots, 3, length, width), BF16),
        in_specs=[SMEM_SPEC] * 3 + [VMEM_SPEC] * 4,
        out_specs=HBM_SPEC,
        scratch_shapes=[
            pltpu.VMEM((pairs, width), F32),
            pltpu.VMEM((pairs, 3, length, width), BF16),
            pltpu.SemaphoreType.DMA((pairs,)),
        ],
        compiler_params=params(SECOND_BYTES),
        name="second_terms",
    )(slot, lead, mate, logits, target, dq, dkv)


def first_kernel(first_ref, logits_ref, target_ref, dq_ref, dkv_ref, own_ref, scale_ref):
    pairs = dq_ref.shape[0]
    scale_ref[...] = grad_scale(logits_ref[...], target_ref[...])
    own_ref[...] = jnp.zeros_like(own_ref)

    def step(p, carry):
        a = first_ref[p]
        scale = scale_ref[pl.ds(p, 1), :]
        for c in range(3):
            own_ref[a, c] += scale * (dq_ref[p] if c == 0 else dkv_ref[p, c - 1]).astype(F32)
        return carry

    lax.fori_loop(0, pairs, step, 0)


def first_terms(first, logits, target, dq, dkv, mols):
    pairs, length, width = dq.shape
    return pl.pallas_call(
        first_kernel,
        out_shape=jax.ShapeDtypeStruct((mols, 3, length, width), F32),
        in_specs=[SMEM_SPEC] + [VMEM_SPEC] * 4,
        out_specs=VMEM_SPEC,
        scratch_shapes=[pltpu.VMEM((pairs, width), F32)],
        compiler_params=params(),
        name="first_terms",
    )(first, logits, target, dq, dkv)


def finish_kernel(code_ref, own_ref, back_ref, out_ref, sum_ref):
    slots = back_ref.shape[0]
    sum_ref[...] = own_ref[:, 0]

    def step(s, carry):
        m = code_ref[s]

        @pl.when(m >= 0)
        def add():
            sum_ref[jnp.maximum(m, 0)] += back_ref[s, 0].astype(F32)

        return carry

    lax.fori_loop(0, slots, step, 0)
    out_ref[:, 0] = sum_ref[...].astype(BF16)


def finish(code, own, back):
    mols, parts, length, width = own.shape
    slots = back.shape[0]
    part = lambda i: (0, i, 0, 0)
    return pl.pallas_call(
        finish_kernel,
        grid=(parts,),
        out_shape=jax.ShapeDtypeStruct(own.shape, BF16),
        in_specs=[
            SMEM_SPEC,
            pl.BlockSpec((mols, 1, length, width), part),
            pl.BlockSpec((slots, 1, length, width), part),
        ],
        out_specs=pl.BlockSpec((mols, 1, length, width), part),
        scratch_shapes=[pltpu.VMEM((mols, length, width), F32)],
        compiler_params=params(),
        name="finish_parts",
    )(code, own, back)


def hop(value, axis, size, change):
    return lax.ppermute(value, axis, [(i, change(i)) for i in range(size)])


def sum_quarter(value, recv):
    near, far, last = recv
    return (value + far) + (near + last)


def quarters(value, size):
    quarter = size // 4
    return [hop(value, "fsdp", size, lambda i: (i + k * quarter) % size) for k in (1, 2, 3)]


def sum_shards(value, size):
    step = 1
    while step < size // 4:
        value = value + hop(value, "fsdp", size, lambda i: i ^ step)
        step *= 2
    return sum_quarter(value, quarters(value, size))


def sum_shards_beside(value, size, first_work, second_work):
    step = 1
    while step < size // 8:
        value = value + hop(value, "fsdp", size, lambda i: i ^ step)
        step *= 2
    recv = hop(value, "fsdp", size, lambda i: i ^ step)
    done = first_work(value)
    recv, done = lax.optimization_barrier((recv, done))
    value = value + recv
    recv = quarters(value, size)
    more = second_work(value)
    recv, more = lax.optimization_barrier((recv, more))
    return sum_quarter(value, recv), done, more


def sum_groups(value, groups, shards):
    where = [(g * shards + f, (g ^ f) * shards + f) for g in range(groups) for f in range(shards)]
    return sum_shards(lax.ppermute(value, ("group", "fsdp"), where), shards)


def exchange(value):
    return lax.all_to_all(value, "group", split_axis=0, concat_axis=0, tiled=True)


def local(mol_qkv, pair_list, head_proj, head_out, labels):
    groups = lax.axis_size("group")
    shards = lax.axis_size("fsdp")
    device = lax.axis_index("group")
    mols = mol_qkv.shape[0]
    total_pairs = pair_list.shape[0]
    pairs = total_pairs // groups
    mol = jnp.transpose(mol_qkv, (0, 2, 1, 3))

    blocks = pair_list.T.reshape(3, groups, pairs)
    code = jnp.max(jnp.where(blocks[1] == device, blocks[2], -1), axis=1)
    mine = lax.dynamic_index_in_dim(blocks, device, 1, keepdims=False)
    first, slot = mine[0], mine[1]
    place = jnp.arange(pairs, dtype=jnp.int32)
    same = slot[:, None] == slot[None, :]
    lead = jnp.logical_not(jnp.any(same & (place[None, :] < place[:, None]), axis=1)).astype(jnp.int32)
    mate = jnp.max(jnp.where(same & (place[None, :] > place[:, None]), place[None, :], -1), axis=1)
    targets = labels.astype(F32)
    target_wide = jnp.broadcast_to(targets[:, None], (pairs, 128))

    inc = exchange(pick(jnp.maximum(code, 0), mol))
    inc, lead, mate, target_wide = lax.optimization_barrier((inc, lead, mate, target_wide))
    part, weights, dhidden = forward(first, slot, mol, inc, head_proj, head_out)

    def grads(direction):
        def work(after):
            index, _ = lax.optimization_barrier((first, after))
            return backward(direction, index, slot, mol, inc, head_proj, weights, dhidden)

        return work

    logits_wide, (dq_a, dkv_b), (dq_b, dkv_a) = sum_shards_beside(part, shards, grads(0), grads(1))

    back = exchange(second_terms(slot, lead, mate, logits_wide, target_wide, dq_b, dkv_b, groups))
    own = first_terms(first, logits_wide, target_wide, dq_a, dkv_a, mols)
    logits = logits_wide[:, 0]
    loss_terms = jax.nn.softplus(logits) - targets * logits
    mean_loss = sum_groups(jnp.sum(loss_terms), groups, shards) / total_pairs
    mol_grad = jnp.transpose(finish(code, own, back), (0, 2, 1, 3))
    return (mol_grad, logits, mean_loss)


def solution(mesh):
    placed = (
        P("group", None, None, "fsdp"),
        P(),
        P("fsdp", None, None),
        P("fsdp", None),
        P("group"),
    )
    return jax.shard_map(
        local,
        mesh=mesh,
        in_specs=placed,
        out_specs=(P("group", None, None, "fsdp"), P("group"), P()),
        check_vma=False,
    )
```

time: 238 us -> 226 us (0.950)
  waiting for transfers between devices: 120 us -> 136 us
  starting transfers between devices: 56.2 us -> 40.6 us
  Pallas kernels: 39.9 us -> 24.9 us
    ppermute x8 -> x11, waiting for transfers between devices: 19.6 us -> 62.4 us  [the longest x1 57.5 us: sum_groups(): return sum_shards(lax.ppermute(value, ('group', 'fsdp'), where), shards)]
    all_to_all x4 -> x2, waiting for transfers between devices: 101 us -> 73.3 us  [exchange(): lax.all_to_all(value, 'group', split_axis=0, concat_axis=0, tiled=True)]
    pallas_call x10 -> x7, Pallas kernels: 39.9 us -> 24.9 us  [the longest x1 6.47 us: forward(): pl.pallas_call(functools.partial(forward_kernel, min(8, pairs)), out_shap...]
    ppermute x8 -> x11, starting transfers between devices: 33 us -> 25.1 us  [the longest x10 20.4 us: hop(): return lax.ppermute(value, axis, [(i, change(i)) for i in range(size)])]
    all_to_all x4 -> x2, starting transfers between devices: 23.2 us -> 15.5 us  [exchange(): lax.all_to_all(value, 'group', split_axis=0, concat_axis=0, tiled=True)]
    unnamed x38 -> x34, local copies, waits for them, and re-layouts: 13.4 us -> 11.6 us
  transfers between devices with their start and end apart: 12 -> 13, of which waited for: 11 -> 6; matrix products, arithmetic and copies ran while one was open for 1% -> 1% of each run, Pallas kernels for 9% -> 3%
where the time goes in v3:
time: 226 us; the launch traced here: 224 us
  waiting for transfers between devices  136 us (60%)
  starting transfers between devices  40.6 us (18%)
  Pallas kernels  24.9 us (11%)
  local copies, waits for them, and re-layouts  12.5 us (6%)
  between operations  5.85 us (3%)
  other arithmetic  4.11 us (2%)
    all_to_all x2, waiting for transfers between devices, exchange(): lax.all_to_all(value, 'group', split_axis=0, concat_axis=0, tiled=True)  73.3 us
    ppermute x1, waiting for transfers between devices, sum_groups(): return sum_shards(lax.ppermute(value, ('group', 'fsdp'), where), shards)  57.5 us
    ppermute x10, starting transfers between devices, hop(): return lax.ppermute(value, axis, [(i, change(i)) for i in range(size)])  20.4 us
    all_to_all x2, starting transfers between devices, exchange(): lax.all_to_all(value, 'group', split_axis=0, concat_axis=0, tiled=True)  15.5 us
    unnamed x34, local copies, waits for them, and re-layouts  11.6 us
    pallas_call x1, Pallas kernels, forward(): pl.pallas_call(functools.partial(forward_kernel, min(8, pairs)), out_shap...  6.47 us
    pallas_call x2, Pallas kernels, backward(): pl.pallas_call(functools.partial(backward_kernel, direction, min(16, pair...  5.89 us
    ppermute x10, waiting for transfers between devices, hop(): return lax.ppermute(value, axis, [(i, change(i)) for i in range(size)])  4.87 us
  transfers between devices with their start and end apart: 13, of which 6 were waited for; matrix products, arithmetic and copies ran while one was open for 1% of the time, Pallas kernels for 3%

profile of v3, /device:TPU:8, one launch (start us, length us, event | category | flops | bytes accessed | tf_op | source)
XLA Modules:
  0.0 223.7 jit_solution(947665296380471656)
XLA Ops:
  0.6 0.8 fusion.1
  1.4 0.1 select_n.24
  1.5 0.1 reduce_max.18.code_ref
  1.6 0.5 broadcast_maximum_fusion.member_ref
  2.1 4.0 %pick_rows.1 = bf16[16,3,128,256]{3,2,1,0:T(8,128)(2,1)} custom-call(s32[16]{0:T(128)} %broadcast_maximum_fusion.member_ref, bf16[8,3,128,256]{3,2,1,0:T(8,128)(2,1)} %bitcast.7), custom_call_target="tpu_custom_call" | custom-call | tf_op jit(solution)/shard_map/pick_rows/pallas_call | solution.py:50
  6.1 0.0 copy-start.14
  6.2 0.0 copy-start.13
  6.2 11.2 %all-to-all-start = ((bf16[16,3,128,256]{3,2,1,0:T(8,128)(2,1)}), bf16[16,3,128,256]{3,2,1,0:T(8,128)(2,1)S(1)}, u32[]{:S(2)}, u32[]{:S(2)}) async-start(bf16[16,3,128,256]{3,2,1,0:T(8,128)(2,1)} %pick_rows.1), calls=%async_computation | async-start | bytes 6291456 | tf_op jit(solution)/shard_map/all_to_all | solution.py:361
  17.4 0.1 reshape.25
  17.5 0.2 fusion
  17.7 0.8 select_reduce_fusion.mate_ref
  18.4 0.5 not_convert_fusion.lead_ref
  18.9 73.3 %all-to-all-done.inc_ref = bf16[16,3,128,256]{3,2,1,0:T(8,128)(2,1)S(1)} async-done(((bf16[16,3,128,256]{3,2,1,0:T(8,128)(2,1)}), bf16[16,3,128,256]{3,2,1,0:T(8,128)(2,1)S(1)}, u32[]{:S(2)}, u32[]{:S(2)}) %all-to-all-start) | async-done | bytes 3145760 | tf_op jit(solution)/shard_map/all_to_all | solution.py:361
  92.3 0.7 broadcast_in_dim.18.target_ref
  92.9 1.4 copy-done
  94.3 6.5 %pair_forward.1 = (f32[16,128]{1,0:T(8,128)S(1)}, f32[2,16,2,128,128]{4,3,2,1,0:T(8,128)S(1)}, bf16[2,16,2,128,256]{4,3,2,1,0:T(8,128)(2,1)S(1)}) custom-call(s32[16]{0:T(128)S(1)} %get-tuple-element.32.first_ref, s32[16]{0:T(128)S(1)} %get-tuple-element.45.slot_ref, bf16[8,3,128,256]{3,2,1,0:T(8,128)(2,1)S(1)} %bitcast.8, ...), custom_call_target="tpu_custom_call" | custom-call | tf_op jit(solution)/shard_map/pair_forward/pallas_call | solution.py:123
  100.8 0.0 collective-permute-start
  100.8 1.2 collective-permute-done
  102.0 0.6 collective-permute-start.1
  102.6 3.0 %pair_backward.2 = (bf16[16,128,256]{2,1,0:T(8,128)(2,1)S(1)}, bf16[16,2,128,256]{3,2,1,0:T(8,128)(2,1)S(1)}) custom-call(s32[16]{0:T(128)S(1)} %get-tuple-element.32.first_ref, s32[16]{0:T(128)S(1)} %get-tuple-element.45.slot_ref, bf16[8,3,128,256]{3,2,1,0:T(8,128)(2,1)S(1)} %bitcast.9, bf16[16,3,128,256]{3,2,1,0:T(8,128)(2,1)S(1)} %all-to-all-done.inc_ref, ...), custom_call_target="tpu_custom_call" | custom-call | tf_op jit(solution)/shard_map/pair_backward/pallas_call | solution.py:173
  105.6 1.3 copy-done.5
  106.9 0.5 collective-permute-start.4
  107.4 2.6 %collective-permute-start.3 = (f32[16,128]{1,0:T(8,128)S(1)}, f32[16,128]{1,0:T(8,128)S(1)}, u32[]{:S(2)}, u32[]{:S(2)}) collective-permute-start(f32[16,128]{1,0:T(8,128)S(1)} %add.40), channel_id=1, source_target_pairs={{0,8},{1,9},{2,10},{3,11},{4,12},{5,13},{6,14},{7,15},{8,0},{9,1},... | collective-permute-start | bytes 24584 | tf_op jit(solution)/shard_map/ppermute | solution.py:319
  110.0 1.9 collective-permute-start.2
  111.9 2.9 %pair_backward.3 = (bf16[16,128,256]{2,1,0:T(8,128)(2,1)S(1)}, bf16[16,2,128,256]{3,2,1,0:T(8,128)(2,1)S(1)}) custom-call(s32[16]{0:T(128)S(1)} %get-tuple-element.32.first_ref, s32[16]{0:T(128)S(1)} %get-tuple-element.45.slot_ref, bf16[8,3,128,256]{3,2,1,0:T(8,128)(2,1)S(1)} %bitcast.10, bf16[16,3,128,256]{3,2,1,0:T(8,128)(2,1)S(1)} %all-to-all-done.inc_ref, ...), custom_call_target="tpu_custom_call" | custom-call | tf_op jit(solution)/shard_map/pair_backward/pallas_call | solution.py:173
  114.9 1.4 copy-done.3
  116.2 1.0 copy-done.9
  117.3 0.6 add_add_fusion.logits_ref
  117.9 3.8 %second_terms.1 = bf16[16,3,128,256]{3,2,1,0:T(8,128)(2,1)} custom-call(s32[16]{0:T(128)} %copy-done.12, s32[16]{0:T(128)} %not_convert_fusion.lead_ref, s32[16]{0:T(128)} %select_reduce_fusion.mate_ref, f32[16,128]{1,0:T(8,128)} %add_add_fusion.logits_ref, f32[16,128]{1,0:T(8,128)} %broadcast_in_dim.18.target_ref, bf16[16,128,256]{2,1,0:T(8,128)(2,1)} %copy-done.9, ...), custom_call_target="tpu_custom_call" | custom-call | tf_op jit(solution)/shard_map/second_terms/pallas_call | solution.py:238
  121.7 4.4 %all-to-all-start.1 = ((bf16[16,3,128,256]{3,2,1,0:T(8,128)(2,1)}), bf16[16,3,128,256]{3,2,1,0:T(8,128)(2,1)S(1)}, u32[]{:S(2)}, u32[]{:S(2)}) async-start(bf16[16,3,128,256]{3,2,1,0:T(8,128)(2,1)} %second_terms.1), calls=%async_computation.1 | async-start | bytes 6291456 | tf_op jit(solution)/shard_map/all_to_all | solution.py:361
  126.1 0.1 slice_reduce_fusion
  126.2 0.6 fusion.3
  126.8 4.7 %collective-permute-start.5 = (f32[]{:T(128)}, f32[]{:T(128)}, u32[]{:S(2)}, u32[]{:S(2)}) collective-permute-start(f32[]{:T(128)} %fusion.3), channel_id=1, source_target_pairs={{0,0},{1,17},{2,34},{3,51},{4,68},{5,85},{6,102},{7,119},{8,136},{... | collective-permute-start | bytes 20 | tf_op jit(solution)/shard_map/ppermute | solution.py:357
  131.6 1.6 copy-done.4
  133.2 1.2 copy-done.8
  134.4 1.4 first_terms.1.own_ref
  135.8 1.7 copy-done.1
  137.5 57.5 %collective-permute-done.5 = f32[]{:T(128)} collective-permute-done((f32[]{:T(128)}, f32[]{:T(128)}, u32[]{:S(2)}, u32[]{:S(2)}) %collective-permute-start.5) | collective-permute-done | bytes 36 | tf_op jit(solution)/shard_map/ppermute | solution.py:357
  195.0 1.3 collective-permute-start.6
  196.3 1.2 collective-permute-done.6
  198.7 6.0 %collective-permute-start.7 = (f32[]{:T(128)}, f32[]{:T(128)}, u32[]{:S(2)}, u32[]{:S(2)}) collective-permute-start(f32[]{:T(128)} %add.45), channel_id=1, source_target_pairs={{0,2},{1,3},{2,0},{3,1},{4,6},{5,7},{6,4},{7,5},{8,10},{9,11},{10,... | collective-permute-start | bytes 20 | tf_op jit(solution)/shard_map/ppermute | solution.py:319
  204.7 0.3 collective-permute-done.7
  205.7 1.4 collective-permute-start.10
  207.1 3.3 %collective-permute-start.9 = (f32[]{:T(128)}, f32[]{:T(128)}, u32[]{:S(2)}, u32[]{:S(2)}) collective-permute-start(f32[]{:T(128)} %add.46), channel_id=1, source_target_pairs={{0,4},{1,5},{2,6},{3,7},{4,8},{5,9},{6,10},{7,11},{8,12},{9,13},{1... | collective-permute-start | bytes 20 | tf_op jit(solution)/shard_map/ppermute | solution.py:319
  210.4 2.8 %collective-permute-start.8 = (f32[]{:T(128)}, f32[]{:T(128)}, u32[]{:S(2)}, u32[]{:S(2)}) collective-permute-start(f32[]{:T(128)} %add.46), channel_id=1, source_target_pairs={{0,8},{1,9},{2,10},{3,11},{4,12},{5,13},{6,14},{7,15},{8,0},{9,1},... | collective-permute-start | bytes 20 | tf_op jit(solution)/shard_map/ppermute | solution.py:319
  213.2 2.2 collective-permute-done.8
  217.3 1.9 copy-done.2
  219.2 3.4 %finish_parts.1 = bf16[8,3,128,256]{3,2,1,0:T(8,128)(2,1)} custom-call(s32[16]{0:T(128)S(1)} %reduce_max.18.code_ref, f32[8,3,128,256]{3,2,1,0:T(8,128)S(1)} %copy-done.2, bf16[16,3,128,256]{3,2,1,0:T(8,128)(2,1)S(1)} %all-to-all-done.1.back_ref), custom_call_target="tpu_custom_call" | custom-call | tf_op jit(solution)/shard_map/finish_parts/pallas_call | solution.py:302
  (35 shorter events, 0.1 us)
Async XLA Ops:
  6.1 11.2 %copy-start.14 = (s32[256,3]{0,1:T(4,128)S(1)}, s32[256,3]{0,1:T(4,128)}, u32[]{:S(2)}) copy-start(s32[256,3]{0,1:T(4,128)} %param.6) | copy-start | bytes 9220
  6.1 11.3 %copy-start.16 = (s32[16]{0:T(128)S(1)}, s32[16]{0:T(128)}, u32[]{:S(2)}) copy-start(s32[16]{0:T(128)} %param.9) | copy-start | bytes 196
  6.1 86.8 %copy-start.6 = (bf16[2,128,256]{2,1,0:T(8,128)(2,1)S(1)}, bf16[2,128,256]{2,1,0:T(8,128)(2,1)}, u32[]{:S(2)}) copy-start(bf16[2,128,256]{2,1,0:T(8,128)(2,1)} %proj_ref.5) | copy-start | bytes 393220
  6.2 86.8 %copy-start.13 = (f32[2,256]{1,0:T(2,128)S(1)}, f32[2,256]{1,0:T(2,128)}, u32[]{:S(2)}) copy-start(f32[2,256]{1,0:T(2,128)} %readout_ref.1) | copy-start | bytes 6148
  6.2 86.1 %all-to-all-start = ((bf16[16,3,128,256]{3,2,1,0:T(8,128)(2,1)}), bf16[16,3,128,256]{3,2,1,0:T(8,128)(2,1)S(1)}, u32[]{:S(2)}, u32[]{:S(2)}) async-start(bf16[16,3,128,256]{3,2,1,0:T(8,128)(2,1)} %pick_rows.1), calls=%async_computation | async-start | bytes 6291456 | tf_op jit(solution)/shard_map/all_to_all | solution.py:361
  17.5 94.5 %copy-start.12 = (s32[16]{0:T(128)}, s32[16]{0:T(128)S(1)}, u32[]{:S(2)}) copy-start(s32[16]{0:T(128)S(1)} %get-tuple-element.45.slot_ref) | copy-start | bytes 196
  92.9 1.4 copy-start
  100.8 1.2 collective-permute-start
  102.0 4.9 %collective-permute-start.1 = (f32[16,128]{1,0:T(8,128)S(1)}, f32[16,128]{1,0:T(8,128)S(1)}, u32[]{:S(2)}, u32[]{:S(2)}) collective-permute-start(f32[16,128]{1,0:T(8,128)S(1)} %add.39), channel_id=1, source_target_pairs={{0,2},{1,3},{2,0},{3,1},{4,6},{5,7},{6,4},{7,5},{8,10},{9,11},{10,... | collective-permute-start | bytes 24584 | tf_op jit(solution)/shard_map/ppermute | solution.py:319
  105.6 1.4 copy-start.5
  106.9 8.0 %copy-start.7 = (bf16[16,128,256]{2,1,0:T(8,128)(2,1)}, bf16[16,128,256]{2,1,0:T(8,128)(2,1)S(1)}, u32[]{:S(2)}) copy-start(bf16[16,128,256]{2,1,0:T(8,128)(2,1)S(1)} %get-tuple-element.39.dq_ref) | copy-start | bytes 3145732
  106.9 10.4 %collective-permute-start.4 = (f32[16,128]{1,0:T(8,128)S(1)}, f32[16,128]{1,0:T(8,128)S(1)}, u32[]{:S(2)}, u32[]{:S(2)}) collective-permute-start(f32[16,128]{1,0:T(8,128)S(1)} %add.40), channel_id=1, source_target_pairs={{0,12},{1,13},{2,14},{3,15},{4,0},{5,1},{6,2},{7,3},{8,4},{9,5},{1... | collective-permute-start | bytes 24584 | tf_op jit(solution)/shard_map/ppermute | solution.py:319
  107.4 9.8 %collective-permute-start.3 = (f32[16,128]{1,0:T(8,128)S(1)}, f32[16,128]{1,0:T(8,128)S(1)}, u32[]{:S(2)}, u32[]{:S(2)}) collective-permute-start(f32[16,128]{1,0:T(8,128)S(1)} %add.40), channel_id=1, source_target_pairs={{0,8},{1,9},{2,10},{3,11},{4,12},{5,13},{6,14},{7,15},{8,0},{9,1},... | collective-permute-start | bytes 24584 | tf_op jit(solution)/shard_map/ppermute | solution.py:319
  110.0 7.2 %collective-permute-start.2 = (f32[16,128]{1,0:T(8,128)S(1)}, f32[16,128]{1,0:T(8,128)S(1)}, u32[]{:S(2)}, u32[]{:S(2)}) collective-permute-start(f32[16,128]{1,0:T(8,128)S(1)} %add.40), channel_id=1, source_target_pairs={{0,4},{1,5},{2,6},{3,7},{4,8},{5,9},{6,10},{7,11},{8,12},{9,13},{1... | collective-permute-start | bytes 24584 | tf_op jit(solution)/shard_map/ppermute | solution.py:319
  114.9 1.4 copy-start.3
  116.2 1.0 copy-start.9
  121.7 4.4 %copy-start.10 = (f32[16,128]{1,0:T(8,128)S(1)}, f32[16,128]{1,0:T(8,128)}, u32[]{:S(2)}) copy-start(f32[16,128]{1,0:T(8,128)} %add_add_fusion.logits_ref) | copy-start | bytes 24580
  121.7 9.9 %copy-start.11 = (f32[16,128]{1,0:T(8,128)S(1)}, f32[16,128]{1,0:T(8,128)}, u32[]{:S(2)}) copy-start(f32[16,128]{1,0:T(8,128)} %broadcast_in_dim.18.target_ref) | copy-start | bytes 24580
  121.7 95.6 %all-to-all-start.1 = ((bf16[16,3,128,256]{3,2,1,0:T(8,128)(2,1)}), bf16[16,3,128,256]{3,2,1,0:T(8,128)(2,1)S(1)}, u32[]{:S(2)}, u32[]{:S(2)}) async-start(bf16[16,3,128,256]{3,2,1,0:T(8,128)(2,1)} %second_terms.1), calls=%async_computation.1 | async-start | bytes 6291456 | tf_op jit(solution)/shard_map/all_to_all | solution.py:361
  126.2 9.6 %copy-start.15 = (f32[16]{0:T(128)}, f32[16]{0:T(128)S(1)}, u32[]{:S(2)}) copy-start(f32[16]{0:T(128)S(1)} %slice_reduce_fusion) | copy-start | bytes 196
  126.8 68.2 %collective-permute-start.5 = (f32[]{:T(128)}, f32[]{:T(128)}, u32[]{:S(2)}, u32[]{:S(2)}) collective-permute-start(f32[]{:T(128)} %fusion.3), channel_id=1, source_target_pairs={{0,0},{1,17},{2,34},{3,51},{4,68},{5,85},{6,102},{7,119},{8,136},{... | collective-permute-start | bytes 20 | tf_op jit(solution)/shard_map/ppermute | solution.py:357
  131.6 1.6 copy-start.4
  133.2 1.2 copy-start.8
  135.8 1.7 copy-start.1
  195.0 2.5 %collective-permute-start.6 = (f32[]{:T(128)}, f32[]{:T(128)}, u32[]{:S(2)}, u32[]{:S(2)}) collective-permute-start(f32[]{:T(128)} %collective-permute-done.5), channel_id=1, source_target_pairs={{0,1},{1,0},{2,3},{3,2},{4,5},{5,4},{6,7},{7,6},{8,9},{9,8},{10,11... | collective-permute-start | bytes 20 | tf_op jit(solution)/shard_map/ppermute | solution.py:319
  198.7 6.3 %collective-permute-start.7 = (f32[]{:T(128)}, f32[]{:T(128)}, u32[]{:S(2)}, u32[]{:S(2)}) collective-permute-start(f32[]{:T(128)} %add.45), channel_id=1, source_target_pairs={{0,2},{1,3},{2,0},{3,1},{4,6},{5,7},{6,4},{7,5},{8,10},{9,11},{10,... | collective-permute-start | bytes 20 | tf_op jit(solution)/shard_map/ppermute | solution.py:319
  205.7 10.3 %collective-permute-start.10 = (f32[]{:T(128)}, f32[]{:T(128)}, u32[]{:S(2)}, u32[]{:S(2)}) collective-permute-start(f32[]{:T(128)} %add.46), channel_id=1, source_target_pairs={{0,12},{1,13},{2,14},{3,15},{4,0},{5,1},{6,2},{7,3},{8,4},{9,5},{1... | collective-permute-start | bytes 20 | tf_op jit(solution)/shard_map/ppermute | solution.py:319
  207.1 9.0 %collective-permute-start.9 = (f32[]{:T(128)}, f32[]{:T(128)}, u32[]{:S(2)}, u32[]{:S(2)}) collective-permute-start(f32[]{:T(128)} %add.46), channel_id=1, source_target_pairs={{0,4},{1,5},{2,6},{3,7},{4,8},{5,9},{6,10},{7,11},{8,12},{9,13},{1... | collective-permute-start | bytes 20 | tf_op jit(solution)/shard_map/ppermute | solution.py:319
  210.4 5.0 %collective-permute-start.8 = (f32[]{:T(128)}, f32[]{:T(128)}, u32[]{:S(2)}, u32[]{:S(2)}) collective-permute-start(f32[]{:T(128)} %add.46), channel_id=1, source_target_pairs={{0,8},{1,9},{2,10},{3,11},{4,12},{5,13},{6,14},{7,15},{8,0},{9,1},... | collective-permute-start | bytes 20 | tf_op jit(solution)/shard_map/ppermute | solution.py:319
  217.3 1.9 copy-start.2

commit v4 on v3

--- a/solution.py
+++ b/solution.py
@@ -9,7 +9,7 @@
 
 loss_scale = 8192.0
 VMEM_BYTES = 24 * 1024 * 1024
-SECOND_BYTES = 54 * 1024 * 1024
+SECOND_BYTES = 40 * 1024 * 1024
 VMEM_ALL = 60 * 1024 * 1024
 F32 = jnp.float32
 BF16 = jnp.bfloat16
@@ -310,7 +310,7 @@
         ],
         out_specs=pl.BlockSpec((mols, 1, length, width), part),
         scratch_shapes=[pltpu.VMEM((mols, length, width), F32)],
-        compiler_params=params(),
+        compiler_params=params(VMEM_ALL),
         name="finish_parts",
     )(code, own, back)
 
@@ -352,9 +352,9 @@
     return sum_quarter(value, recv), done, more
 
 
-def sum_groups(value, groups, shards):
+def turn_groups(value, groups, shards):
     where = [(g * shards + f, (g ^ f) * shards + f) for g in range(groups) for f in range(shards)]
-    return sum_shards(lax.ppermute(value, ("group", "fsdp"), where), shards)
+    return lax.ppermute(value, ("group", "fsdp"), where)
 
 
 def exchange(value):
@@ -394,11 +394,15 @@
 
     logits_wide, (dq_a, dkv_b), (dq_b, dkv_a) = sum_shards_beside(part, shards, grads(0), grads(1))
 
-    back = exchange(second_terms(slot, lead, mate, logits_wide, target_wide, dq_b, dkv_b, groups))
+    loss_wide = jax.nn.softplus(logits_wide) - target_wide * logits_wide
+    loss_moved = turn_groups(loss_wide, groups, shards)
+    out = second_terms(slot, lead, mate, logits_wide, target_wide, dq_b, dkv_b, groups)
+    out, loss_moved = lax.optimization_barrier((out, loss_moved))
+    back = exchange(out)
     own = first_terms(first, logits_wide, target_wide, dq_a, dkv_a, mols)
+    loss_sum = jnp.sum(sum_shards(loss_moved, shards)[:, 0])
+    mean_loss = loss_sum / total_pairs
     logits = logits_wide[:, 0]
-    loss_terms = jax.nn.softplus(logits) - targets * logits
-    mean_loss = sum_groups(jnp.sum(loss_terms), groups, shards) / total_pairs
     mol_grad = jnp.transpose(finish(code, own, back), (0, 2, 1, 3))
     return (mol_grad, logits, mean_loss)
 

time: 226 us -> 211 us (0.934)
  starting transfers between devices: 40.6 us -> 31.8 us
  local copies, waits for them, and re-layouts: 12.5 us -> 5.34 us
  waiting for transfers between devices: 136 us -> 140 us
  between operations: 5.85 us -> 2.64 us
    all_to_all x2, waiting for transfers between devices: 73.3 us -> 133 us  [exchange(): lax.all_to_all(value, 'group', split_axis=0, concat_axis=0, tiled=True)]
    ppermute x1, waiting for transfers between devices: 57.5 us -> 0.49 us  [turn_groups(): return lax.ppermute(value, ('group', 'fsdp'), where)]
    ppermute x10, starting transfers between devices: 20.4 us -> 12.4 us  [hop(): return lax.ppermute(value, axis, [(i, change(i)) for i in range(size)])]
    unnamed x34 -> x22, local copies, waits for them, and re-layouts: 11.6 us -> 4.47 us
  transfers between devices with their start and end apart: 13 -> 13, of which waited for: 6 -> 7; matrix products, arithmetic and copies ran while one was open for 1% -> 1% of each run, Pallas kernels for 3% -> 5%
where the time goes in v4:
time: 211 us; the launch traced here: 208 us
  waiting for transfers between devices  140 us (66%)
  starting transfers between devices  31.8 us (15%)
  Pallas kernels  25.4 us (12%)
  local copies, waits for them, and re-layouts  5.34 us (3%)
  between operations  2.64 us (1%)
  other arithmetic  2.43 us (1%)
    all_to_all x2, waiting for transfers between devices, exchange(): lax.all_to_all(value, 'group', split_axis=0, concat_axis=0, tiled=True)  133 us
    all_to_all x2, starting transfers between devices, exchange(): lax.all_to_all(value, 'group', split_axis=0, concat_axis=0, tiled=True)  15.8 us
    ppermute x10, starting transfers between devices, hop(): return lax.ppermute(value, axis, [(i, change(i)) for i in range(size)])  12.4 us
    ppermute x10, waiting for transfers between devices, hop(): return lax.ppermute(value, axis, [(i, change(i)) for i in range(size)])  6.75 us
    pallas_call x1, Pallas kernels, forward(): pl.pallas_call(functools.partial(forward_kernel, min(8, pairs)), out_shap...  6.38 us
    pallas_call x2, Pallas kernels, backward(): pl.pallas_call(functools.partial(backward_kernel, direction, min(16, pair...  5.82 us
    pallas_call x1, Pallas kernels, finish(): pl.pallas_call(finish_kernel, grid=(parts,), out_shape=jax.ShapeDtypeStru...  5.39 us
    unnamed x22, local copies, waits for them, and re-layouts  4.47 us
  transfers between devices with their start and end apart: 13, of which 7 were waited for; matrix products, arithmetic and copies ran while one was open for 1% of the time, Pallas kernels for 5%

profile of v4, /device:TPU:8, one launch (start us, length us, event | category | flops | bytes accessed | tf_op | source)
XLA Modules:
  0.0 207.7 jit_solution(11610158721050376849)
XLA Ops:
  0.6 0.8 fusion.4
  1.4 0.1 select_n.24
  1.5 0.1 reduce_max.18.code_ref
  1.6 0.5 broadcast_maximum_fusion.member_ref
  2.1 4.0 %pick_rows.1 = bf16[16,3,128,256]{3,2,1,0:T(8,128)(2,1)} custom-call(s32[16]{0:T(128)} %broadcast_maximum_fusion.member_ref, bf16[8,3,128,256]{3,2,1,0:T(8,128)(2,1)} %bitcast.7), custom_call_target="tpu_custom_call" | custom-call | tf_op jit(solution)/shard_map/pick_rows/pallas_call | solution.py:50
  6.1 0.0 copy-start.8
  6.1 0.0 copy-start.10
  6.1 0.0 copy-start.4
  6.1 0.0 copy-start.7
  6.2 11.2 %all-to-all-start = ((bf16[16,3,128,256]{3,2,1,0:T(8,128)(2,1)}), bf16[16,3,128,256]{3,2,1,0:T(8,128)(2,1)S(1)}, u32[]{:S(2)}, u32[]{:S(2)}) async-start(bf16[16,3,128,256]{3,2,1,0:T(8,128)(2,1)} %pick_rows.1), calls=%async_computation | async-start | bytes 6291456 | tf_op jit(solution)/shard_map/all_to_all | solution.py:361
  17.4 0.1 reshape.25
  17.5 0.2 fusion.3
  17.7 0.2 select_reduce_fusion.mate_ref
  17.9 74.4 %all-to-all-done.inc_ref = bf16[16,3,128,256]{3,2,1,0:T(8,128)(2,1)S(1)} async-done(((bf16[16,3,128,256]{3,2,1,0:T(8,128)(2,1)}), bf16[16,3,128,256]{3,2,1,0:T(8,128)(2,1)S(1)}, u32[]{:S(2)}, u32[]{:S(2)}) %all-to-all-start) | async-done | bytes 3145760 | tf_op jit(solution)/shard_map/all_to_all | solution.py:361
  92.3 0.1 broadcast_in_dim.18.target_ref
  92.3 1.4 copy-done
  93.7 6.4 %pair_forward.1 = (f32[16,128]{1,0:T(8,128)S(1)}, f32[2,16,2,128,128]{4,3,2,1,0:T(8,128)S(1)}, bf16[2,16,2,128,256]{4,3,2,1,0:T(8,128)(2,1)S(1)}) custom-call(s32[16]{0:T(128)S(1)} %get-tuple-element.34.first_ref, s32[16]{0:T(128)S(1)} %get-tuple-element.51.slot_ref, bf16[8,3,128,256]{3,2,1,0:T(8,128)(2,1)S(1)} %bitcast.8, ...), custom_call_target="tpu_custom_call" | custom-call | tf_op jit(solution)/shard_map/pair_forward/pallas_call | solution.py:123
  100.1 0.0 collective-permute-start
  100.2 1.2 collective-permute-done
  101.3 0.6 collective-permute-start.1
  101.9 2.9 %pair_backward.2 = (bf16[16,128,256]{2,1,0:T(8,128)(2,1)S(1)}, bf16[16,2,128,256]{3,2,1,0:T(8,128)(2,1)S(1)}) custom-call(s32[16]{0:T(128)S(1)} %get-tuple-element.34.first_ref, s32[16]{0:T(128)S(1)} %get-tuple-element.51.slot_ref, bf16[8,3,128,256]{3,2,1,0:T(8,128)(2,1)S(1)} %bitcast.9, bf16[16,3,128,256]{3,2,1,0:T(8,128)(2,1)S(1)} %all-to-all-done.inc_ref, ...), custom_call_target="tpu_custom_call" | custom-call | tf_op jit(solution)/shard_map/pair_backward/pallas_call | solution.py:173
  104.8 0.0 copy-start.5
  104.8 0.1 collective-permute-done.1
  105.0 0.4 collective-permute-start.4
  105.4 2.6 %collective-permute-start.3 = (f32[16,128]{1,0:T(8,128)S(1)}, f32[16,128]{1,0:T(8,128)S(1)}, u32[]{:S(2)}, u32[]{:S(2)}) collective-permute-start(f32[16,128]{1,0:T(8,128)S(1)} %add.40), channel_id=1, source_target_pairs={{0,8},{1,9},{2,10},{3,11},{4,12},{5,13},{6,14},{7,15},{8,0},{9,1},... | collective-permute-start | bytes 24584 | tf_op jit(solution)/shard_map/ppermute | solution.py:319
  108.0 1.9 collective-permute-start.2
  109.9 2.9 %pair_backward.3 = (bf16[16,128,256]{2,1,0:T(8,128)(2,1)S(1)}, bf16[16,2,128,256]{3,2,1,0:T(8,128)(2,1)S(1)}) custom-call(s32[16]{0:T(128)S(1)} %get-tuple-element.34.first_ref, s32[16]{0:T(128)S(1)} %get-tuple-element.51.slot_ref, bf16[8,3,128,256]{3,2,1,0:T(8,128)(2,1)S(1)} %bitcast.10, bf16[16,3,128,256]{3,2,1,0:T(8,128)(2,1)S(1)} %all-to-all-done.inc_ref, ...), custom_call_target="tpu_custom_call" | custom-call | tf_op jit(solution)/shard_map/pair_backward/pallas_call | solution.py:173
  112.9 1.4 copy-done.2
  114.2 0.0 collective-permute-done.4
  114.2 0.0 collective-permute-done.3
  114.2 0.0 collective-permute-done.2
  114.2 3.6 %collective-permute-start.5 = (f32[16,128]{1,0:T(8,128)S(1)}, f32[16,128]{1,0:T(8,128)S(1)}, u32[]{:S(2)}, u32[]{:S(2)}) collective-permute-start(f32[16,128]{1,0:T(8,128)S(1)} %get-tuple-element.49), channel_id=1, source_target_pairs={{0,0},{1,17},{2,34},{3,51},{4,68},{5,85},{6,102},{7,119},{8,136},{... | collective-permute-start | bytes 24584 | tf_op jit(solution)/shard_map/ppermute | solution.py:357
  117.8 2.4 %second_terms.1 = bf16[16,3,128,256]{3,2,1,0:T(8,128)(2,1)} custom-call(s32[16]{0:T(128)S(1)} %get-tuple-element.51.slot_ref, s32[16]{0:T(128)S(1)} %not_convert_fusion.lead_ref, s32[16]{0:T(128)S(1)} %select_reduce_fusion.mate_ref, f32[16,128]{1,0:T(8,128)S(1)} %get-tuple-element.50.logits_ref, f32[16,128]{1,0:T(8,128)S(1)} %broadcast_in_dim.18.target_ref, ...), custom_call_target="tpu_custom_call" | custom-call | tf_op jit(solution)/shard_map/second_terms/pallas_call | solution.py:238
  120.2 0.0 copy-start.6
  120.2 0.5 collective-permute-done.5
  120.7 4.6 %all-to-all-start.1 = ((bf16[16,3,128,256]{3,2,1,0:T(8,128)(2,1)}), bf16[16,3,128,256]{3,2,1,0:T(8,128)(2,1)}, u32[]{:S(2)}, u32[]{:S(2)}) async-start(bf16[16,3,128,256]{3,2,1,0:T(8,128)(2,1)} %second_terms.1), calls=%async_computation.1 | async-start | bytes 6291456 | tf_op jit(solution)/shard_map/all_to_all | solution.py:361
  125.3 0.2 collective-permute-start.6
  125.5 1.0 collective-permute-done.6
  126.6 2.2 %collective-permute-start.7 = (f32[16,128]{1,0:T(8,128)S(1)}, f32[16,128]{1,0:T(8,128)S(1)}, u32[]{:S(2)}, u32[]{:S(2)}) collective-permute-start(f32[16,128]{1,0:T(8,128)S(1)} %add.45), channel_id=1, source_target_pairs={{0,2},{1,3},{2,0},{3,1},{4,6},{5,7},{6,4},{7,5},{8,10},{9,11},{10,... | collective-permute-start | bytes 24584 | tf_op jit(solution)/shard_map/ppermute | solution.py:319
  128.7 4.4 %collective-permute-done.7 = f32[16,128]{1,0:T(8,128)S(1)} collective-permute-done((f32[16,128]{1,0:T(8,128)S(1)}, f32[16,128]{1,0:T(8,128)S(1)}, u32[]{:S(2)}, u32[]{:S(2)}) %collective-permute-start.7) | collective-permute-done | bytes 8224 | tf_op jit(solution)/shard_map/ppermute | solution.py:319
  133.1 2.0 collective-permute-start.9
  135.2 2.5 %collective-permute-start.8 = (f32[16,128]{1,0:T(8,128)S(1)}, f32[16,128]{1,0:T(8,128)S(1)}, u32[]{:S(2)}, u32[]{:S(2)}) collective-permute-start(f32[16,128]{1,0:T(8,128)S(1)} %add.46), channel_id=1, source_target_pairs={{0,8},{1,9},{2,10},{3,11},{4,12},{5,13},{6,14},{7,15},{8,0},{9,1},... | collective-permute-start | bytes 24584 | tf_op jit(solution)/shard_map/ppermute | solution.py:319
  137.6 0.6 slice_reduce_fusion
  138.3 1.5 first_terms.1.own_ref
  139.7 1.7 copy-done.1
  141.4 0.6 fusion.2
  142.7 58.5 %all-to-all-done.1.back_ref = bf16[16,3,128,256]{3,2,1,0:T(8,128)(2,1)} async-done(((bf16[16,3,128,256]{3,2,1,0:T(8,128)(2,1)}), bf16[16,3,128,256]{3,2,1,0:T(8,128)(2,1)}, u32[]{:S(2)}, u32[]{:S(2)}) %all-to-all-start.1) | async-done | bytes 3145760 | tf_op jit(solution)/shard_map/all_to_all | solution.py:361
  201.1 5.4 %finish_parts.1 = bf16[8,3,128,256]{3,2,1,0:T(8,128)(2,1)} custom-call(s32[16]{0:T(128)} %copy-done.9, f32[8,3,128,256]{3,2,1,0:T(8,128)} %copy-done.1, bf16[16,3,128,256]{3,2,1,0:T(8,128)(2,1)} %all-to-all-done.1.back_ref), custom_call_target="tpu_custom_call" | custom-call | tf_op jit(solution)/shard_map/finish_parts/pallas_call | solution.py:302
  (25 shorter events, 0.1 us)
Async XLA Ops:
  1.6 4.5 %copy-start.9 = (s32[16]{0:T(128)}, s32[16]{0:T(128)S(1)}, u32[]{:S(2)}) copy-start(s32[16]{0:T(128)S(1)} %reduce_max.18.code_ref) | copy-start | bytes 196
  6.1 11.2 %copy-start.8 = (s32[256,3]{0,1:T(4,128)S(1)}, s32[256,3]{0,1:T(4,128)}, u32[]{:S(2)}) copy-start(s32[256,3]{0,1:T(4,128)} %param.6) | copy-start | bytes 9220
  6.1 11.3 %copy-start.10 = (s32[16]{0:T(128)S(1)}, s32[16]{0:T(128)}, u32[]{:S(2)}) copy-start(s32[16]{0:T(128)} %param.9) | copy-start | bytes 196
  6.1 86.2 %copy-start.4 = (bf16[2,128,256]{2,1,0:T(8,128)(2,1)S(1)}, bf16[2,128,256]{2,1,0:T(8,128)(2,1)}, u32[]{:S(2)}) copy-start(bf16[2,128,256]{2,1,0:T(8,128)(2,1)} %proj_ref.5) | copy-start | bytes 393220
  6.1 86.2 %copy-start.7 = (f32[2,256]{1,0:T(2,128)S(1)}, f32[2,256]{1,0:T(2,128)}, u32[]{:S(2)}) copy-start(f32[2,256]{1,0:T(2,128)} %readout_ref.1) | copy-start | bytes 6148
  6.2 86.1 %all-to-all-start = ((bf16[16,3,128,256]{3,2,1,0:T(8,128)(2,1)}), bf16[16,3,128,256]{3,2,1,0:T(8,128)(2,1)S(1)}, u32[]{:S(2)}, u32[]{:S(2)}) async-start(bf16[16,3,128,256]{3,2,1,0:T(8,128)(2,1)} %pick_rows.1), calls=%async_computation | async-start | bytes 6291456 | tf_op jit(solution)/shard_map/all_to_all | solution.py:361
  92.3 1.4 copy-start
  100.1 1.2 collective-permute-start
  101.3 3.7 %collective-permute-start.1 = (f32[16,128]{1,0:T(8,128)S(1)}, f32[16,128]{1,0:T(8,128)S(1)}, u32[]{:S(2)}, u32[]{:S(2)}) collective-permute-start(f32[16,128]{1,0:T(8,128)S(1)} %add.39), channel_id=1, source_target_pairs={{0,2},{1,3},{2,0},{3,1},{4,6},{5,7},{6,4},{7,5},{8,10},{9,11},{10,... | collective-permute-start | bytes 24584 | tf_op jit(solution)/shard_map/ppermute | solution.py:319
  104.8 8.0 %copy-start.5 = (bf16[16,128,256]{2,1,0:T(8,128)(2,1)}, bf16[16,128,256]{2,1,0:T(8,128)(2,1)S(1)}, u32[]{:S(2)}) copy-start(bf16[16,128,256]{2,1,0:T(8,128)(2,1)S(1)} %get-tuple-element.41.dq_ref) | copy-start | bytes 3145732
  105.0 9.2 %collective-permute-start.4 = (f32[16,128]{1,0:T(8,128)S(1)}, f32[16,128]{1,0:T(8,128)S(1)}, u32[]{:S(2)}, u32[]{:S(2)}) collective-permute-start(f32[16,128]{1,0:T(8,128)S(1)} %add.40), channel_id=1, source_target_pairs={{0,12},{1,13},{2,14},{3,15},{4,0},{5,1},{6,2},{7,3},{8,4},{9,5},{1... | collective-permute-start | bytes 24584 | tf_op jit(solution)/shard_map/ppermute | solution.py:319
  105.4 8.8 %collective-permute-start.3 = (f32[16,128]{1,0:T(8,128)S(1)}, f32[16,128]{1,0:T(8,128)S(1)}, u32[]{:S(2)}, u32[]{:S(2)}) collective-permute-start(f32[16,128]{1,0:T(8,128)S(1)} %add.40), channel_id=1, source_target_pairs={{0,8},{1,9},{2,10},{3,11},{4,12},{5,13},{6,14},{7,15},{8,0},{9,1},... | collective-permute-start | bytes 24584 | tf_op jit(solution)/shard_map/ppermute | solution.py:319
  108.0 6.2 %collective-permute-start.2 = (f32[16,128]{1,0:T(8,128)S(1)}, f32[16,128]{1,0:T(8,128)S(1)}, u32[]{:S(2)}, u32[]{:S(2)}) collective-permute-start(f32[16,128]{1,0:T(8,128)S(1)} %add.40), channel_id=1, source_target_pairs={{0,4},{1,5},{2,6},{3,7},{4,8},{5,9},{6,10},{7,11},{8,12},{9,13},{1... | collective-permute-start | bytes 24584 | tf_op jit(solution)/shard_map/ppermute | solution.py:319
  112.8 1.4 copy-start.2
  114.2 6.4 %collective-permute-start.5 = (f32[16,128]{1,0:T(8,128)S(1)}, f32[16,128]{1,0:T(8,128)S(1)}, u32[]{:S(2)}, u32[]{:S(2)}) collective-permute-start(f32[16,128]{1,0:T(8,128)S(1)} %get-tuple-element.49), channel_id=1, source_target_pairs={{0,0},{1,17},{2,34},{3,51},{4,68},{5,85},{6,102},{7,119},{8,136},{... | collective-permute-start | bytes 24584 | tf_op jit(solution)/shard_map/ppermute | solution.py:357
  120.2 18.1 %copy-start.3 = (bf16[16,2,128,256]{3,2,1,0:T(8,128)(2,1)S(1)}, bf16[16,2,128,256]{3,2,1,0:T(8,128)(2,1)}, u32[]{:S(2)}) copy-start(bf16[16,2,128,256]{3,2,1,0:T(8,128)(2,1)} %copy-done.2) | copy-start | bytes 6291460
  120.2 18.1 %copy-start.6 = (bf16[16,128,256]{2,1,0:T(8,128)(2,1)S(1)}, bf16[16,128,256]{2,1,0:T(8,128)(2,1)}, u32[]{:S(2)}) copy-start(bf16[16,128,256]{2,1,0:T(8,128)(2,1)} %copy-done.5) | copy-start | bytes 3145732
  120.7 80.4 %all-to-all-start.1 = ((bf16[16,3,128,256]{3,2,1,0:T(8,128)(2,1)}), bf16[16,3,128,256]{3,2,1,0:T(8,128)(2,1)}, u32[]{:S(2)}, u32[]{:S(2)}) async-start(bf16[16,3,128,256]{3,2,1,0:T(8,128)(2,1)} %second_terms.1), calls=%async_computation.1 | async-start | bytes 6291456 | tf_op jit(solution)/shard_map/all_to_all | solution.py:361
  125.3 1.3 collective-permute-start.6
  126.6 6.6 %collective-permute-start.7 = (f32[16,128]{1,0:T(8,128)S(1)}, f32[16,128]{1,0:T(8,128)S(1)}, u32[]{:S(2)}, u32[]{:S(2)}) collective-permute-start(f32[16,128]{1,0:T(8,128)S(1)} %add.45), channel_id=1, source_target_pairs={{0,2},{1,3},{2,0},{3,1},{4,6},{5,7},{6,4},{7,5},{8,10},{9,11},{10,... | collective-permute-start | bytes 24584 | tf_op jit(solution)/shard_map/ppermute | solution.py:319
  133.1 8.3 %collective-permute-start.10 = (f32[16,128]{1,0:T(8,128)S(1)}, f32[16,128]{1,0:T(8,128)S(1)}, u32[]{:S(2)}, u32[]{:S(2)}) collective-permute-start(f32[16,128]{1,0:T(8,128)S(1)} %add.46), channel_id=1, source_target_pairs={{0,12},{1,13},{2,14},{3,15},{4,0},{5,1},{6,2},{7,3},{8,4},{9,5},{1... | collective-permute-start | bytes 24584 | tf_op jit(solution)/shard_map/ppermute | solution.py:319
  133.1 8.3 %collective-permute-start.9 = (f32[16,128]{1,0:T(8,128)S(1)}, f32[16,128]{1,0:T(8,128)S(1)}, u32[]{:S(2)}, u32[]{:S(2)}) collective-permute-start(f32[16,128]{1,0:T(8,128)S(1)} %add.46), channel_id=1, source_target_pairs={{0,4},{1,5},{2,6},{3,7},{4,8},{5,9},{6,10},{7,11},{8,12},{9,13},{1... | collective-permute-start | bytes 24584 | tf_op jit(solution)/shard_map/ppermute | solution.py:319
  135.2 6.3 %collective-permute-start.8 = (f32[16,128]{1,0:T(8,128)S(1)}, f32[16,128]{1,0:T(8,128)S(1)}, u32[]{:S(2)}, u32[]{:S(2)}) collective-permute-start(f32[16,128]{1,0:T(8,128)S(1)} %add.46), channel_id=1, source_target_pairs={{0,8},{1,9},{2,10},{3,11},{4,12},{5,13},{6,14},{7,15},{8,0},{9,1},... | collective-permute-start | bytes 24584 | tf_op jit(solution)/shard_map/ppermute | solution.py:319
  139.7 1.7 copy-start.1

commit v5 on v4

--- a/solution.py
+++ b/solution.py
@@ -9,6 +9,7 @@
 
 loss_scale = 8192.0
 VMEM_BYTES = 24 * 1024 * 1024
+FINISH_BYTES = 48 * 1024 * 1024
 SECOND_BYTES = 40 * 1024 * 1024
 VMEM_ALL = 60 * 1024 * 1024
 F32 = jnp.float32
@@ -28,25 +29,27 @@
 HBM_SPEC = pl.BlockSpec(memory_space=pltpu.HBM)
 
 
-def pick_kernel(member_ref, mol_ref, out_ref, hold_ref, in_sems, out_sems):
+def pick_kernel(code_ref, mol_ref, out_ref, hold_ref, in_sems, out_sems):
     slots = out_ref.shape[0]
     mols = mol_ref.shape[0]
     loads = [pltpu.make_async_copy(mol_ref.at[m], hold_ref.at[m], in_sems.at[m]) for m in range(mols)]
     for c in loads:
         c.start()
-    for c in loads:
-        c.wait()
-    copies = [
-        pltpu.make_async_copy(hold_ref.at[member_ref[s]], out_ref.at[s], out_sems.at[s]) for s in range(slots)
-    ]
-    for c in copies:
-        c.start()
-    for c in copies:
-        c.wait()
-
-
-def pick(member, mol):
-    slots = member.shape[0]
+    members = [jnp.maximum(code_ref[s], 0) for s in range(slots)]
+    for m in range(mols):
+        loads[m].wait()
+        for s in range(slots):
+
+            @pl.when(members[s] == m)
+            def send():
+                pltpu.make_async_copy(hold_ref.at[m], out_ref.at[s], out_sems.at[s]).start()
+
+    for s in range(slots):
+        pltpu.make_async_copy(hold_ref.at[members[s]], out_ref.at[s], out_sems.at[s]).wait()
+
+
+def pick(code, mol):
+    slots = code.shape[0]
     return pl.pallas_call(
         pick_kernel,
         out_shape=jax.ShapeDtypeStruct((slots,) + mol.shape[1:], mol.dtype),
@@ -59,7 +62,7 @@
         ],
         compiler_params=params(VMEM_ALL),
         name="pick_rows",
-    )(member, mol)
+    )(code, mol)
 
 
 def load_units(ids, first_ref, slot_ref, mol_ref, inc_ref, heads, hd, directions):
@@ -280,7 +283,8 @@
 
 def finish_kernel(code_ref, own_ref, back_ref, out_ref, sum_ref):
     slots = back_ref.shape[0]
-    sum_ref[...] = own_ref[:, 0]
+    c = pl.program_id(0)
+    sum_ref[...] = own_ref[:, c]
 
     def step(s, carry):
         m = code_ref[s]
@@ -297,20 +301,15 @@
 
 def finish(code, own, back):
     mols, parts, length, width = own.shape
-    slots = back.shape[0]
     part = lambda i: (0, i, 0, 0)
     return pl.pallas_call(
         finish_kernel,
         grid=(parts,),
         out_shape=jax.ShapeDtypeStruct(own.shape, BF16),
-        in_specs=[
-            SMEM_SPEC,
-            pl.BlockSpec((mols, 1, length, width), part),
-            pl.BlockSpec((slots, 1, length, width), part),
-        ],
+        in_specs=[SMEM_SPEC, VMEM_SPEC, pl.BlockSpec((back.shape[0], 1, length, width), part)],
         out_specs=pl.BlockSpec((mols, 1, length, width), part),
         scratch_shapes=[pltpu.VMEM((mols, length, width), F32)],
-        compiler_params=params(VMEM_ALL),
+        compiler_params=params(FINISH_BYTES),
         name="finish_parts",
     )(code, own, back)
 
@@ -381,7 +380,7 @@
     targets = labels.astype(F32)
     target_wide = jnp.broadcast_to(targets[:, None], (pairs, 128))
 
-    inc = exchange(pick(jnp.maximum(code, 0), mol))
+    inc = exchange(pick(code, mol))
     inc, lead, mate, target_wide = lax.optimization_barrier((inc, lead, mate, target_wide))
     part, weights, dhidden = forward(first, slot, mol, inc, head_proj, head_out)
 
@@ -392,7 +391,7 @@
 
         return work
 
-    logits_wide, (dq_a, dkv_b), (dq_b, dkv_a) = sum_shards_beside(part, shards, grads(0), grads(1))
+    logits_wide, (dq_b, dkv_a), (dq_a, dkv_b) = sum_shards_beside(part, shards, grads(1), grads(0))
 
     loss_wide = jax.nn.softplus(logits_wide) - target_wide * logits_wide
     loss_moved = turn_groups(loss_wide, groups, shards)

time: 211 us -> 208 us (0.986)
    unnamed x22 -> x20, local copies, waits for them, and re-layouts: 4.47 us -> 5.59 us
  transfers between devices with their start and end apart: 13 -> 13, of which waited for: 7 -> 6; matrix products, arithmetic and copies ran while one was open for 1% -> 1% of each run, Pallas kernels for 5% -> 5%
where the time goes in v5:
time: 208 us; the launch traced here: 206 us
  waiting for transfers between devices  139 us (67%)
  starting transfers between devices  32 us (15%)
  Pallas kernels  24 us (12%)
  local copies, waits for them, and re-layouts  6.46 us (3%)
  between operations  2.64 us (1%)
  other arithmetic  2.5 us (1%)
    all_to_all x2, waiting for transfers between devices, exchange(): lax.all_to_all(value, 'group', split_axis=0, concat_axis=0, tiled=True)  132 us
    all_to_all x2, starting transfers between devices, exchange(): lax.all_to_all(value, 'group', split_axis=0, concat_axis=0, tiled=True)  15.8 us
    ppermute x10, starting transfers between devices, hop(): return lax.ppermute(value, axis, [(i, change(i)) for i in range(size)])  12.6 us
    pallas_call x1, Pallas kernels, forward(): pl.pallas_call(functools.partial(forward_kernel, min(8, pairs)), out_shap...  6.35 us
    ppermute x10, waiting for transfers between devices, hop(): return lax.ppermute(value, axis, [(i, change(i)) for i in range(size)])  6.27 us
    pallas_call x2, Pallas kernels, backward(): pl.pallas_call(functools.partial(backward_kernel, direction, min(16, pair...  5.7 us
    unnamed x20, local copies, waits for them, and re-layouts  5.59 us
    pallas_call x1, Pallas kernels, finish(): pl.pallas_call(finish_kernel, grid=(parts,), out_shape=jax.ShapeDtypeStru...  4.55 us
  transfers between devices with their start and end apart: 13, of which 6 were waited for; matrix products, arithmetic and copies ran while one was open for 1% of the time, Pallas kernels for 5%

profile of v5, /device:TPU:8, one launch (start us, length us, event | category | flops | bytes accessed | tf_op | source)
XLA Modules:
  0.0 206.3 jit_solution(4179953522650463360)
XLA Ops:
  0.6 0.8 fusion.4
  1.4 0.1 select_n.24
  1.5 0.7 reduce_max.18.code_ref
  2.2 3.5 %pick_rows.1 = bf16[16,3,128,256]{3,2,1,0:T(8,128)(2,1)} custom-call(s32[16]{0:T(128)} %reduce_max.18.code_ref, bf16[8,3,128,256]{3,2,1,0:T(8,128)(2,1)} %bitcast.7), custom_call_target="tpu_custom_call" | custom-call | tf_op jit(solution)/shard_map/pick_rows/pallas_call | solution.py:53
  5.7 0.0 copy-start.8
  5.7 0.0 copy-start.9
  5.7 0.0 copy-start.3
  5.7 0.0 copy-start.7
  5.7 11.3 %all-to-all-start = ((bf16[16,3,128,256]{3,2,1,0:T(8,128)(2,1)}), bf16[16,3,128,256]{3,2,1,0:T(8,128)(2,1)S(1)}, u32[]{:S(2)}, u32[]{:S(2)}) async-start(bf16[16,3,128,256]{3,2,1,0:T(8,128)(2,1)} %pick_rows.1), calls=%async_computation | async-start | bytes 6291456 | tf_op jit(solution)/shard_map/all_to_all | solution.py:360
  17.1 0.1 reshape.25
  17.2 0.2 fusion.3
  17.4 0.2 select_reduce_fusion.mate_ref
  17.5 74.4 %all-to-all-done.inc_ref = bf16[16,3,128,256]{3,2,1,0:T(8,128)(2,1)S(1)} async-done(((bf16[16,3,128,256]{3,2,1,0:T(8,128)(2,1)}), bf16[16,3,128,256]{3,2,1,0:T(8,128)(2,1)S(1)}, u32[]{:S(2)}, u32[]{:S(2)}) %all-to-all-start) | async-done | bytes 3145760 | tf_op jit(solution)/shard_map/all_to_all | solution.py:360
  92.0 0.1 broadcast_in_dim.18.target_ref
  92.0 1.4 copy-done
  93.4 6.4 %pair_forward.1 = (f32[16,128]{1,0:T(8,128)S(1)}, f32[2,16,2,128,128]{4,3,2,1,0:T(8,128)S(1)}, bf16[2,16,2,128,256]{4,3,2,1,0:T(8,128)(2,1)S(1)}) custom-call(s32[16]{0:T(128)S(1)} %get-tuple-element.34.first_ref, s32[16]{0:T(128)S(1)} %get-tuple-element.51.slot_ref, bf16[8,3,128,256]{3,2,1,0:T(8,128)(2,1)S(1)} %bitcast.8, ...), custom_call_target="tpu_custom_call" | custom-call | tf_op jit(solution)/shard_map/pair_forward/pallas_call | solution.py:126
  99.8 0.0 collective-permute-start
  99.8 1.2 collective-permute-done
  101.0 0.6 collective-permute-start.1
  101.6 2.9 %pair_backward.2 = (bf16[16,128,256]{2,1,0:T(8,128)(2,1)S(1)}, bf16[16,2,128,256]{3,2,1,0:T(8,128)(2,1)S(1)}) custom-call(s32[16]{0:T(128)S(1)} %get-tuple-element.34.first_ref, s32[16]{0:T(128)S(1)} %get-tuple-element.51.slot_ref, bf16[8,3,128,256]{3,2,1,0:T(8,128)(2,1)S(1)} %bitcast.9, bf16[16,3,128,256]{3,2,1,0:T(8,128)(2,1)S(1)} %all-to-all-done.inc_ref, ...), custom_call_target="tpu_custom_call" | custom-call | tf_op jit(solution)/shard_map/pair_backward/pallas_call | solution.py:176
  104.5 1.3 copy-done.1
  105.8 0.4 collective-permute-start.4
  106.2 2.6 %collective-permute-start.3 = (f32[16,128]{1,0:T(8,128)S(1)}, f32[16,128]{1,0:T(8,128)S(1)}, u32[]{:S(2)}, u32[]{:S(2)}) collective-permute-start(f32[16,128]{1,0:T(8,128)S(1)} %add.40), channel_id=1, source_target_pairs={{0,8},{1,9},{2,10},{3,11},{4,12},{5,13},{6,14},{7,15},{8,0},{9,1},... | collective-permute-start | bytes 24584 | tf_op jit(solution)/shard_map/ppermute | solution.py:318
  108.8 1.9 collective-permute-start.2
  110.7 2.9 %pair_backward.3 = (bf16[16,128,256]{2,1,0:T(8,128)(2,1)S(1)}, bf16[16,2,128,256]{3,2,1,0:T(8,128)(2,1)S(1)}) custom-call(s32[16]{0:T(128)S(1)} %get-tuple-element.34.first_ref, s32[16]{0:T(128)S(1)} %get-tuple-element.51.slot_ref, bf16[8,3,128,256]{3,2,1,0:T(8,128)(2,1)S(1)} %bitcast.10, bf16[16,3,128,256]{3,2,1,0:T(8,128)(2,1)S(1)} %all-to-all-done.inc_ref, ...), custom_call_target="tpu_custom_call" | custom-call | tf_op jit(solution)/shard_map/pair_backward/pallas_call | solution.py:176
  113.6 0.0 copy-start.4
  113.6 0.0 collective-permute-done.4
  113.6 0.0 collective-permute-done.3
  113.6 3.6 %collective-permute-start.5 = (f32[16,128]{1,0:T(8,128)S(1)}, f32[16,128]{1,0:T(8,128)S(1)}, u32[]{:S(2)}, u32[]{:S(2)}) collective-permute-start(f32[16,128]{1,0:T(8,128)S(1)} %get-tuple-element.49), channel_id=1, source_target_pairs={{0,0},{1,17},{2,34},{3,51},{4,68},{5,85},{6,102},{7,119},{8,136},{... | collective-permute-start | bytes 24584 | tf_op jit(solution)/shard_map/ppermute | solution.py:356
  117.2 2.4 %second_terms.1 = bf16[16,3,128,256]{3,2,1,0:T(8,128)(2,1)} custom-call(s32[16]{0:T(128)S(1)} %get-tuple-element.51.slot_ref, s32[16]{0:T(128)S(1)} %not_convert_fusion.lead_ref, s32[16]{0:T(128)S(1)} %select_reduce_fusion.mate_ref, f32[16,128]{1,0:T(8,128)S(1)} %get-tuple-element.50.logits_ref, f32[16,128]{1,0:T(8,128)S(1)} %broadcast_in_dim.18.target_ref, ...), custom_call_target="tpu_custom_call" | custom-call | tf_op jit(solution)/shard_map/second_terms/pallas_call | solution.py:241
  119.6 0.5 collective-permute-done.5
  120.1 4.5 %all-to-all-start.1 = ((bf16[16,3,128,256]{3,2,1,0:T(8,128)(2,1)}), bf16[16,3,128,256]{3,2,1,0:T(8,128)(2,1)}, u32[]{:S(2)}, u32[]{:S(2)}) async-start(bf16[16,3,128,256]{3,2,1,0:T(8,128)(2,1)} %second_terms.1), calls=%async_computation.1 | async-start | bytes 6291456 | tf_op jit(solution)/shard_map/all_to_all | solution.py:360
  124.6 0.6 collective-permute-start.6
  125.1 0.9 collective-permute-done.6
  126.0 2.3 %collective-permute-start.7 = (f32[16,128]{1,0:T(8,128)S(1)}, f32[16,128]{1,0:T(8,128)S(1)}, u32[]{:S(2)}, u32[]{:S(2)}) collective-permute-start(f32[16,128]{1,0:T(8,128)S(1)} %add.45), channel_id=1, source_target_pairs={{0,2},{1,3},{2,0},{3,1},{4,6},{5,7},{6,4},{7,5},{8,10},{9,11},{10,... | collective-permute-start | bytes 24584 | tf_op jit(solution)/shard_map/ppermute | solution.py:318
  128.4 4.2 %collective-permute-done.7 = f32[16,128]{1,0:T(8,128)S(1)} collective-permute-done((f32[16,128]{1,0:T(8,128)S(1)}, f32[16,128]{1,0:T(8,128)S(1)}, u32[]{:S(2)}, u32[]{:S(2)}) %collective-permute-start.7) | collective-permute-done | bytes 8224 | tf_op jit(solution)/shard_map/ppermute | solution.py:318
  132.6 0.0 collective-permute-start.10
  132.6 2.0 collective-permute-start.9
  134.6 2.1 %collective-permute-start.8 = (f32[16,128]{1,0:T(8,128)S(1)}, f32[16,128]{1,0:T(8,128)S(1)}, u32[]{:S(2)}, u32[]{:S(2)}) collective-permute-start(f32[16,128]{1,0:T(8,128)S(1)} %add.46), channel_id=1, source_target_pairs={{0,8},{1,9},{2,10},{3,11},{4,12},{5,13},{6,14},{7,15},{8,0},{9,1},... | collective-permute-start | bytes 24584 | tf_op jit(solution)/shard_map/ppermute | solution.py:318
  136.7 0.6 slice_reduce_fusion
  137.4 1.6 copy-done.2
  139.0 1.2 copy-done.5
  140.2 1.6 first_terms.1.own_ref
  141.8 0.0 collective-permute-done.9
  141.8 0.0 collective-permute-done.8
  141.8 0.6 fusion.2
  143.0 57.6 %all-to-all-done.1.back_ref = bf16[16,3,128,256]{3,2,1,0:T(8,128)(2,1)} async-done(((bf16[16,3,128,256]{3,2,1,0:T(8,128)(2,1)}), bf16[16,3,128,256]{3,2,1,0:T(8,128)(2,1)}, u32[]{:S(2)}, u32[]{:S(2)}) %all-to-all-start.1) | async-done | bytes 3145760 | tf_op jit(solution)/shard_map/all_to_all | solution.py:360
  200.6 4.6 %finish_parts.1 = bf16[8,3,128,256]{3,2,1,0:T(8,128)(2,1)} custom-call(s32[16]{0:T(128)S(1)} %copy-done.6, f32[8,3,128,256]{3,2,1,0:T(8,128)S(1)} %first_terms.1.own_ref, bf16[16,3,128,256]{3,2,1,0:T(8,128)(2,1)} %all-to-all-done.1.back_ref), custom_call_target="tpu_custom_call" | custom-call | tf_op jit(solution)/shard_map/finish_parts/pallas_call | solution.py:305
  (22 shorter events, 0.1 us)
Async XLA Ops:
  5.7 11.4 %copy-start.8 = (s32[256,3]{0,1:T(4,128)S(1)}, s32[256,3]{0,1:T(4,128)}, u32[]{:S(2)}) copy-start(s32[256,3]{0,1:T(4,128)} %param.6) | copy-start | bytes 9220
  5.7 11.5 %copy-start.9 = (s32[16]{0:T(128)S(1)}, s32[16]{0:T(128)}, u32[]{:S(2)}) copy-start(s32[16]{0:T(128)} %param.9) | copy-start | bytes 196
  5.7 86.3 %copy-start.3 = (bf16[2,128,256]{2,1,0:T(8,128)(2,1)S(1)}, bf16[2,128,256]{2,1,0:T(8,128)(2,1)}, u32[]{:S(2)}) copy-start(bf16[2,128,256]{2,1,0:T(8,128)(2,1)} %proj_ref.5) | copy-start | bytes 393220
  5.7 86.3 %copy-start.7 = (f32[2,256]{1,0:T(2,128)S(1)}, f32[2,256]{1,0:T(2,128)}, u32[]{:S(2)}) copy-start(f32[2,256]{1,0:T(2,128)} %readout_ref.1) | copy-start | bytes 6148
  5.7 86.2 %all-to-all-start = ((bf16[16,3,128,256]{3,2,1,0:T(8,128)(2,1)}), bf16[16,3,128,256]{3,2,1,0:T(8,128)(2,1)S(1)}, u32[]{:S(2)}, u32[]{:S(2)}) async-start(bf16[16,3,128,256]{3,2,1,0:T(8,128)(2,1)} %pick_rows.1), calls=%async_computation | async-start | bytes 6291456 | tf_op jit(solution)/shard_map/all_to_all | solution.py:360
  92.0 1.4 copy-start
  99.8 1.2 collective-permute-start
  101.0 4.8 %collective-permute-start.1 = (f32[16,128]{1,0:T(8,128)S(1)}, f32[16,128]{1,0:T(8,128)S(1)}, u32[]{:S(2)}, u32[]{:S(2)}) collective-permute-start(f32[16,128]{1,0:T(8,128)S(1)} %add.39), channel_id=1, source_target_pairs={{0,2},{1,3},{2,0},{3,1},{4,6},{5,7},{6,4},{7,5},{8,10},{9,11},{10,... | collective-permute-start | bytes 24584 | tf_op jit(solution)/shard_map/ppermute | solution.py:318
  104.4 1.3 copy-start.1
  105.8 7.8 %collective-permute-start.4 = (f32[16,128]{1,0:T(8,128)S(1)}, f32[16,128]{1,0:T(8,128)S(1)}, u32[]{:S(2)}, u32[]{:S(2)}) collective-permute-start(f32[16,128]{1,0:T(8,128)S(1)} %add.40), channel_id=1, source_target_pairs={{0,12},{1,13},{2,14},{3,15},{4,0},{5,1},{6,2},{7,3},{8,4},{9,5},{1... | collective-permute-start | bytes 24584 | tf_op jit(solution)/shard_map/ppermute | solution.py:318
  106.2 7.4 %collective-permute-start.3 = (f32[16,128]{1,0:T(8,128)S(1)}, f32[16,128]{1,0:T(8,128)S(1)}, u32[]{:S(2)}, u32[]{:S(2)}) collective-permute-start(f32[16,128]{1,0:T(8,128)S(1)} %add.40), channel_id=1, source_target_pairs={{0,8},{1,9},{2,10},{3,11},{4,12},{5,13},{6,14},{7,15},{8,0},{9,1},... | collective-permute-start | bytes 24584 | tf_op jit(solution)/shard_map/ppermute | solution.py:318
  108.8 4.8 %collective-permute-start.2 = (f32[16,128]{1,0:T(8,128)S(1)}, f32[16,128]{1,0:T(8,128)S(1)}, u32[]{:S(2)}, u32[]{:S(2)}) collective-permute-start(f32[16,128]{1,0:T(8,128)S(1)} %add.40), channel_id=1, source_target_pairs={{0,4},{1,5},{2,6},{3,7},{4,8},{5,9},{6,10},{7,11},{8,12},{9,13},{1... | collective-permute-start | bytes 24584 | tf_op jit(solution)/shard_map/ppermute | solution.py:318
  113.6 6.0 %copy-start.4 = (bf16[16,128,256]{2,1,0:T(8,128)(2,1)}, bf16[16,128,256]{2,1,0:T(8,128)(2,1)S(1)}, u32[]{:S(2)}) copy-start(bf16[16,128,256]{2,1,0:T(8,128)(2,1)S(1)} %get-tuple-element.41.dq_ref) | copy-start | bytes 3145732
  113.6 6.4 %collective-permute-start.5 = (f32[16,128]{1,0:T(8,128)S(1)}, f32[16,128]{1,0:T(8,128)S(1)}, u32[]{:S(2)}, u32[]{:S(2)}) collective-permute-start(f32[16,128]{1,0:T(8,128)S(1)} %get-tuple-element.49), channel_id=1, source_target_pairs={{0,0},{1,17},{2,34},{3,51},{4,68},{5,85},{6,102},{7,119},{8,136},{... | collective-permute-start | bytes 24584 | tf_op jit(solution)/shard_map/ppermute | solution.py:356
  120.1 80.5 %all-to-all-start.1 = ((bf16[16,3,128,256]{3,2,1,0:T(8,128)(2,1)}), bf16[16,3,128,256]{3,2,1,0:T(8,128)(2,1)}, u32[]{:S(2)}, u32[]{:S(2)}) async-start(bf16[16,3,128,256]{3,2,1,0:T(8,128)(2,1)} %second_terms.1), calls=%async_computation.1 | async-start | bytes 6291456 | tf_op jit(solution)/shard_map/all_to_all | solution.py:360
  124.6 1.4 collective-permute-start.6
  126.0 6.5 %collective-permute-start.7 = (f32[16,128]{1,0:T(8,128)S(1)}, f32[16,128]{1,0:T(8,128)S(1)}, u32[]{:S(2)}, u32[]{:S(2)}) collective-permute-start(f32[16,128]{1,0:T(8,128)S(1)} %add.45), channel_id=1, source_target_pairs={{0,2},{1,3},{2,0},{3,1},{4,6},{5,7},{6,4},{7,5},{8,10},{9,11},{10,... | collective-permute-start | bytes 24584 | tf_op jit(solution)/shard_map/ppermute | solution.py:318
  132.6 9.2 %collective-permute-start.10 = (f32[16,128]{1,0:T(8,128)S(1)}, f32[16,128]{1,0:T(8,128)S(1)}, u32[]{:S(2)}, u32[]{:S(2)}) collective-permute-start(f32[16,128]{1,0:T(8,128)S(1)} %add.46), channel_id=1, source_target_pairs={{0,12},{1,13},{2,14},{3,15},{4,0},{5,1},{6,2},{7,3},{8,4},{9,5},{1... | collective-permute-start | bytes 24584 | tf_op jit(solution)/shard_map/ppermute | solution.py:318
  132.6 9.2 %collective-permute-start.9 = (f32[16,128]{1,0:T(8,128)S(1)}, f32[16,128]{1,0:T(8,128)S(1)}, u32[]{:S(2)}, u32[]{:S(2)}) collective-permute-start(f32[16,128]{1,0:T(8,128)S(1)} %add.46), channel_id=1, source_target_pairs={{0,4},{1,5},{2,6},{3,7},{4,8},{5,9},{6,10},{7,11},{8,12},{9,13},{1... | collective-permute-start | bytes 24584 | tf_op jit(solution)/shard_map/ppermute | solution.py:318
  134.6 7.2 %collective-permute-start.8 = (f32[16,128]{1,0:T(8,128)S(1)}, f32[16,128]{1,0:T(8,128)S(1)}, u32[]{:S(2)}, u32[]{:S(2)}) collective-permute-start(f32[16,128]{1,0:T(8,128)S(1)} %add.46), channel_id=1, source_target_pairs={{0,8},{1,9},{2,10},{3,11},{4,12},{5,13},{6,14},{7,15},{8,0},{9,1},... | collective-permute-start | bytes 24584 | tf_op jit(solution)/shard_map/ppermute | solution.py:318
  137.4 1.6 copy-start.2
  139.0 1.2 copy-start.5
  140.2 60.4 %copy-start.6 = (s32[16]{0:T(128)S(1)}, s32[16]{0:T(128)}, u32[]{:S(2)}) copy-start(s32[16]{0:T(128)} %reduce_max.18.code_ref) | copy-start | bytes 196

commit v6 on v5

--- a/solution.py
+++ b/solution.py
@@ -9,6 +9,7 @@
 
 loss_scale = 8192.0
 VMEM_BYTES = 24 * 1024 * 1024
+LOSS_ROWS = 16
 FINISH_BYTES = 48 * 1024 * 1024
 SECOND_BYTES = 40 * 1024 * 1024
 VMEM_ALL = 60 * 1024 * 1024
@@ -29,13 +30,20 @@
 HBM_SPEC = pl.BlockSpec(memory_space=pltpu.HBM)
 
 
-def pick_kernel(code_ref, mol_ref, out_ref, hold_ref, in_sems, out_sems):
+def pick_kernel(pairs_ref, mol_ref, out_ref, hold_ref, in_sems, out_sems):
     slots = out_ref.shape[0]
     mols = mol_ref.shape[0]
+    per_owner = pairs_ref.shape[1] // slots
+    here = lax.axis_index("group")
     loads = [pltpu.make_async_copy(mol_ref.at[m], hold_ref.at[m], in_sems.at[m]) for m in range(mols)]
     for c in loads:
         c.start()
-    members = [jnp.maximum(code_ref[s], 0) for s in range(slots)]
+    members = []
+    for s in range(slots):
+        member = jnp.int32(0)
+        for p in range(s * per_owner, (s + 1) * per_owner):
+            member = jnp.where(pairs_ref[1, p] == here, pairs_ref[2, p], member)
+        members.append(member)
     for m in range(mols):
         loads[m].wait()
         for s in range(slots):
@@ -48,8 +56,7 @@
         pltpu.make_async_copy(hold_ref.at[members[s]], out_ref.at[s], out_sems.at[s]).wait()
 
 
-def pick(code, mol):
-    slots = code.shape[0]
+def pick(pairs, mol, slots):
     return pl.pallas_call(
         pick_kernel,
         out_shape=jax.ShapeDtypeStruct((slots,) + mol.shape[1:], mol.dtype),
@@ -62,7 +69,7 @@
         ],
         compiler_params=params(VMEM_ALL),
         name="pick_rows",
-    )(code, mol)
+    )(pairs, mol)
 
 
 def load_units(ids, first_ref, slot_ref, mol_ref, inc_ref, heads, hd, directions):
@@ -194,12 +201,32 @@
     return jnp.concatenate([scale, scale], axis=1)
 
 
-def second_kernel(slot_ref, lead_ref, mate_ref, logits_ref, target_ref, dq_ref, dkv_ref, out_ref, scale_ref, hold_ref, sems):
-    pairs = dq_ref.shape[0]
+def three_parts(value):
+    high = value.astype(BF16).astype(F32)
+    middle = (value - high).astype(BF16).astype(F32)
+    low = value - high - middle
+    row = lax.broadcasted_iota(jnp.int32, (LOSS_ROWS, value.shape[1]), 0)
+    rows = jnp.where(row == 0, high, jnp.where(row == 1, middle, jnp.where(row == 2, low, 0.0)))
+    return rows.astype(BF16)
+
+
+def second_kernel(
+    slot_ref, lead_ref, mate_ref, logits_ref, target_ref, loss_ref, dq_ref, dkv_ref, out_ref, scale_ref, hold_ref, tail_ref, sems, tail_sems
+):
+    pairs, length, _ = dq_ref.shape
+    slots = out_ref.shape[0]
+    rows = 3 * length
+    loss = jnp.sum(loss_ref[...], axis=0, keepdims=True)
+    tail_ref[...] = three_parts(jnp.concatenate([loss, loss], axis=1))
+    tails = [
+        pltpu.make_async_copy(tail_ref, out_ref.at[s, pl.ds(rows, LOSS_ROWS)], tail_sems.at[s]) for s in range(slots)
+    ]
+    for c in tails:
+        c.start()
     scale_ref[...] = grad_scale(logits_ref[...], target_ref[...])
 
     def send(p):
-        return pltpu.make_async_copy(hold_ref.at[p], out_ref.at[slot_ref[p]], sems.at[p])
+        return pltpu.make_async_copy(hold_ref.at[p], out_ref.at[slot_ref[p], pl.ds(0, rows)], sems.at[p])
 
     def part(p, c):
         return (dq_ref[p] if c == 0 else dkv_ref[p, c - 1]).astype(F32)
@@ -211,7 +238,7 @@
         @pl.when((lead_ref[p] == 1) & (mate < 0))
         def single():
             for c in range(3):
-                hold_ref[p, c] = (own * part(p, c)).astype(BF16)
+                hold_ref[p, c * length : (c + 1) * length] = (own * part(p, c)).astype(BF16)
             send(p).start()
 
         @pl.when((lead_ref[p] == 1) & (mate >= 0))
@@ -219,7 +246,7 @@
             at = jnp.maximum(mate, 0)
             other = scale_ref[pl.ds(at, 1), :]
             for c in range(3):
-                hold_ref[p, c] = (own * part(p, c) + other * part(at, c)).astype(BF16)
+                hold_ref[p, c * length : (c + 1) * length] = (own * part(p, c) + other * part(at, c)).astype(BF16)
             send(p).start()
 
         return carry
@@ -234,23 +261,27 @@
         return carry
 
     lax.fori_loop(0, pairs, land, 0)
-
-
-def second_terms(slot, lead, mate, logits, target, dq, dkv, slots):
+    for c in tails:
+        c.wait()
+
+
+def second_terms(slot, lead, mate, logits, target, loss, dq, dkv, slots):
     pairs, length, width = dq.shape
     return pl.pallas_call(
         second_kernel,
-        out_shape=jax.ShapeDtypeStruct((slots, 3, length, width), BF16),
-        in_specs=[SMEM_SPEC] * 3 + [VMEM_SPEC] * 4,
+        out_shape=jax.ShapeDtypeStruct((slots, 3 * length + LOSS_ROWS, width), BF16),
+        in_specs=[SMEM_SPEC] * 3 + [VMEM_SPEC] * 5,
         out_specs=HBM_SPEC,
         scratch_shapes=[
             pltpu.VMEM((pairs, width), F32),
-            pltpu.VMEM((pairs, 3, length, width), BF16),
+            pltpu.VMEM((pairs, 3 * length, width), BF16),
+            pltpu.VMEM((LOSS_ROWS, width), BF16),
             pltpu.SemaphoreType.DMA((pairs,)),
+            pltpu.SemaphoreType.DMA((slots,)),
         ],
         compiler_params=params(SECOND_BYTES),
         name="second_terms",
-    )(slot, lead, mate, logits, target, dq, dkv)
+    )(slot, lead, mate, logits, target, loss, dq, dkv)
 
 
 def first_kernel(first_ref, logits_ref, target_ref, dq_ref, dkv_ref, own_ref, scale_ref):
@@ -281,37 +312,50 @@
     )(first, logits, target, dq, dkv)
 
 
-def finish_kernel(code_ref, own_ref, back_ref, out_ref, sum_ref):
+def finish_kernel(code_ref, own_ref, back_ref, tail_ref, out_ref, loss_ref, sum_ref):
     slots = back_ref.shape[0]
     c = pl.program_id(0)
     sum_ref[...] = own_ref[:, c]
 
+    @pl.when(c == 0)
+    def loss():
+        total = tail_ref[0].astype(F32)
+        for s in range(1, slots):
+            total = total + tail_ref[s].astype(F32)
+        loss_ref[...] = jnp.broadcast_to(jnp.sum(total, axis=0, keepdims=True)[:, :128], loss_ref.shape)
+
     def step(s, carry):
         m = code_ref[s]
 
         @pl.when(m >= 0)
         def add():
-            sum_ref[jnp.maximum(m, 0)] += back_ref[s, 0].astype(F32)
-
-        return carry
-
-    lax.fori_loop(0, slots, step, 0)
+            sum_ref[jnp.maximum(m, 0)] += back_ref[s].astype(F32)
+
+        return carry
+
+    lax.fori_loop(0, slots, step, 0, unroll=True)
     out_ref[:, 0] = sum_ref[...].astype(BF16)
 
 
 def finish(code, own, back):
     mols, parts, length, width = own.shape
+    slots = back.shape[0]
     part = lambda i: (0, i, 0, 0)
     return pl.pallas_call(
         finish_kernel,
         grid=(parts,),
-        out_shape=jax.ShapeDtypeStruct(own.shape, BF16),
-        in_specs=[SMEM_SPEC, VMEM_SPEC, pl.BlockSpec((back.shape[0], 1, length, width), part)],
-        out_specs=pl.BlockSpec((mols, 1, length, width), part),
+        out_shape=(jax.ShapeDtypeStruct(own.shape, BF16), jax.ShapeDtypeStruct((8, 128), F32)),
+        in_specs=[
+            SMEM_SPEC,
+            VMEM_SPEC,
+            pl.BlockSpec((slots, length, width), lambda i: (0, i, 0)),
+            pl.BlockSpec((slots, LOSS_ROWS, width), lambda i: (0, parts * length // LOSS_ROWS, 0)),
+        ],
+        out_specs=(pl.BlockSpec((mols, 1, length, width), part), pl.BlockSpec((8, 128), lambda i: (0, 0))),
         scratch_shapes=[pltpu.VMEM((mols, length, width), F32)],
         compiler_params=params(FINISH_BYTES),
         name="finish_parts",
-    )(code, own, back)
+    )(code, own, back, back)
 
 
 def hop(value, axis, size, change):
@@ -326,14 +370,6 @@
 def quarters(value, size):
     quarter = size // 4
     return [hop(value, "fsdp", size, lambda i: (i + k * quarter) % size) for k in (1, 2, 3)]
-
-
-def sum_shards(value, size):
-    step = 1
-    while step < size // 4:
-        value = value + hop(value, "fsdp", size, lambda i: i ^ step)
-        step *= 2
-    return sum_quarter(value, quarters(value, size))
 
 
 def sum_shards_beside(value, size, first_work, second_work):
@@ -351,11 +387,6 @@
     return sum_quarter(value, recv), done, more
 
 
-def turn_groups(value, groups, shards):
-    where = [(g * shards + f, (g ^ f) * shards + f) for g in range(groups) for f in range(shards)]
-    return lax.ppermute(value, ("group", "fsdp"), where)
-
-
 def exchange(value):
     return lax.all_to_all(value, "group", split_axis=0, concat_axis=0, tiled=True)
 
@@ -380,7 +411,7 @@
     targets = labels.astype(F32)
     target_wide = jnp.broadcast_to(targets[:, None], (pairs, 128))
 
-    inc = exchange(pick(code, mol))
+    inc = exchange(pick(pair_list.T, mol, groups))
     inc, lead, mate, target_wide = lax.optimization_barrier((inc, lead, mate, target_wide))
     part, weights, dhidden = forward(first, slot, mol, inc, head_proj, head_out)
 
@@ -394,15 +425,13 @@
     logits_wide, (dq_b, dkv_a), (dq_a, dkv_b) = sum_shards_beside(part, shards, grads(1), grads(0))
 
     loss_wide = jax.nn.softplus(logits_wide) - target_wide * logits_wide
-    loss_moved = turn_groups(loss_wide, groups, shards)
-    out = second_terms(slot, lead, mate, logits_wide, target_wide, dq_b, dkv_b, groups)
-    out, loss_moved = lax.optimization_barrier((out, loss_moved))
+    out = second_terms(slot, lead, mate, logits_wide, target_wide, loss_wide, dq_b, dkv_b, groups)
     back = exchange(out)
     own = first_terms(first, logits_wide, target_wide, dq_a, dkv_a, mols)
-    loss_sum = jnp.sum(sum_shards(loss_moved, shards)[:, 0])
-    mean_loss = loss_sum / total_pairs
     logits = logits_wide[:, 0]
-    mol_grad = jnp.transpose(finish(code, own, back), (0, 2, 1, 3))
+    grads, loss_sum = finish(code, own, back)
+    mean_loss = loss_sum[0, 0] / total_pairs
+    mol_grad = jnp.transpose(grads, (0, 2, 1, 3))
     return (mol_grad, logits, mean_loss)
 
 

time: 208 us -> 204 us (0.981)
  starting transfers between devices: 32 us -> 21.1 us
  waiting for transfers between devices: 139 us -> 147 us
    all_to_all x2, waiting for transfers between devices: 132 us -> 146 us  [exchange(): lax.all_to_all(value, 'group', split_axis=0, concat_axis=0, tiled=True)]
    ppermute x10 -> x5, starting transfers between devices: 12.6 us -> 5.53 us  [hop(): return lax.ppermute(value, axis, [(i, change(i)) for i in range(size)])]
    ppermute x10 -> x5, waiting for transfers between devices: 6.27 us -> 1.17 us  [hop(): return lax.ppermute(value, axis, [(i, change(i)) for i in range(size)])]
    ppermute x1 -> x0, starting transfers between devices: 3.56 us -> none  [turn_groups(): return lax.ppermute(value, ('group', 'fsdp'), where)]
    unnamed x20 -> x18, local copies, waits for them, and re-layouts: 5.59 us -> 6.59 us
  transfers between devices with their start and end apart: 13 -> 7, of which waited for: 6 -> 3; matrix products, arithmetic and copies ran while one was open for 1% -> 1% of each run, Pallas kernels for 5% -> 4%
where the time goes in v6:
time: 204 us
  waiting for transfers between devices  147 us (72%)
  Pallas kernels  24.4 us (12%)
  starting transfers between devices  21.1 us (10%)
  local copies, waits for them, and re-layouts  7.97 us (4%)
  between operations  2.58 us (1%)
    all_to_all x2, waiting for transfers between devices, exchange(): lax.all_to_all(value, 'group', split_axis=0, concat_axis=0, tiled=True)  146 us
    all_to_all x2, starting transfers between devices, exchange(): lax.all_to_all(value, 'group', split_axis=0, concat_axis=0, tiled=True)  15.6 us
    unnamed x18, local copies, waits for them, and re-layouts  6.59 us
    pallas_call x1, Pallas kernels, forward(): pl.pallas_call(functools.partial(forward_kernel, min(8, pairs)), out_shap...  6.41 us
    pallas_call x2, Pallas kernels, backward(): pl.pallas_call(functools.partial(backward_kernel, direction, min(16, pair...  5.84 us
    ppermute x5, starting transfers between devices, hop(): return lax.ppermute(value, axis, [(i, change(i)) for i in range(size)])  5.53 us
    pallas_call x1, Pallas kernels, finish(): pl.pallas_call(finish_kernel, grid=(parts,), out_shape=(jax.ShapeDtypeStr...  4.4 us
  transfers between devices with their start and end apart: 7, of which 3 were waited for; matrix products, arithmetic and copies ran while one was open for 1% of the time, Pallas kernels for 4%

profile of v6, /device:TPU:8, one launch (start us, length us, event | category | flops | bytes accessed | tf_op | source)
XLA Modules:
  0.0 204.0 jit_solution(4796429156180683904)
XLA Ops:
  0.6 3.6 %pick_rows.1 = bf16[16,3,128,256]{3,2,1,0:T(8,128)(2,1)} custom-call(s32[3,256]{1,0:T(4,128)} %bitcast.12, bf16[8,3,128,256]{3,2,1,0:T(8,128)(2,1)} %bitcast.8), custom_call_target="tpu_custom_call" | custom-call | tf_op jit(solution)/shard_map/pick_rows/pallas_call | solution.py:60
  4.3 0.0 copy-start.7
  4.3 0.0 copy-start.8
  4.3 0.0 copy-start.3
  4.3 0.0 copy-start.6
  4.3 11.1 %all-to-all-start = ((bf16[16,3,128,256]{3,2,1,0:T(8,128)(2,1)}), bf16[16,3,128,256]{3,2,1,0:T(8,128)(2,1)S(1)}, u32[]{:S(2)}, u32[]{:S(2)}) async-start(bf16[16,3,128,256]{3,2,1,0:T(8,128)(2,1)} %pick_rows.1), calls=%async_computation | async-start | bytes 6291456 | tf_op jit(solution)/shard_map/all_to_all | solution.py:391
  15.4 0.0 copy-done.7
  15.4 0.1 reshape.27
  15.5 0.0 copy-done.8
  15.5 0.2 fusion.1
  15.7 0.2 select_reduce_fusion.mate_ref
  15.9 74.4 %all-to-all-done.inc_ref = bf16[16,3,128,256]{3,2,1,0:T(8,128)(2,1)S(1)} async-done(((bf16[16,3,128,256]{3,2,1,0:T(8,128)(2,1)}), bf16[16,3,128,256]{3,2,1,0:T(8,128)(2,1)S(1)}, u32[]{:S(2)}, u32[]{:S(2)}) %all-to-all-start) | async-done | bytes 3145760 | tf_op jit(solution)/shard_map/all_to_all | solution.py:391
  90.3 0.1 broadcast_in_dim.18.target_ref
  90.4 0.0 copy-done.3
  90.4 0.0 copy-done.6
  90.4 0.0 copy-start
  90.4 1.4 copy-done
  91.8 6.4 %pair_forward.1 = (f32[16,128]{1,0:T(8,128)S(1)}, f32[2,16,2,128,128]{4,3,2,1,0:T(8,128)S(1)}, bf16[2,16,2,128,256]{4,3,2,1,0:T(8,128)(2,1)S(1)}) custom-call(s32[16]{0:T(128)S(1)} %get-tuple-element.34.first_ref, s32[16]{0:T(128)S(1)} %get-tuple-element.51.slot_ref, bf16[8,3,128,256]{3,2,1,0:T(8,128)(2,1)S(1)} %bitcast.9, ...), custom_call_target="tpu_custom_call" | custom-call | tf_op jit(solution)/shard_map/pair_forward/pallas_call | solution.py:133
  98.2 0.0 collective-permute-start
  98.2 1.2 collective-permute-done
  99.4 0.6 collective-permute-start.1
  100.0 2.9 %pair_backward.2 = (bf16[16,128,256]{2,1,0:T(8,128)(2,1)S(1)}, bf16[16,2,128,256]{3,2,1,0:T(8,128)(2,1)S(1)}) custom-call(s32[16]{0:T(128)S(1)} %get-tuple-element.34.first_ref, s32[16]{0:T(128)S(1)} %get-tuple-element.51.slot_ref, bf16[8,3,128,256]{3,2,1,0:T(8,128)(2,1)S(1)} %bitcast.10, bf16[16,3,128,256]{3,2,1,0:T(8,128)(2,1)S(1)} %all-to-all-done.inc_ref, ...), custom_call_target="tpu_custom_call" | custom-call | tf_op jit(solution)/shard_map/pair_backward/pallas_call | solution.py:183
  102.9 0.0 copy-start.1
  102.9 1.4 copy-done.1
  104.3 0.0 collective-permute-done.1
  104.3 0.4 collective-permute-start.4
  104.8 2.6 %collective-permute-start.3 = (f32[16,128]{1,0:T(8,128)S(1)}, f32[16,128]{1,0:T(8,128)S(1)}, u32[]{:S(2)}, u32[]{:S(2)}) collective-permute-start(f32[16,128]{1,0:T(8,128)S(1)} %add.25), channel_id=1, source_target_pairs={{0,8},{1,9},{2,10},{3,11},{4,12},{5,13},{6,14},{7,15},{8,0},{9,1},... | collective-permute-start | bytes 24584 | tf_op jit(solution)/shard_map/ppermute | solution.py:362
  107.3 1.9 collective-permute-start.2
  109.2 2.9 %pair_backward.3 = (bf16[16,128,256]{2,1,0:T(8,128)(2,1)S(1)}, bf16[16,2,128,256]{3,2,1,0:T(8,128)(2,1)S(1)}) custom-call(s32[16]{0:T(128)S(1)} %get-tuple-element.34.first_ref, s32[16]{0:T(128)S(1)} %get-tuple-element.51.slot_ref, bf16[8,3,128,256]{3,2,1,0:T(8,128)(2,1)S(1)} %bitcast.11, bf16[16,3,128,256]{3,2,1,0:T(8,128)(2,1)S(1)} %all-to-all-done.inc_ref, ...), custom_call_target="tpu_custom_call" | custom-call | tf_op jit(solution)/shard_map/pair_backward/pallas_call | solution.py:183
  112.2 0.0 copy-start.4
  112.2 1.0 copy-done.4
  113.1 0.0 collective-permute-done.4
  113.1 0.0 collective-permute-done.3
  113.1 0.0 collective-permute-done.2
  113.2 2.6 %second_terms.1 = bf16[16,400,256]{2,1,0:T(8,128)(2,1)} custom-call(s32[16]{0:T(128)S(1)} %get-tuple-element.51.slot_ref, s32[16]{0:T(128)S(1)} %not_convert_fusion.lead_ref, s32[16]{0:T(128)S(1)} %select_reduce_fusion.mate_ref, f32[16,128]{1,0:T(8,128)S(1)} %get-tuple-element.50.logits_ref, f32[16,128]{1,0:T(8,128)S(1)} %broadcast_in_dim.18.target_ref, ...), custom_call_target="tpu_custom_call" | custom-call | tf_op jit(solution)/shard_map/second_terms/pallas_call | solution.py:270
  115.8 4.5 %all-to-all-start.1 = ((bf16[16,400,256]{2,1,0:T(8,128)(2,1)}), bf16[16,400,256]{2,1,0:T(8,128)(2,1)}, u32[]{:S(2)}, u32[]{:S(2)}) async-start(bf16[16,400,256]{2,1,0:T(8,128)(2,1)} %second_terms.1), calls=%async_computation.1 | async-start | bytes 6553600 | tf_op jit(solution)/shard_map/all_to_all | solution.py:391
  120.3 0.1 select_n.24
  120.4 0.1 reduce_max.18.code_ref
  120.5 0.0 copy-start.2
  120.5 1.6 copy-done.2
  122.1 0.0 copy-start.5
  122.1 1.2 copy-done.5
  123.3 1.5 first_terms.1.own_ref
  124.8 0.6 slice_reduce_fusion
  125.4 71.9 %all-to-all-done.1.back_ref.tail_ref = bf16[16,400,256]{2,1,0:T(8,128)(2,1)} async-done(((bf16[16,400,256]{2,1,0:T(8,128)(2,1)}), bf16[16,400,256]{2,1,0:T(8,128)(2,1)}, u32[]{:S(2)}, u32[]{:S(2)}) %all-to-all-start.1) | async-done | bytes 3276832 | tf_op jit(solution)/shard_map/all_to_all | solution.py:391
  197.3 4.4 %finish_parts.1 = (bf16[8,3,128,256]{3,2,1,0:T(8,128)(2,1)}, f32[8,128]{1,0:T(8,128)S(1)}) custom-call(s32[16]{0:T(128)S(1)} %reduce_max.18.code_ref, f32[8,3,128,256]{3,2,1,0:T(8,128)S(1)} %first_terms.1.own_ref, bf16[16,400,256]{2,1,0:T(8,128)(2,1)} %all-to-all-done.1.back_ref.tail_ref, bf16[16,400,256]{2,1,0:T(8,128)(2,1)} %all-to-all-done.1.back_ref.tail_ref), custom_call_target="tpu_custom_call" | custom-call | tf_op jit(solution)/shard_map/finish_parts/pallas_call | solution.py:344
  201.7 0.5 slice.27
  (7 shorter events, 0.1 us)
Async XLA Ops:
  4.3 11.1 %copy-start.7 = (s32[256,3]{0,1:T(4,128)S(1)}, s32[256,3]{0,1:T(4,128)}, u32[]{:S(2)}) copy-start(s32[256,3]{0,1:T(4,128)} %param.6) | copy-start | bytes 9220
  4.3 11.2 %copy-start.8 = (s32[16]{0:T(128)S(1)}, s32[16]{0:T(128)}, u32[]{:S(2)}) copy-start(s32[16]{0:T(128)} %param.9) | copy-start | bytes 196
  4.3 86.1 %copy-start.3 = (bf16[2,128,256]{2,1,0:T(8,128)(2,1)S(1)}, bf16[2,128,256]{2,1,0:T(8,128)(2,1)}, u32[]{:S(2)}) copy-start(bf16[2,128,256]{2,1,0:T(8,128)(2,1)} %proj_ref.5) | copy-start | bytes 393220
  4.3 86.1 %copy-start.6 = (f32[2,256]{1,0:T(2,128)S(1)}, f32[2,256]{1,0:T(2,128)}, u32[]{:S(2)}) copy-start(f32[2,256]{1,0:T(2,128)} %readout_ref.1) | copy-start | bytes 6148
  4.3 86.0 %all-to-all-start = ((bf16[16,3,128,256]{3,2,1,0:T(8,128)(2,1)}), bf16[16,3,128,256]{3,2,1,0:T(8,128)(2,1)S(1)}, u32[]{:S(2)}, u32[]{:S(2)}) async-start(bf16[16,3,128,256]{3,2,1,0:T(8,128)(2,1)} %pick_rows.1), calls=%async_computation | async-start | bytes 6291456 | tf_op jit(solution)/shard_map/all_to_all | solution.py:391
  90.4 1.4 copy-start
  98.2 1.2 collective-permute-start
  99.4 4.9 %collective-permute-start.1 = (f32[16,128]{1,0:T(8,128)S(1)}, f32[16,128]{1,0:T(8,128)S(1)}, u32[]{:S(2)}, u32[]{:S(2)}) collective-permute-start(f32[16,128]{1,0:T(8,128)S(1)} %add.24), channel_id=1, source_target_pairs={{0,2},{1,3},{2,0},{3,1},{4,6},{5,7},{6,4},{7,5},{8,10},{9,11},{10,... | collective-permute-start | bytes 24584 | tf_op jit(solution)/shard_map/ppermute | solution.py:362
  102.9 1.4 copy-start.1
  104.3 8.8 %collective-permute-start.4 = (f32[16,128]{1,0:T(8,128)S(1)}, f32[16,128]{1,0:T(8,128)S(1)}, u32[]{:S(2)}, u32[]{:S(2)}) collective-permute-start(f32[16,128]{1,0:T(8,128)S(1)} %add.25), channel_id=1, source_target_pairs={{0,12},{1,13},{2,14},{3,15},{4,0},{5,1},{6,2},{7,3},{8,4},{9,5},{1... | collective-permute-start | bytes 24584 | tf_op jit(solution)/shard_map/ppermute | solution.py:362
  104.8 8.4 %collective-permute-start.3 = (f32[16,128]{1,0:T(8,128)S(1)}, f32[16,128]{1,0:T(8,128)S(1)}, u32[]{:S(2)}, u32[]{:S(2)}) collective-permute-start(f32[16,128]{1,0:T(8,128)S(1)} %add.25), channel_id=1, source_target_pairs={{0,8},{1,9},{2,10},{3,11},{4,12},{5,13},{6,14},{7,15},{8,0},{9,1},... | collective-permute-start | bytes 24584 | tf_op jit(solution)/shard_map/ppermute | solution.py:362
  107.3 5.8 %collective-permute-start.2 = (f32[16,128]{1,0:T(8,128)S(1)}, f32[16,128]{1,0:T(8,128)S(1)}, u32[]{:S(2)}, u32[]{:S(2)}) collective-permute-start(f32[16,128]{1,0:T(8,128)S(1)} %add.25), channel_id=1, source_target_pairs={{0,4},{1,5},{2,6},{3,7},{4,8},{5,9},{6,10},{7,11},{8,12},{9,13},{1... | collective-permute-start | bytes 24584 | tf_op jit(solution)/shard_map/ppermute | solution.py:362
  112.2 1.0 copy-start.4
  115.8 81.5 %all-to-all-start.1 = ((bf16[16,400,256]{2,1,0:T(8,128)(2,1)}), bf16[16,400,256]{2,1,0:T(8,128)(2,1)}, u32[]{:S(2)}, u32[]{:S(2)}) async-start(bf16[16,400,256]{2,1,0:T(8,128)(2,1)} %second_terms.1), calls=%async_computation.1 | async-start | bytes 6553600 | tf_op jit(solution)/shard_map/all_to_all | solution.py:391
  120.5 1.6 copy-start.2
  122.1 1.2 copy-start.5

commit v7 on v6

--- a/solution.py
+++ b/solution.py
@@ -131,7 +131,7 @@
     length = mol.shape[2]
     heads, _, width = proj.shape
     return pl.pallas_call(
-        functools.partial(forward_kernel, min(8, pairs)),
+        functools.partial(forward_kernel, min(16, pairs)),
         out_shape=(
             jax.ShapeDtypeStruct((pairs, 128), F32),
             jax.ShapeDtypeStruct((2, pairs, heads, length, length), F32),
@@ -210,8 +210,25 @@
     return rows.astype(BF16)
 
 
-def second_kernel(
-    slot_ref, lead_ref, mate_ref, logits_ref, target_ref, loss_ref, dq_ref, dkv_ref, out_ref, scale_ref, hold_ref, tail_ref, sems, tail_sems
+def scale_kernel(
+    first_ref,
+    slot_ref,
+    lead_ref,
+    mate_ref,
+    logits_ref,
+    target_ref,
+    loss_ref,
+    dq_ref,
+    dkv_ref,
+    own_dq_ref,
+    own_dkv_ref,
+    out_ref,
+    own_ref,
+    scale_ref,
+    hold_ref,
+    tail_ref,
+    sems,
+    tail_sems,
 ):
     pairs, length, _ = dq_ref.shape
     slots = out_ref.shape[0]
@@ -252,6 +269,16 @@
         return carry
 
     lax.fori_loop(0, pairs, step, 0)
+    own_ref[...] = jnp.zeros_like(own_ref)
+
+    def own_step(p, carry):
+        a = first_ref[p]
+        scale = scale_ref[pl.ds(p, 1), :]
+        for c in range(3):
+            own_ref[a, c] += scale * (own_dq_ref[p] if c == 0 else own_dkv_ref[p, c - 1]).astype(F32)
+        return carry
+
+    lax.fori_loop(0, pairs, own_step, 0)
 
     def land(p, carry):
         @pl.when(lead_ref[p] == 1)
@@ -265,13 +292,16 @@
         c.wait()
 
 
-def second_terms(slot, lead, mate, logits, target, loss, dq, dkv, slots):
-    pairs, length, width = dq.shape
+def scaled_terms(first, slot, lead, mate, logits, target, loss, second, own, slots, mols):
+    pairs, length, width = second[0].shape
     return pl.pallas_call(
-        second_kernel,
-        out_shape=jax.ShapeDtypeStruct((slots, 3 * length + LOSS_ROWS, width), BF16),
-        in_specs=[SMEM_SPEC] * 3 + [VMEM_SPEC] * 5,
-        out_specs=HBM_SPEC,
+        scale_kernel,
+        out_shape=(
+            jax.ShapeDtypeStruct((slots, 3 * length + LOSS_ROWS, width), BF16),
+            jax.ShapeDtypeStruct((mols, 3, length, width), F32),
+        ),
+        in_specs=[SMEM_SPEC] * 4 + [VMEM_SPEC] * 7,
+        out_specs=(HBM_SPEC, VMEM_SPEC),
         scratch_shapes=[
             pltpu.VMEM((pairs, width), F32),
             pltpu.VMEM((pairs, 3 * length, width), BF16),
@@ -280,82 +310,66 @@
             pltpu.SemaphoreType.DMA((slots,)),
         ],
         compiler_params=params(SECOND_BYTES),
-        name="second_terms",
-    )(slot, lead, mate, logits, target, loss, dq, dkv)
-
-
-def first_kernel(first_ref, logits_ref, target_ref, dq_ref, dkv_ref, own_ref, scale_ref):
-    pairs = dq_ref.shape[0]
-    scale_ref[...] = grad_scale(logits_ref[...], target_ref[...])
-    own_ref[...] = jnp.zeros_like(own_ref)
-
-    def step(p, carry):
-        a = first_ref[p]
-        scale = scale_ref[pl.ds(p, 1), :]
-        for c in range(3):
-            own_ref[a, c] += scale * (dq_ref[p] if c == 0 else dkv_ref[p, c - 1]).astype(F32)
-        return carry
-
-    lax.fori_loop(0, pairs, step, 0)
-
-
-def first_terms(first, logits, target, dq, dkv, mols):
-    pairs, length, width = dq.shape
-    return pl.pallas_call(
-        first_kernel,
-        out_shape=jax.ShapeDtypeStruct((mols, 3, length, width), F32),
-        in_specs=[SMEM_SPEC] + [VMEM_SPEC] * 4,
-        out_specs=VMEM_SPEC,
-        scratch_shapes=[pltpu.VMEM((pairs, width), F32)],
-        compiler_params=params(),
-        name="first_terms",
-    )(first, logits, target, dq, dkv)
-
-
-def finish_kernel(code_ref, own_ref, back_ref, tail_ref, out_ref, loss_ref, sum_ref):
+        name="scaled_terms",
+    )(first, slot, lead, mate, logits, target, loss, *second, *own)
+
+
+def finish_kernel(scale, code_ref, own_ref, back_ref, out_ref, loss_ref, held_ref, tail_ref, sum_ref, done_ref, sems, tail_sem, out_sems):
     slots = back_ref.shape[0]
-    c = pl.program_id(0)
-    sum_ref[...] = own_ref[:, c]
-
-    @pl.when(c == 0)
-    def loss():
-        total = tail_ref[0].astype(F32)
-        for s in range(1, slots):
-            total = total + tail_ref[s].astype(F32)
-        loss_ref[...] = jnp.broadcast_to(jnp.sum(total, axis=0, keepdims=True)[:, :128], loss_ref.shape)
-
-    def step(s, carry):
-        m = code_ref[s]
-
-        @pl.when(m >= 0)
-        def add():
-            sum_ref[jnp.maximum(m, 0)] += back_ref[s].astype(F32)
-
-        return carry
-
-    lax.fori_loop(0, slots, step, 0, unroll=True)
-    out_ref[:, 0] = sum_ref[...].astype(BF16)
-
-
-def finish(code, own, back):
+    mols, parts, length, _ = own_ref.shape
+    codes = [code_ref[s] for s in range(slots)]
+
+    def load(c, s):
+        rows = pl.ds(c * length, length)
+        return pltpu.make_async_copy(back_ref.at[s, rows], held_ref.at[s, rows], sems.at[c, s])
+
+    for c in range(parts):
+        for s in range(slots):
+            pl.when(codes[s] >= 0)(load(c, s).start)
+    tail = pltpu.make_async_copy(back_ref.at[:, pl.ds(parts * length, LOSS_ROWS)], tail_ref, tail_sem)
+    tail.start()
+
+    for c in range(parts):
+        sum_ref[...] = own_ref[:, c]
+        for s in range(slots):
+
+            @pl.when(codes[s] >= 0)
+            def add():
+                load(c, s).wait()
+                sum_ref[jnp.maximum(codes[s], 0)] += held_ref[s, c * length : (c + 1) * length].astype(F32)
+
+        done_ref[c] = sum_ref[...].astype(BF16)
+        pltpu.make_async_copy(done_ref.at[c], out_ref.at[:, c], out_sems.at[c]).start()
+
+    tail.wait()
+    total = tail_ref[0].astype(F32)
+    for s in range(1, slots):
+        total = total + tail_ref[s].astype(F32)
+    loss_ref[0, 0] = jnp.sum(total[:, :1]) * scale
+    for c in range(parts):
+        pltpu.make_async_copy(done_ref.at[c], out_ref.at[:, c], out_sems.at[c]).wait()
+
+
+def finish(code, own, back, scale):
     mols, parts, length, width = own.shape
     slots = back.shape[0]
-    part = lambda i: (0, i, 0, 0)
     return pl.pallas_call(
-        finish_kernel,
-        grid=(parts,),
-        out_shape=(jax.ShapeDtypeStruct(own.shape, BF16), jax.ShapeDtypeStruct((8, 128), F32)),
-        in_specs=[
-            SMEM_SPEC,
-            VMEM_SPEC,
-            pl.BlockSpec((slots, length, width), lambda i: (0, i, 0)),
-            pl.BlockSpec((slots, LOSS_ROWS, width), lambda i: (0, parts * length // LOSS_ROWS, 0)),
+        functools.partial(finish_kernel, scale),
+        out_shape=(jax.ShapeDtypeStruct(own.shape, BF16), jax.ShapeDtypeStruct((1, 1), F32)),
+        in_specs=[SMEM_SPEC, VMEM_SPEC, HBM_SPEC],
+        out_specs=(HBM_SPEC, SMEM_SPEC),
+        scratch_shapes=[
+            pltpu.VMEM((slots, parts * length, width), BF16),
+            pltpu.VMEM((slots, LOSS_ROWS, width), BF16),
+            pltpu.VMEM((mols, length, width), F32),
+            pltpu.VMEM((parts, mols, length, width), BF16),
+            pltpu.SemaphoreType.DMA((parts, slots)),
+            pltpu.SemaphoreType.DMA,
+            pltpu.SemaphoreType.DMA((parts,)),
         ],
-        out_specs=(pl.BlockSpec((mols, 1, length, width), part), pl.BlockSpec((8, 128), lambda i: (0, 0))),
-        scratch_shapes=[pltpu.VMEM((mols, length, width), F32)],
         compiler_params=params(FINISH_BYTES),
         name="finish_parts",
-    )(code, own, back, back)
+    )(code, own, back)
 
 
 def hop(value, axis, size, change):
@@ -425,12 +439,13 @@
     logits_wide, (dq_b, dkv_a), (dq_a, dkv_b) = sum_shards_beside(part, shards, grads(1), grads(0))
 
     loss_wide = jax.nn.softplus(logits_wide) - target_wide * logits_wide
-    out = second_terms(slot, lead, mate, logits_wide, target_wide, loss_wide, dq_b, dkv_b, groups)
+    out, own = scaled_terms(
+        first, slot, lead, mate, logits_wide, target_wide, loss_wide, (dq_b, dkv_b), (dq_a, dkv_a), groups, mols
+    )
     back = exchange(out)
-    own = first_terms(first, logits_wide, target_wide, dq_a, dkv_a, mols)
     logits = logits_wide[:, 0]
-    grads, loss_sum = finish(code, own, back)
-    mean_loss = loss_sum[0, 0] / total_pairs
+    grads, mean_loss = finish(code, own, back, 1.0 / total_pairs)
+    mean_loss = mean_loss.reshape(())
     mol_grad = jnp.transpose(grads, (0, 2, 1, 3))
     return (mol_grad, logits, mean_loss)
 

time: 204 us -> 200 us (0.980)
  local copies, waits for them, and re-layouts: 7.97 us -> 2.31 us
  waiting for transfers between devices: 147 us -> 152 us
    unnamed x18 -> x10, local copies, waits for them, and re-layouts: 6.59 us -> 1.44 us
    all_to_all x2, waiting for transfers between devices: 146 us -> 150 us  [exchange(): lax.all_to_all(value, 'group', split_axis=0, concat_axis=0, tiled=True)]
    pallas_call x4 -> x3, Pallas kernels: 14.9 us -> 13.4 us  [the longest x1 6.1 us: forward(): pl.pallas_call(functools.partial(forward_kernel, min(16, pairs)), out_sha...]
  transfers between devices with their start and end apart: 7 -> 7, of which waited for: 3 -> 4; matrix products, arithmetic and copies ran while one was open for 1% -> 1% of each run, Pallas kernels for 4% -> 3%
where the time goes in v7:
time: 200 us; the launch traced here: 199 us
  waiting for transfers between devices  152 us (76%)
  Pallas kernels  22.6 us (11%)
  starting transfers between devices  21.3 us (11%)
  local copies, waits for them, and re-layouts  2.31 us (1%)
    all_to_all x2, waiting for transfers between devices, exchange(): lax.all_to_all(value, 'group', split_axis=0, concat_axis=0, tiled=True)  150 us
    all_to_all x2, starting transfers between devices, exchange(): lax.all_to_all(value, 'group', split_axis=0, concat_axis=0, tiled=True)  15.8 us
    pallas_call x1, Pallas kernels, forward(): pl.pallas_call(functools.partial(forward_kernel, min(16, pairs)), out_sha...  6.1 us
    pallas_call x2, Pallas kernels, backward(): pl.pallas_call(functools.partial(backward_kernel, direction, min(16, pair...  5.69 us
    ppermute x5, starting transfers between devices, hop(): return lax.ppermute(value, axis, [(i, change(i)) for i in range(size)])  5.56 us
    pallas_call x1, Pallas kernels, finish(): pl.pallas_call(functools.partial(finish_kernel, scale), out_shape=(jax.Sh...  4.35 us
  transfers between devices with their start and end apart: 7, of which 4 were waited for; matrix products, arithmetic and copies ran while one was open for 1% of the time, Pallas kernels for 3%

profile of v7, /device:TPU:8, one launch (start us, length us, event | category | flops | bytes accessed | tf_op | source)
XLA Modules:
  0.0 199.5 jit_solution(12460268329073240919)
XLA Ops:
  0.6 3.5 %pick_rows.1 = bf16[16,3,128,256]{3,2,1,0:T(8,128)(2,1)} custom-call(s32[3,256]{1,0:T(4,128)} %bitcast.12, bf16[8,3,128,256]{3,2,1,0:T(8,128)(2,1)} %bitcast.8), custom_call_target="tpu_custom_call" | custom-call | tf_op jit(solution)/shard_map/pick_rows/pallas_call | solution.py:60
  4.1 0.0 copy-start.3
  4.1 0.0 copy-start.4
  4.1 0.0 copy-start.1
  4.2 0.0 copy-start.2
  4.2 11.3 %all-to-all-start = ((bf16[16,3,128,256]{3,2,1,0:T(8,128)(2,1)}), bf16[16,3,128,256]{3,2,1,0:T(8,128)(2,1)S(1)}, u32[]{:S(2)}, u32[]{:S(2)}) async-start(bf16[16,3,128,256]{3,2,1,0:T(8,128)(2,1)} %pick_rows.1), calls=%async_computation | async-start | bytes 6291456 | tf_op jit(solution)/shard_map/all_to_all | solution.py:405
  15.5 0.0 copy-done.3
  15.5 0.1 reshape.28
  15.5 0.0 copy-done.4
  15.6 0.2 fusion.1
  15.8 0.2 select_reduce_fusion.mate_ref
  16.0 74.4 %all-to-all-done.inc_ref = bf16[16,3,128,256]{3,2,1,0:T(8,128)(2,1)S(1)} async-done(((bf16[16,3,128,256]{3,2,1,0:T(8,128)(2,1)}), bf16[16,3,128,256]{3,2,1,0:T(8,128)(2,1)S(1)}, u32[]{:S(2)}, u32[]{:S(2)}) %all-to-all-start) | async-done | bytes 3145760 | tf_op jit(solution)/shard_map/all_to_all | solution.py:405
  90.4 0.1 broadcast_in_dim.18.target_ref
  90.4 0.0 copy-done.1
  90.4 0.0 copy-done.2
  90.4 0.0 copy-start
  90.4 1.4 copy-done
  91.8 6.1 %pair_forward.1 = (f32[16,128]{1,0:T(8,128)S(1)}, f32[2,16,2,128,128]{4,3,2,1,0:T(8,128)S(1)}, bf16[2,16,2,128,256]{4,3,2,1,0:T(8,128)(2,1)S(1)}) custom-call(s32[16]{0:T(128)S(1)} %get-tuple-element.38.first_ref, s32[16]{0:T(128)S(1)} %get-tuple-element.55.slot_ref, bf16[8,3,128,256]{3,2,1,0:T(8,128)(2,1)S(1)} %bitcast.9, ...), custom_call_target="tpu_custom_call" | custom-call | tf_op jit(solution)/shard_map/pair_forward/pallas_call | solution.py:133
  97.9 0.0 collective-permute-start
  98.0 1.2 collective-permute-done
  99.1 0.6 collective-permute-start.1
  99.8 2.8 %pair_backward.2 = (bf16[16,128,256]{2,1,0:T(8,128)(2,1)S(1)}, bf16[16,2,128,256]{3,2,1,0:T(8,128)(2,1)S(1)}) custom-call(s32[16]{0:T(128)S(1)} %get-tuple-element.38.first_ref, s32[16]{0:T(128)S(1)} %get-tuple-element.55.slot_ref, bf16[8,3,128,256]{3,2,1,0:T(8,128)(2,1)S(1)} %bitcast.10, bf16[16,3,128,256]{3,2,1,0:T(8,128)(2,1)S(1)} %all-to-all-done.inc_ref, ...), custom_call_target="tpu_custom_call" | custom-call | tf_op jit(solution)/shard_map/pair_backward/pallas_call | solution.py:183
  102.6 0.2 collective-permute-done.1
  102.8 0.5 collective-permute-start.4
  103.3 2.6 %collective-permute-start.3 = (f32[16,128]{1,0:T(8,128)S(1)}, f32[16,128]{1,0:T(8,128)S(1)}, u32[]{:S(2)}, u32[]{:S(2)}) collective-permute-start(f32[16,128]{1,0:T(8,128)S(1)} %add.25), channel_id=1, source_target_pairs={{0,8},{1,9},{2,10},{3,11},{4,12},{5,13},{6,14},{7,15},{8,0},{9,1},... | collective-permute-start | bytes 24584 | tf_op jit(solution)/shard_map/ppermute | solution.py:376
  105.8 1.9 collective-permute-start.2
  107.7 2.8 %pair_backward.3 = (bf16[16,128,256]{2,1,0:T(8,128)(2,1)S(1)}, bf16[16,2,128,256]{3,2,1,0:T(8,128)(2,1)S(1)}) custom-call(s32[16]{0:T(128)S(1)} %get-tuple-element.38.first_ref, s32[16]{0:T(128)S(1)} %get-tuple-element.55.slot_ref, bf16[8,3,128,256]{3,2,1,0:T(8,128)(2,1)S(1)} %bitcast.11, bf16[16,3,128,256]{3,2,1,0:T(8,128)(2,1)S(1)} %all-to-all-done.inc_ref, ...), custom_call_target="tpu_custom_call" | custom-call | tf_op jit(solution)/shard_map/pair_backward/pallas_call | solution.py:183
  110.6 0.0 collective-permute-done.4
  110.6 0.0 collective-permute-done.3
  110.6 0.0 collective-permute-done.2
  110.6 3.0 %scaled_terms.1 = (bf16[16,400,256]{2,1,0:T(8,128)(2,1)}, f32[8,3,128,256]{3,2,1,0:T(8,128)S(1)}) custom-call(s32[16]{0:T(128)S(1)} %get-tuple-element.38.first_ref, s32[16]{0:T(128)S(1)} %get-tuple-element.55.slot_ref, s32[16]{0:T(128)S(1)} %not_convert_fusion.lead_ref, s32[16]{0:T(128)S(1)} %select_reduce_fusion.mate_ref, ...), custom_call_target="tpu_custom_call" | custom-call | tf_op jit(solution)/shard_map/scaled_terms/pallas_call | solution.py:297
  113.6 4.5 %all-to-all-start.1 = ((bf16[16,400,256]{2,1,0:T(8,128)(2,1)}), bf16[16,400,256]{2,1,0:T(8,128)(2,1)}, u32[]{:S(2)}, u32[]{:S(2)}) async-start(bf16[16,400,256]{2,1,0:T(8,128)(2,1)} %get-tuple-element.50), calls=%async_computation.1 | async-start | bytes 6553600 | tf_op jit(solution)/shard_map/all_to_all | solution.py:405
  118.1 0.1 select_n.24
  118.2 0.1 reduce_max.18.code_ref
  118.3 0.6 slice_reduce_fusion
  119.0 76.0 %all-to-all-done.1.back_ref = bf16[16,400,256]{2,1,0:T(8,128)(2,1)} async-done(((bf16[16,400,256]{2,1,0:T(8,128)(2,1)}), bf16[16,400,256]{2,1,0:T(8,128)(2,1)}, u32[]{:S(2)}, u32[]{:S(2)}) %all-to-all-start.1) | async-done | bytes 3276832 | tf_op jit(solution)/shard_map/all_to_all | solution.py:405
  195.0 4.4 %finish_parts.1 = (bf16[8,3,128,256]{3,2,1,0:T(8,128)(2,1)}, f32[1,1]{1,0:T(1,128)}) custom-call(s32[16]{0:T(128)S(1)} %reduce_max.18.code_ref, f32[8,3,128,256]{3,2,1,0:T(8,128)S(1)} %get-tuple-element.49.own_ref, bf16[16,400,256]{2,1,0:T(8,128)(2,1)} %all-to-all-done.1.back_ref), custom_call_target="tpu_custom_call" | custom-call | tf_op jit(solution)/shard_map/finish_parts/pallas_call | solution.py:356
  (7 shorter events, 0.1 us)
Async XLA Ops:
  4.1 11.3 %copy-start.3 = (s32[256,3]{0,1:T(4,128)S(1)}, s32[256,3]{0,1:T(4,128)}, u32[]{:S(2)}) copy-start(s32[256,3]{0,1:T(4,128)} %param.6) | copy-start | bytes 9220
  4.1 11.4 %copy-start.4 = (s32[16]{0:T(128)S(1)}, s32[16]{0:T(128)}, u32[]{:S(2)}) copy-start(s32[16]{0:T(128)} %param.9) | copy-start | bytes 196
  4.1 86.3 %copy-start.1 = (bf16[2,128,256]{2,1,0:T(8,128)(2,1)S(1)}, bf16[2,128,256]{2,1,0:T(8,128)(2,1)}, u32[]{:S(2)}) copy-start(bf16[2,128,256]{2,1,0:T(8,128)(2,1)} %proj_ref.5) | copy-start | bytes 393220
  4.2 86.3 %copy-start.2 = (f32[2,256]{1,0:T(2,128)S(1)}, f32[2,256]{1,0:T(2,128)}, u32[]{:S(2)}) copy-start(f32[2,256]{1,0:T(2,128)} %readout_ref.1) | copy-start | bytes 6148
  4.2 86.2 %all-to-all-start = ((bf16[16,3,128,256]{3,2,1,0:T(8,128)(2,1)}), bf16[16,3,128,256]{3,2,1,0:T(8,128)(2,1)S(1)}, u32[]{:S(2)}, u32[]{:S(2)}) async-start(bf16[16,3,128,256]{3,2,1,0:T(8,128)(2,1)} %pick_rows.1), calls=%async_computation | async-start | bytes 6291456 | tf_op jit(solution)/shard_map/all_to_all | solution.py:405
  90.4 1.4 copy-start
  97.9 1.2 collective-permute-start
  99.1 3.7 %collective-permute-start.1 = (f32[16,128]{1,0:T(8,128)S(1)}, f32[16,128]{1,0:T(8,128)S(1)}, u32[]{:S(2)}, u32[]{:S(2)}) collective-permute-start(f32[16,128]{1,0:T(8,128)S(1)} %add.24), channel_id=1, source_target_pairs={{0,2},{1,3},{2,0},{3,1},{4,6},{5,7},{6,4},{7,5},{8,10},{9,11},{10,... | collective-permute-start | bytes 24584 | tf_op jit(solution)/shard_map/ppermute | solution.py:376
  102.8 7.8 %collective-permute-start.4 = (f32[16,128]{1,0:T(8,128)S(1)}, f32[16,128]{1,0:T(8,128)S(1)}, u32[]{:S(2)}, u32[]{:S(2)}) collective-permute-start(f32[16,128]{1,0:T(8,128)S(1)} %add.25), channel_id=1, source_target_pairs={{0,12},{1,13},{2,14},{3,15},{4,0},{5,1},{6,2},{7,3},{8,4},{9,5},{1... | collective-permute-start | bytes 24584 | tf_op jit(solution)/shard_map/ppermute | solution.py:376
  103.3 7.3 %collective-permute-start.3 = (f32[16,128]{1,0:T(8,128)S(1)}, f32[16,128]{1,0:T(8,128)S(1)}, u32[]{:S(2)}, u32[]{:S(2)}) collective-permute-start(f32[16,128]{1,0:T(8,128)S(1)} %add.25), channel_id=1, source_target_pairs={{0,8},{1,9},{2,10},{3,11},{4,12},{5,13},{6,14},{7,15},{8,0},{9,1},... | collective-permute-start | bytes 24584 | tf_op jit(solution)/shard_map/ppermute | solution.py:376
  105.8 4.8 %collective-permute-start.2 = (f32[16,128]{1,0:T(8,128)S(1)}, f32[16,128]{1,0:T(8,128)S(1)}, u32[]{:S(2)}, u32[]{:S(2)}) collective-permute-start(f32[16,128]{1,0:T(8,128)S(1)} %add.25), channel_id=1, source_target_pairs={{0,4},{1,5},{2,6},{3,7},{4,8},{5,9},{6,10},{7,11},{8,12},{9,13},{1... | collective-permute-start | bytes 24584 | tf_op jit(solution)/shard_map/ppermute | solution.py:376
  113.6 81.4 %all-to-all-start.1 = ((bf16[16,400,256]{2,1,0:T(8,128)(2,1)}), bf16[16,400,256]{2,1,0:T(8,128)(2,1)}, u32[]{:S(2)}, u32[]{:S(2)}) async-start(bf16[16,400,256]{2,1,0:T(8,128)(2,1)} %get-tuple-element.50), calls=%async_computation.1 | async-start | bytes 6553600 | tf_op jit(solution)/shard_map/all_to_all | solution.py:405

commit v8 on v7

--- a/solution.py
+++ b/solution.py
@@ -230,11 +230,11 @@
     sems,
     tail_sems,
 ):
-    pairs, length, _ = dq_ref.shape
-    slots = out_ref.shape[0]
-    rows = 3 * length
-    loss = jnp.sum(loss_ref[...], axis=0, keepdims=True)
-    tail_ref[...] = three_parts(jnp.concatenate([loss, loss], axis=1))
+    pairs, length, width = dq_ref.shape
+    slots, _, hd = out_ref.shape
+    heads = width // hd
+    rows = 3 * heads * length
+    tail_ref[...] = three_parts(jnp.sum(loss_ref[...], axis=0, keepdims=True))
     tails = [
         pltpu.make_async_copy(tail_ref, out_ref.at[s, pl.ds(rows, LOSS_ROWS)], tail_sems.at[s]) for s in range(slots)
     ]
@@ -248,6 +248,12 @@
     def part(p, c):
         return (dq_ref[p] if c == 0 else dkv_ref[p, c - 1]).astype(F32)
 
+    def hold(p, c, value):
+        value = value.astype(BF16)
+        for h in range(heads):
+            at = (c * heads + h) * length
+            hold_ref[p, at : at + length] = value[:, h * hd : (h + 1) * hd]
+
     def step(p, carry):
         mate = mate_ref[p]
         own = scale_ref[pl.ds(p, 1), :]
@@ -255,7 +261,7 @@
         @pl.when((lead_ref[p] == 1) & (mate < 0))
         def single():
             for c in range(3):
-                hold_ref[p, c * length : (c + 1) * length] = (own * part(p, c)).astype(BF16)
+                hold(p, c, own * part(p, c))
             send(p).start()
 
         @pl.when((lead_ref[p] == 1) & (mate >= 0))
@@ -263,7 +269,7 @@
             at = jnp.maximum(mate, 0)
             other = scale_ref[pl.ds(at, 1), :]
             for c in range(3):
-                hold_ref[p, c * length : (c + 1) * length] = (own * part(p, c) + other * part(at, c)).astype(BF16)
+                hold(p, c, own * part(p, c) + other * part(at, c))
             send(p).start()
 
         return carry
@@ -294,18 +300,20 @@
 
 def scaled_terms(first, slot, lead, mate, logits, target, loss, second, own, slots, mols):
     pairs, length, width = second[0].shape
+    hd = logits.shape[1]
+    rows = 3 * length * (width // hd)
     return pl.pallas_call(
         scale_kernel,
         out_shape=(
-            jax.ShapeDtypeStruct((slots, 3 * length + LOSS_ROWS, width), BF16),
+            jax.ShapeDtypeStruct((slots, rows + LOSS_ROWS, hd), BF16),
             jax.ShapeDtypeStruct((mols, 3, length, width), F32),
         ),
         in_specs=[SMEM_SPEC] * 4 + [VMEM_SPEC] * 7,
         out_specs=(HBM_SPEC, VMEM_SPEC),
         scratch_shapes=[
             pltpu.VMEM((pairs, width), F32),
-            pltpu.VMEM((pairs, 3 * length, width), BF16),
-            pltpu.VMEM((LOSS_ROWS, width), BF16),
+            pltpu.VMEM((pairs, rows, hd), BF16),
+            pltpu.VMEM((LOSS_ROWS, hd), BF16),
             pltpu.SemaphoreType.DMA((pairs,)),
             pltpu.SemaphoreType.DMA((slots,)),
         ],
@@ -315,18 +323,20 @@
 
 
 def finish_kernel(scale, code_ref, own_ref, back_ref, out_ref, loss_ref, held_ref, tail_ref, sum_ref, done_ref, sems, tail_sem, out_sems):
-    slots = back_ref.shape[0]
-    mols, parts, length, _ = own_ref.shape
+    slots, _, hd = back_ref.shape
+    mols, parts, length, width = own_ref.shape
+    heads = width // hd
+    block = heads * length
     codes = [code_ref[s] for s in range(slots)]
 
     def load(c, s):
-        rows = pl.ds(c * length, length)
+        rows = pl.ds(c * block, block)
         return pltpu.make_async_copy(back_ref.at[s, rows], held_ref.at[s, rows], sems.at[c, s])
 
     for c in range(parts):
         for s in range(slots):
             pl.when(codes[s] >= 0)(load(c, s).start)
-    tail = pltpu.make_async_copy(back_ref.at[:, pl.ds(parts * length, LOSS_ROWS)], tail_ref, tail_sem)
+    tail = pltpu.make_async_copy(back_ref.at[:, pl.ds(parts * block, LOSS_ROWS)], tail_ref, tail_sem)
     tail.start()
 
     for c in range(parts):
@@ -336,7 +346,10 @@
             @pl.when(codes[s] >= 0)
             def add():
                 load(c, s).wait()
-                sum_ref[jnp.maximum(codes[s], 0)] += held_ref[s, c * length : (c + 1) * length].astype(F32)
+                for h in range(heads):
+                    at = c * block + h * length
+                    cols = slice(h * hd, (h + 1) * hd)
+                    sum_ref[jnp.maximum(codes[s], 0), :, cols] += held_ref[s, at : at + length].astype(F32)
 
         done_ref[c] = sum_ref[...].astype(BF16)
         pltpu.make_async_copy(done_ref.at[c], out_ref.at[:, c], out_sems.at[c]).start()
@@ -352,15 +365,15 @@
 
 def finish(code, own, back, scale):
     mols, parts, length, width = own.shape
-    slots = back.shape[0]
+    slots, rows, hd = back.shape
     return pl.pallas_call(
         functools.partial(finish_kernel, scale),
         out_shape=(jax.ShapeDtypeStruct(own.shape, BF16), jax.ShapeDtypeStruct((1, 1), F32)),
         in_specs=[SMEM_SPEC, VMEM_SPEC, HBM_SPEC],
         out_specs=(HBM_SPEC, SMEM_SPEC),
         scratch_shapes=[
-            pltpu.VMEM((slots, parts * length, width), BF16),
-            pltpu.VMEM((slots, LOSS_ROWS, width), BF16),
+            pltpu.VMEM((slots, rows - LOSS_ROWS, hd), BF16),
+            pltpu.VMEM((slots, LOSS_ROWS, hd), BF16),
             pltpu.VMEM((mols, length, width), F32),
             pltpu.VMEM((parts, mols, length, width), BF16),
             pltpu.SemaphoreType.DMA((parts, slots)),

time: 200 us -> 198 us (0.990)
  waiting for transfers between devices: 152 us -> 150 us
where the time goes in v8:
time: 198 us
  waiting for transfers between devices  150 us (76%)
  Pallas kernels  22.6 us (11%)
  starting transfers between devices  21.2 us (11%)
  local copies, waits for them, and re-layouts  2.31 us (1%)
    all_to_all x2, waiting for transfers between devices, exchange(): lax.all_to_all(value, 'group', split_axis=0, concat_axis=0, tiled=True)  149 us
    all_to_all x2, starting transfers between devices, exchange(): lax.all_to_all(value, 'group', split_axis=0, concat_axis=0, tiled=True)  15.6 us
    pallas_call x1, Pallas kernels, forward(): pl.pallas_call(functools.partial(forward_kernel, min(16, pairs)), out_sha...  6.11 us
    pallas_call x2, Pallas kernels, backward(): pl.pallas_call(functools.partial(backward_kernel, direction, min(16, pair...  5.7 us
    ppermute x5, starting transfers between devices, hop(): return lax.ppermute(value, axis, [(i, change(i)) for i in range(size)])  5.54 us
    pallas_call x1, Pallas kernels, finish(): pl.pallas_call(functools.partial(finish_kernel, scale), out_shape=(jax.Sh...  4.35 us
  transfers between devices with their start and end apart: 7, of which 4 were waited for; matrix products, arithmetic and copies ran while one was open for 1% of the time, Pallas kernels for 3%

profile of v8, /device:TPU:8, one launch (start us, length us, event | category | flops | bytes accessed | tf_op | source)
XLA Modules:
  0.0 197.9 jit_solution(10709832191565025947)
XLA Ops:
  0.6 3.5 %pick_rows.1 = bf16[16,3,128,256]{3,2,1,0:T(8,128)(2,1)} custom-call(s32[3,256]{1,0:T(4,128)} %bitcast.12, bf16[8,3,128,256]{3,2,1,0:T(8,128)(2,1)} %bitcast.8), custom_call_target="tpu_custom_call" | custom-call | tf_op jit(solution)/shard_map/pick_rows/pallas_call | solution.py:60
  4.2 0.0 copy-start.3
  4.2 0.0 copy-start.4
  4.2 0.0 copy-start.1
  4.2 0.0 copy-start.2
  4.2 11.1 %all-to-all-start = ((bf16[16,3,128,256]{3,2,1,0:T(8,128)(2,1)}), bf16[16,3,128,256]{3,2,1,0:T(8,128)(2,1)S(1)}, u32[]{:S(2)}, u32[]{:S(2)}) async-start(bf16[16,3,128,256]{3,2,1,0:T(8,128)(2,1)} %pick_rows.1), calls=%async_computation | async-start | bytes 6291456 | tf_op jit(solution)/shard_map/all_to_all | solution.py:418
  15.3 0.0 copy-done.3
  15.4 0.1 reshape.28
  15.4 0.0 copy-done.4
  15.5 0.2 fusion.1
  15.6 0.2 select_reduce_fusion.mate_ref
  15.8 74.4 %all-to-all-done.inc_ref = bf16[16,3,128,256]{3,2,1,0:T(8,128)(2,1)S(1)} async-done(((bf16[16,3,128,256]{3,2,1,0:T(8,128)(2,1)}), bf16[16,3,128,256]{3,2,1,0:T(8,128)(2,1)S(1)}, u32[]{:S(2)}, u32[]{:S(2)}) %all-to-all-start) | async-done | bytes 3145760 | tf_op jit(solution)/shard_map/all_to_all | solution.py:418
  90.2 0.1 broadcast_in_dim.18.target_ref
  90.3 0.0 copy-done.1
  90.3 0.0 copy-done.2
  90.3 0.0 copy-start
  90.3 1.4 copy-done
  91.7 6.1 %pair_forward.1 = (f32[16,128]{1,0:T(8,128)S(1)}, f32[2,16,2,128,128]{4,3,2,1,0:T(8,128)S(1)}, bf16[2,16,2,128,256]{4,3,2,1,0:T(8,128)(2,1)S(1)}) custom-call(s32[16]{0:T(128)S(1)} %get-tuple-element.38.first_ref, s32[16]{0:T(128)S(1)} %get-tuple-element.55.slot_ref, bf16[8,3,128,256]{3,2,1,0:T(8,128)(2,1)S(1)} %bitcast.9, ...), custom_call_target="tpu_custom_call" | custom-call | tf_op jit(solution)/shard_map/pair_forward/pallas_call | solution.py:133
  97.8 0.0 collective-permute-start
  97.9 1.2 collective-permute-done
  99.0 0.6 collective-permute-start.1
  99.6 2.9 %pair_backward.2 = (bf16[16,128,256]{2,1,0:T(8,128)(2,1)S(1)}, bf16[16,2,128,256]{3,2,1,0:T(8,128)(2,1)S(1)}) custom-call(s32[16]{0:T(128)S(1)} %get-tuple-element.38.first_ref, s32[16]{0:T(128)S(1)} %get-tuple-element.55.slot_ref, bf16[8,3,128,256]{3,2,1,0:T(8,128)(2,1)S(1)} %bitcast.10, bf16[16,3,128,256]{3,2,1,0:T(8,128)(2,1)S(1)} %all-to-all-done.inc_ref, ...), custom_call_target="tpu_custom_call" | custom-call | tf_op jit(solution)/shard_map/pair_backward/pallas_call | solution.py:183
  102.5 0.2 collective-permute-done.1
  102.7 0.4 collective-permute-start.4
  103.1 2.6 %collective-permute-start.3 = (f32[16,128]{1,0:T(8,128)S(1)}, f32[16,128]{1,0:T(8,128)S(1)}, u32[]{:S(2)}, u32[]{:S(2)}) collective-permute-start(f32[16,128]{1,0:T(8,128)S(1)} %add.25), channel_id=1, source_target_pairs={{0,8},{1,9},{2,10},{3,11},{4,12},{5,13},{6,14},{7,15},{8,0},{9,1},... | collective-permute-start | bytes 24584 | tf_op jit(solution)/shard_map/ppermute | solution.py:389
  105.7 1.9 collective-permute-start.2
  107.6 2.8 %pair_backward.3 = (bf16[16,128,256]{2,1,0:T(8,128)(2,1)S(1)}, bf16[16,2,128,256]{3,2,1,0:T(8,128)(2,1)S(1)}) custom-call(s32[16]{0:T(128)S(1)} %get-tuple-element.38.first_ref, s32[16]{0:T(128)S(1)} %get-tuple-element.55.slot_ref, bf16[8,3,128,256]{3,2,1,0:T(8,128)(2,1)S(1)} %bitcast.11, bf16[16,3,128,256]{3,2,1,0:T(8,128)(2,1)S(1)} %all-to-all-done.inc_ref, ...), custom_call_target="tpu_custom_call" | custom-call | tf_op jit(solution)/shard_map/pair_backward/pallas_call | solution.py:183
  110.5 0.0 collective-permute-done.4
  110.5 0.0 collective-permute-done.3
  110.5 0.0 collective-permute-done.2
  110.5 3.0 %scaled_terms.1 = (bf16[16,784,128]{2,1,0:T(8,128)(2,1)}, f32[8,3,128,256]{3,2,1,0:T(8,128)S(1)}) custom-call(s32[16]{0:T(128)S(1)} %get-tuple-element.38.first_ref, s32[16]{0:T(128)S(1)} %get-tuple-element.55.slot_ref, s32[16]{0:T(128)S(1)} %not_convert_fusion.lead_ref, s32[16]{0:T(128)S(1)} %select_reduce_fusion.mate_ref, ...), custom_call_target="tpu_custom_call" | custom-call | tf_op jit(solution)/shard_map/scaled_terms/pallas_call | solution.py:305
  113.5 4.5 %all-to-all-start.1 = ((bf16[16,784,128]{2,1,0:T(8,128)(2,1)}), bf16[16,784,128]{2,1,0:T(8,128)(2,1)}, u32[]{:S(2)}, u32[]{:S(2)}) async-start(bf16[16,784,128]{2,1,0:T(8,128)(2,1)} %get-tuple-element.50), calls=%async_computation.1 | async-start | bytes 6422528 | tf_op jit(solution)/shard_map/all_to_all | solution.py:418
  118.0 0.1 select_n.24
  118.1 0.1 reduce_max.18.code_ref
  118.2 0.6 slice_reduce_fusion
  118.9 74.5 %all-to-all-done.1.back_ref = bf16[16,784,128]{2,1,0:T(8,128)(2,1)} async-done(((bf16[16,784,128]{2,1,0:T(8,128)(2,1)}), bf16[16,784,128]{2,1,0:T(8,128)(2,1)}, u32[]{:S(2)}, u32[]{:S(2)}) %all-to-all-start.1) | async-done | bytes 3211296 | tf_op jit(solution)/shard_map/all_to_all | solution.py:418
  193.3 4.4 %finish_parts.1 = (bf16[8,3,128,256]{3,2,1,0:T(8,128)(2,1)}, f32[1,1]{1,0:T(1,128)}) custom-call(s32[16]{0:T(128)S(1)} %reduce_max.18.code_ref, f32[8,3,128,256]{3,2,1,0:T(8,128)S(1)} %get-tuple-element.49.own_ref, bf16[16,784,128]{2,1,0:T(8,128)(2,1)} %all-to-all-done.1.back_ref), custom_call_target="tpu_custom_call" | custom-call | tf_op jit(solution)/shard_map/finish_parts/pallas_call | solution.py:369
  (7 shorter events, 0.1 us)
Async XLA Ops:
  4.2 11.2 %copy-start.3 = (s32[256,3]{0,1:T(4,128)S(1)}, s32[256,3]{0,1:T(4,128)}, u32[]{:S(2)}) copy-start(s32[256,3]{0,1:T(4,128)} %param.6) | copy-start | bytes 9220
  4.2 11.3 %copy-start.4 = (s32[16]{0:T(128)S(1)}, s32[16]{0:T(128)}, u32[]{:S(2)}) copy-start(s32[16]{0:T(128)} %param.9) | copy-start | bytes 196
  4.2 86.1 %copy-start.1 = (bf16[2,128,256]{2,1,0:T(8,128)(2,1)S(1)}, bf16[2,128,256]{2,1,0:T(8,128)(2,1)}, u32[]{:S(2)}) copy-start(bf16[2,128,256]{2,1,0:T(8,128)(2,1)} %proj_ref.5) | copy-start | bytes 393220
  4.2 86.1 %copy-start.2 = (f32[2,256]{1,0:T(2,128)S(1)}, f32[2,256]{1,0:T(2,128)}, u32[]{:S(2)}) copy-start(f32[2,256]{1,0:T(2,128)} %readout_ref.1) | copy-start | bytes 6148
  4.2 86.0 %all-to-all-start = ((bf16[16,3,128,256]{3,2,1,0:T(8,128)(2,1)}), bf16[16,3,128,256]{3,2,1,0:T(8,128)(2,1)S(1)}, u32[]{:S(2)}, u32[]{:S(2)}) async-start(bf16[16,3,128,256]{3,2,1,0:T(8,128)(2,1)} %pick_rows.1), calls=%async_computation | async-start | bytes 6291456 | tf_op jit(solution)/shard_map/all_to_all | solution.py:418
  90.3 1.4 copy-start
  97.8 1.2 collective-permute-start
  99.0 3.7 %collective-permute-start.1 = (f32[16,128]{1,0:T(8,128)S(1)}, f32[16,128]{1,0:T(8,128)S(1)}, u32[]{:S(2)}, u32[]{:S(2)}) collective-permute-start(f32[16,128]{1,0:T(8,128)S(1)} %add.24), channel_id=1, source_target_pairs={{0,2},{1,3},{2,0},{3,1},{4,6},{5,7},{6,4},{7,5},{8,10},{9,11},{10,... | collective-permute-start | bytes 24584 | tf_op jit(solution)/shard_map/ppermute | solution.py:389
  102.7 7.8 %collective-permute-start.4 = (f32[16,128]{1,0:T(8,128)S(1)}, f32[16,128]{1,0:T(8,128)S(1)}, u32[]{:S(2)}, u32[]{:S(2)}) collective-permute-start(f32[16,128]{1,0:T(8,128)S(1)} %add.25), channel_id=1, source_target_pairs={{0,12},{1,13},{2,14},{3,15},{4,0},{5,1},{6,2},{7,3},{8,4},{9,5},{1... | collective-permute-start | bytes 24584 | tf_op jit(solution)/shard_map/ppermute | solution.py:389
  103.1 7.4 %collective-permute-start.3 = (f32[16,128]{1,0:T(8,128)S(1)}, f32[16,128]{1,0:T(8,128)S(1)}, u32[]{:S(2)}, u32[]{:S(2)}) collective-permute-start(f32[16,128]{1,0:T(8,128)S(1)} %add.25), channel_id=1, source_target_pairs={{0,8},{1,9},{2,10},{3,11},{4,12},{5,13},{6,14},{7,15},{8,0},{9,1},... | collective-permute-start | bytes 24584 | tf_op jit(solution)/shard_map/ppermute | solution.py:389
  105.7 4.8 %collective-permute-start.2 = (f32[16,128]{1,0:T(8,128)S(1)}, f32[16,128]{1,0:T(8,128)S(1)}, u32[]{:S(2)}, u32[]{:S(2)}) collective-permute-start(f32[16,128]{1,0:T(8,128)S(1)} %add.25), channel_id=1, source_target_pairs={{0,4},{1,5},{2,6},{3,7},{4,8},{5,9},{6,10},{7,11},{8,12},{9,13},{1... | collective-permute-start | bytes 24584 | tf_op jit(solution)/shard_map/ppermute | solution.py:389
  113.5 79.8 %all-to-all-start.1 = ((bf16[16,784,128]{2,1,0:T(8,128)(2,1)}), bf16[16,784,128]{2,1,0:T(8,128)(2,1)}, u32[]{:S(2)}, u32[]{:S(2)}) async-start(bf16[16,784,128]{2,1,0:T(8,128)(2,1)} %get-tuple-element.50), calls=%async_computation.1 | async-start | bytes 6422528 | tf_op jit(solution)/shard_map/all_to_all | solution.py:418

commit v9 on v8

--- a/solution.py
+++ b/solution.py
@@ -10,6 +10,7 @@
 loss_scale = 8192.0
 VMEM_BYTES = 24 * 1024 * 1024
 LOSS_ROWS = 16
+FORWARD_BYTES = int(24 * 1024 * 1024)
 FINISH_BYTES = 48 * 1024 * 1024
 SECOND_BYTES = 40 * 1024 * 1024
 VMEM_ALL = 60 * 1024 * 1024
@@ -87,8 +88,21 @@
     return units
 
 
-def forward_kernel(group, first_ref, slot_ref, mol_ref, inc_ref, proj_ref, readout_ref, lp_ref, w_ref, dh_ref):
+def forward_kernel(
+    group, first_ref, slot_ref, home_ref, inc_ref, proj_ref, readout_ref, lp_ref, w_ref, dh_ref, mol_ref, sems
+):
     pairs = lp_ref.shape[0]
+    mols = home_ref.shape[0]
+
+    def load(m, part, parts):
+        at = pl.ds(part, parts)
+        return pltpu.make_async_copy(home_ref.at[m, at], mol_ref.at[m, at], sems.at[part, m])
+
+    for part, parts in ((0, 1), (1, 2)):
+        for m in range(mols):
+            load(m, part, parts).start()
+    for m in range(mols):
+        load(m, 0, 1).wait()
     length = mol_ref.shape[2]
     heads, hd, _ = proj_ref.shape
     inv_root = hd ** (-0.5)
@@ -96,31 +110,44 @@
 
     def step(i, carry):
         ids = [i * group + j for j in range(group)]
-        units = load_units(ids, first_ref, slot_ref, mol_ref, inc_ref, heads, hd, (0, 1))
-        scores = [mm(u[4], u[3], 1, 1) for u in units]
-        weights = []
-        for sc in scores:
-            lifted = jnp.exp((sc - jnp.max(sc, axis=0, keepdims=True)) * inv_root)
-            weights.append(lifted * (1.0 / jnp.sum(lifted, axis=0, keepdims=True)))
-        context = [mm(w.astype(BF16), u[5], 0, 0).astype(BF16) for w, u in zip(weights, units)]
-        count = len(units) // heads
+        units, weights, context = [], [], []
+        for direction in (0, 1):
+            if direction == 1:
+
+                @pl.when(i == 0)
+                def land():
+                    for m in range(mols):
+                        load(m, 1, 2).wait()
+
+            here = load_units(ids, first_ref, slot_ref, mol_ref, inc_ref, heads, hd, (direction,))
+            scores = [mm(u[4], u[3], 1, 1) for u in here]
+            fresh = []
+            for sc in scores:
+                lifted = jnp.exp((sc - jnp.max(sc, axis=0, keepdims=True)) * inv_root)
+                fresh.append(lifted * (1.0 / jnp.sum(lifted, axis=0, keepdims=True)))
+            context.append([mm(w.astype(BF16), u[5], 0, 0).astype(BF16) for w, u in zip(fresh, here)])
+            units.append(here)
+            weights.append(fresh)
         totals = [None] * group
         dhidden = []
         for h in range(heads):
-            hidden = mm(jnp.concatenate(context[h * count : (h + 1) * count], axis=0), proj_ref[h], 1, 0)
+            mine = [context[d][h * group + j] for d in (0, 1) for j in range(group)]
+            hidden = mm(jnp.concatenate(mine, axis=0), proj_ref[h], 1, 0)
             sig = 0.5 + 0.5 * jnp.tanh(0.5 * hidden)
             act = hidden * sig
-            for j in range(group):
-                rows = jnp.sum(act[2 * j * length : (2 * j + 2) * length], axis=0, keepdims=True) * readouts[h]
+            for n in range(2 * group):
+                rows = jnp.sum(act[n * length : (n + 1) * length], axis=0, keepdims=True) * readouts[h]
+                j = n % group
                 totals[j] = rows if totals[j] is None else totals[j] + rows
             dhidden.append(((sig + act * (1.0 - sig)) * readouts[h]).astype(BF16))
         for j, p in enumerate(ids):
             total = jnp.sum(totals[j], axis=1, keepdims=True)
             lp_ref[pl.ds(p, 1), :] = jnp.broadcast_to(total, (1, lp_ref.shape[1]))
-        for n, (j, d, h, *_) in enumerate(units):
-            at = n - h * count
-            w_ref[d, ids[j], h] = weights[n]
-            dh_ref[d, ids[j], h] = dhidden[h][at * length : (at + 1) * length]
+        for d in (0, 1):
+            for n, (j, _, h, *_) in enumerate(units[d]):
+                at = d * group + j
+                w_ref[d, ids[j], h] = weights[d][n]
+                dh_ref[d, ids[j], h] = dhidden[h][at * length : (at + 1) * length]
         return carry
 
     lax.fori_loop(0, pairs // group, step, 0)
@@ -136,10 +163,12 @@
             jax.ShapeDtypeStruct((pairs, 128), F32),
             jax.ShapeDtypeStruct((2, pairs, heads, length, length), F32),
             jax.ShapeDtypeStruct((2, pairs, heads, length, width), BF16),
+            jax.ShapeDtypeStruct(mol.shape, mol.dtype),
         ),
-        in_specs=[SMEM_SPEC] * 2 + [VMEM_SPEC] * 4,
-        out_specs=(VMEM_SPEC,) * 3,
-        compiler_params=params(),
+        in_specs=[SMEM_SPEC] * 2 + [HBM_SPEC] + [VMEM_SPEC] * 3,
+        out_specs=(VMEM_SPEC,) * 4,
+        scratch_shapes=[pltpu.SemaphoreType.DMA((2, mol.shape[0]))],
+        compiler_params=params(FORWARD_BYTES),
         name="pair_forward",
     )(first, slot, mol, inc, proj, readout)
 
@@ -440,12 +469,12 @@
 
     inc = exchange(pick(pair_list.T, mol, groups))
     inc, lead, mate, target_wide = lax.optimization_barrier((inc, lead, mate, target_wide))
-    part, weights, dhidden = forward(first, slot, mol, inc, head_proj, head_out)
+    part, weights, dhidden, near = forward(first, slot, pltpu.with_memory_space_constraint(mol, pltpu.HBM), inc, head_proj, head_out)
 
     def grads(direction):
         def work(after):
             index, _ = lax.optimization_barrier((first, after))
-            return backward(direction, index, slot, mol, inc, head_proj, weights, dhidden)
+            return backward(direction, index, slot, near, inc, head_proj, weights, dhidden)
 
         return work
 

time: 198 us -> 199 us (level)
  no operation moved by 1% of the time
where the time goes in v9:
time: 199 us; the launch traced here: 198 us
  waiting for transfers between devices  150 us (75%)
  Pallas kernels  24.5 us (12%)
  starting transfers between devices  21.2 us (11%)
    all_to_all x2, waiting for transfers between devices, exchange(): lax.all_to_all(value, 'group', split_axis=0, concat_axis=0, tiled=True)  149 us
    all_to_all x2, starting transfers between devices, exchange(): lax.all_to_all(value, 'group', split_axis=0, concat_axis=0, tiled=True)  15.6 us
    pallas_call x1, Pallas kernels, forward(): pl.pallas_call(functools.partial(forward_kernel, min(16, pairs)), out_sha...  7.73 us
    pallas_call x2, Pallas kernels, backward(): pl.pallas_call(functools.partial(backward_kernel, direction, min(16, pair...  5.86 us
    ppermute x5, starting transfers between devices, hop(): return lax.ppermute(value, axis, [(i, change(i)) for i in range(size)])  5.6 us
    pallas_call x1, Pallas kernels, finish(): pl.pallas_call(functools.partial(finish_kernel, scale), out_shape=(jax.Sh...  4.4 us
  transfers between devices with their start and end apart: 7, of which 4 were waited for; matrix products, arithmetic and copies ran while one was open for 1% of the time, Pallas kernels for 3%

profile of v9, /device:TPU:8, one launch (start us, length us, event | category | flops | bytes accessed | tf_op | source)
XLA Modules:
  0.0 198.4 jit_solution(6336363271376805023)
XLA Ops:
  0.6 3.6 %pick_rows.1 = bf16[16,3,128,256]{3,2,1,0:T(8,128)(2,1)} custom-call(s32[3,256]{1,0:T(4,128)} %bitcast.10, bf16[8,3,128,256]{3,2,1,0:T(8,128)(2,1)} %bitcast.8), custom_call_target="tpu_custom_call" | custom-call | tf_op jit(solution)/shard_map/pick_rows/pallas_call | solution.py:61
  4.3 0.0 copy-start.2
  4.3 0.0 copy-start.3
  4.3 0.0 copy-start
  4.3 0.0 copy-start.1
  4.3 11.1 %all-to-all-start = ((bf16[16,3,128,256]{3,2,1,0:T(8,128)(2,1)}), bf16[16,3,128,256]{3,2,1,0:T(8,128)(2,1)S(1)}, u32[]{:S(2)}, u32[]{:S(2)}) async-start(bf16[16,3,128,256]{3,2,1,0:T(8,128)(2,1)} %pick_rows.1), calls=%async_computation | async-start | bytes 6291456 | tf_op jit(solution)/shard_map/all_to_all | solution.py:447
  15.4 0.0 copy-done.2
  15.5 0.1 reshape.28
  15.5 0.0 copy-done.3
  15.6 0.2 fusion.1
  15.8 0.2 select_reduce_fusion.mate_ref
  15.9 74.4 %all-to-all-done.inc_ref = bf16[16,3,128,256]{3,2,1,0:T(8,128)(2,1)S(1)} async-done(((bf16[16,3,128,256]{3,2,1,0:T(8,128)(2,1)}), bf16[16,3,128,256]{3,2,1,0:T(8,128)(2,1)S(1)}, u32[]{:S(2)}, u32[]{:S(2)}) %all-to-all-start) | async-done | bytes 3145760 | tf_op jit(solution)/shard_map/all_to_all | solution.py:447
  90.4 0.1 broadcast_in_dim.18.target_ref
  90.4 0.0 copy-done
  90.4 0.0 copy-done.1
  90.4 7.7 %pair_forward.1 = (f32[16,128]{1,0:T(8,128)S(1)}, f32[2,16,2,128,128]{4,3,2,1,0:T(8,128)S(1)}, bf16[2,16,2,128,256]{4,3,2,1,0:T(8,128)(2,1)S(1)}, bf16[8,3,128,256]{3,2,1,0:T(8,128)(2,1)S(1)}) custom-call(s32[16]{0:T(128)S(1)} %get-tuple-element.40.first_ref, s32[16]{0:T(128)S(1)} %get-tuple-element.57.slot_ref, bf16[8,3,128,256]{3,2,1,0:T(8,128)(2,1)} %bitcast.9, ...), custom_call_target="tpu_custom_call" | custom-call | tf_op jit(solution)/shard_map/pair_forward/pallas_call | solution.py:160
  98.2 0.1 collective-permute-start
  98.3 1.2 collective-permute-done
  99.4 0.6 collective-permute-start.1
  100.0 2.9 %pair_backward.2 = (bf16[16,128,256]{2,1,0:T(8,128)(2,1)S(1)}, bf16[16,2,128,256]{3,2,1,0:T(8,128)(2,1)S(1)}) custom-call(s32[16]{0:T(128)S(1)} %get-tuple-element.40.first_ref, s32[16]{0:T(128)S(1)} %get-tuple-element.57.slot_ref, bf16[8,3,128,256]{3,2,1,0:T(8,128)(2,1)S(1)} %get-tuple-element.34.mol_ref, ...), custom_call_target="tpu_custom_call" | custom-call | tf_op jit(solution)/shard_map/pair_backward/pallas_call | solution.py:212
  103.0 0.1 collective-permute-done.1
  103.1 0.4 collective-permute-start.4
  103.5 2.6 %collective-permute-start.3 = (f32[16,128]{1,0:T(8,128)S(1)}, f32[16,128]{1,0:T(8,128)S(1)}, u32[]{:S(2)}, u32[]{:S(2)}) collective-permute-start(f32[16,128]{1,0:T(8,128)S(1)} %add.25), channel_id=1, source_target_pairs={{0,8},{1,9},{2,10},{3,11},{4,12},{5,13},{6,14},{7,15},{8,0},{9,1},... | collective-permute-start | bytes 24584 | tf_op jit(solution)/shard_map/ppermute | solution.py:418
  106.1 1.9 collective-permute-start.2
  108.0 2.9 %pair_backward.3 = (bf16[16,128,256]{2,1,0:T(8,128)(2,1)S(1)}, bf16[16,2,128,256]{3,2,1,0:T(8,128)(2,1)S(1)}) custom-call(s32[16]{0:T(128)S(1)} %get-tuple-element.40.first_ref, s32[16]{0:T(128)S(1)} %get-tuple-element.57.slot_ref, bf16[8,3,128,256]{3,2,1,0:T(8,128)(2,1)S(1)} %get-tuple-element.34.mol_ref, ...), custom_call_target="tpu_custom_call" | custom-call | tf_op jit(solution)/shard_map/pair_backward/pallas_call | solution.py:212
  110.9 0.0 collective-permute-done.4
  111.0 0.0 collective-permute-done.3
  111.0 0.0 collective-permute-done.2
  111.0 2.9 %scaled_terms.1 = (bf16[16,784,128]{2,1,0:T(8,128)(2,1)}, f32[8,3,128,256]{3,2,1,0:T(8,128)S(1)}) custom-call(s32[16]{0:T(128)S(1)} %get-tuple-element.40.first_ref, s32[16]{0:T(128)S(1)} %get-tuple-element.57.slot_ref, s32[16]{0:T(128)S(1)} %not_convert_fusion.lead_ref, s32[16]{0:T(128)S(1)} %select_reduce_fusion.mate_ref, ...), custom_call_target="tpu_custom_call" | custom-call | tf_op jit(solution)/shard_map/scaled_terms/pallas_call | solution.py:334
  113.9 4.5 %all-to-all-start.1 = ((bf16[16,784,128]{2,1,0:T(8,128)(2,1)}), bf16[16,784,128]{2,1,0:T(8,128)(2,1)}, u32[]{:S(2)}, u32[]{:S(2)}) async-start(bf16[16,784,128]{2,1,0:T(8,128)(2,1)} %get-tuple-element.52), calls=%async_computation.1 | async-start | bytes 6422528 | tf_op jit(solution)/shard_map/all_to_all | solution.py:447
  118.4 0.1 select_n.24
  118.5 0.1 reduce_max.18.code_ref
  118.6 0.6 slice_reduce_fusion
  119.2 74.6 %all-to-all-done.1.back_ref = bf16[16,784,128]{2,1,0:T(8,128)(2,1)} async-done(((bf16[16,784,128]{2,1,0:T(8,128)(2,1)}), bf16[16,784,128]{2,1,0:T(8,128)(2,1)}, u32[]{:S(2)}, u32[]{:S(2)}) %all-to-all-start.1) | async-done | bytes 3211296 | tf_op jit(solution)/shard_map/all_to_all | solution.py:447
  193.8 4.4 %finish_parts.1 = (bf16[8,3,128,256]{3,2,1,0:T(8,128)(2,1)}, f32[1,1]{1,0:T(1,128)}) custom-call(s32[16]{0:T(128)S(1)} %reduce_max.18.code_ref, f32[8,3,128,256]{3,2,1,0:T(8,128)S(1)} %get-tuple-element.51.own_ref, bf16[16,784,128]{2,1,0:T(8,128)(2,1)} %all-to-all-done.1.back_ref), custom_call_target="tpu_custom_call" | custom-call | tf_op jit(solution)/shard_map/finish_parts/pallas_call | solution.py:398
  (7 shorter events, 0.1 us)
Async XLA Ops:
  4.3 11.2 %copy-start.2 = (s32[256,3]{0,1:T(4,128)S(1)}, s32[256,3]{0,1:T(4,128)}, u32[]{:S(2)}) copy-start(s32[256,3]{0,1:T(4,128)} %param.6) | copy-start | bytes 9220
  4.3 11.3 %copy-start.3 = (s32[16]{0:T(128)S(1)}, s32[16]{0:T(128)}, u32[]{:S(2)}) copy-start(s32[16]{0:T(128)} %param.9) | copy-start | bytes 196
  4.3 86.1 %copy-start = (bf16[2,128,256]{2,1,0:T(8,128)(2,1)S(1)}, bf16[2,128,256]{2,1,0:T(8,128)(2,1)}, u32[]{:S(2)}) copy-start(bf16[2,128,256]{2,1,0:T(8,128)(2,1)} %proj_ref.5) | copy-start | bytes 393220
  4.3 86.1 %copy-start.1 = (f32[2,256]{1,0:T(2,128)S(1)}, f32[2,256]{1,0:T(2,128)}, u32[]{:S(2)}) copy-start(f32[2,256]{1,0:T(2,128)} %readout_ref.1) | copy-start | bytes 6148
  4.3 86.0 %all-to-all-start = ((bf16[16,3,128,256]{3,2,1,0:T(8,128)(2,1)}), bf16[16,3,128,256]{3,2,1,0:T(8,128)(2,1)S(1)}, u32[]{:S(2)}, u32[]{:S(2)}) async-start(bf16[16,3,128,256]{3,2,1,0:T(8,128)(2,1)} %pick_rows.1), calls=%async_computation | async-start | bytes 6291456 | tf_op jit(solution)/shard_map/all_to_all | solution.py:447
  98.2 1.3 collective-permute-start
  99.4 3.7 %collective-permute-start.1 = (f32[16,128]{1,0:T(8,128)S(1)}, f32[16,128]{1,0:T(8,128)S(1)}, u32[]{:S(2)}, u32[]{:S(2)}) collective-permute-start(f32[16,128]{1,0:T(8,128)S(1)} %add.24), channel_id=1, source_target_pairs={{0,2},{1,3},{2,0},{3,1},{4,6},{5,7},{6,4},{7,5},{8,10},{9,11},{10,... | collective-permute-start | bytes 24584 | tf_op jit(solution)/shard_map/ppermute | solution.py:418
  103.1 7.9 %collective-permute-start.4 = (f32[16,128]{1,0:T(8,128)S(1)}, f32[16,128]{1,0:T(8,128)S(1)}, u32[]{:S(2)}, u32[]{:S(2)}) collective-permute-start(f32[16,128]{1,0:T(8,128)S(1)} %add.25), channel_id=1, source_target_pairs={{0,12},{1,13},{2,14},{3,15},{4,0},{5,1},{6,2},{7,3},{8,4},{9,5},{1... | collective-permute-start | bytes 24584 | tf_op jit(solution)/shard_map/ppermute | solution.py:418
  103.5 7.4 %collective-permute-start.3 = (f32[16,128]{1,0:T(8,128)S(1)}, f32[16,128]{1,0:T(8,128)S(1)}, u32[]{:S(2)}, u32[]{:S(2)}) collective-permute-start(f32[16,128]{1,0:T(8,128)S(1)} %add.25), channel_id=1, source_target_pairs={{0,8},{1,9},{2,10},{3,11},{4,12},{5,13},{6,14},{7,15},{8,0},{9,1},... | collective-permute-start | bytes 24584 | tf_op jit(solution)/shard_map/ppermute | solution.py:418
  106.1 4.8 %collective-permute-start.2 = (f32[16,128]{1,0:T(8,128)S(1)}, f32[16,128]{1,0:T(8,128)S(1)}, u32[]{:S(2)}, u32[]{:S(2)}) collective-permute-start(f32[16,128]{1,0:T(8,128)S(1)} %add.25), channel_id=1, source_target_pairs={{0,4},{1,5},{2,6},{3,7},{4,8},{5,9},{6,10},{7,11},{8,12},{9,13},{1... | collective-permute-start | bytes 24584 | tf_op jit(solution)/shard_map/ppermute | solution.py:418
  113.9 80.0 %all-to-all-start.1 = ((bf16[16,784,128]{2,1,0:T(8,128)(2,1)}), bf16[16,784,128]{2,1,0:T(8,128)(2,1)}, u32[]{:S(2)}, u32[]{:S(2)}) async-start(bf16[16,784,128]{2,1,0:T(8,128)(2,1)} %get-tuple-element.52), calls=%async_computation.1 | async-start | bytes 6422528 | tf_op jit(solution)/shard_map/all_to_all | solution.py:447

commit v10 on v8

--- a/solution.py
+++ b/solution.py
@@ -101,8 +101,8 @@
         weights = []
         for sc in scores:
             lifted = jnp.exp((sc - jnp.max(sc, axis=0, keepdims=True)) * inv_root)
-            weights.append(lifted * (1.0 / jnp.sum(lifted, axis=0, keepdims=True)))
-        context = [mm(w.astype(BF16), u[5], 0, 0).astype(BF16) for w, u in zip(weights, units)]
+            weights.append((lifted * (1.0 / jnp.sum(lifted, axis=0, keepdims=True))).astype(BF16))
+        context = [mm(w, u[5], 0, 0).astype(BF16) for w, u in zip(weights, units)]
         count = len(units) // heads
         totals = [None] * group
         dhidden = []
@@ -134,7 +134,7 @@
         functools.partial(forward_kernel, min(16, pairs)),
         out_shape=(
             jax.ShapeDtypeStruct((pairs, 128), F32),
-            jax.ShapeDtypeStruct((2, pairs, heads, length, length), F32),
+            jax.ShapeDtypeStruct((2, pairs, heads, length, length), BF16),
             jax.ShapeDtypeStruct((2, pairs, heads, length, width), BF16),
         ),
         in_specs=[SMEM_SPEC] * 2 + [VMEM_SPEC] * 4,
@@ -158,10 +158,11 @@
             dhidden = jnp.concatenate([dh_ref[0, p, h] for p in ids], axis=0)
             whole = mm(dhidden, proj_ref[h], 1, 1).astype(BF16)
             dcontext += [whole[j * length : (j + 1) * length] for j in range(group)]
-        dvalues = [mm(w.astype(BF16), dc, 1, 0).astype(BF16) for w, dc in zip(weights, dcontext)]
+        dvalues = [mm(w, dc, 1, 0).astype(BF16) for w, dc in zip(weights, dcontext)]
         dweights = [mm(u[5], dc, 1, 1) for u, dc in zip(units, dcontext)]
         dscores = []
         for w, dw in zip(weights, dweights):
+            w = w.astype(F32)
             inner = jnp.sum(dw * w, axis=0, keepdims=True)
             dscores.append((w * (dw - inner) * inv_root).astype(BF16))
         dqueries = [mm(ds, u[4], 0, 0).astype(BF16) for ds, u in zip(dscores, units)]

time: 198 us -> 198 us (level)
  no operation moved by 1% of the time
where the time goes in v10:
time: 198 us
  waiting for transfers between devices  150 us (76%)
  Pallas kernels  22.8 us (12%)
  starting transfers between devices  21.2 us (11%)
  local copies, waits for them, and re-layouts  2.31 us (1%)
    all_to_all x2, waiting for transfers between devices, exchange(): lax.all_to_all(value, 'group', split_axis=0, concat_axis=0, tiled=True)  149 us
    all_to_all x2, starting transfers between devices, exchange(): lax.all_to_all(value, 'group', split_axis=0, concat_axis=0, tiled=True)  15.7 us
    pallas_call x1, Pallas kernels, forward(): pl.pallas_call(functools.partial(forward_kernel, min(16, pairs)), out_sha...  6.07 us
    pallas_call x2, Pallas kernels, backward(): pl.pallas_call(functools.partial(backward_kernel, direction, min(16, pair...  5.84 us
    ppermute x5, starting transfers between devices, hop(): return lax.ppermute(value, axis, [(i, change(i)) for i in range(size)])  5.52 us
    pallas_call x1, Pallas kernels, finish(): pl.pallas_call(functools.partial(finish_kernel, scale), out_shape=(jax.Sh...  4.35 us
  transfers between devices with their start and end apart: 7, of which 4 were waited for; matrix products, arithmetic and copies ran while one was open for 1% of the time, Pallas kernels for 3%

profile of v10, /device:TPU:8, one launch (start us, length us, event | category | flops | bytes accessed | tf_op | source)
XLA Modules:
  0.0 198.0 jit_solution(4757912047686753556)
XLA Ops:
  0.6 3.5 %pick_rows.1 = bf16[16,3,128,256]{3,2,1,0:T(8,128)(2,1)} custom-call(s32[3,256]{1,0:T(4,128)} %bitcast.12, bf16[8,3,128,256]{3,2,1,0:T(8,128)(2,1)} %bitcast.8), custom_call_target="tpu_custom_call" | custom-call | tf_op jit(solution)/shard_map/pick_rows/pallas_call | solution.py:60
  4.2 0.0 copy-start.3
  4.2 0.0 copy-start.4
  4.2 0.0 copy-start.1
  4.2 0.0 copy-start.2
  4.2 11.2 %all-to-all-start = ((bf16[16,3,128,256]{3,2,1,0:T(8,128)(2,1)}), bf16[16,3,128,256]{3,2,1,0:T(8,128)(2,1)S(1)}, u32[]{:S(2)}, u32[]{:S(2)}) async-start(bf16[16,3,128,256]{3,2,1,0:T(8,128)(2,1)} %pick_rows.1), calls=%async_computation | async-start | bytes 6291456 | tf_op jit(solution)/shard_map/all_to_all | solution.py:419
  15.4 0.0 copy-done.3
  15.4 0.1 reshape.28
  15.5 0.0 copy-done.4
  15.5 0.2 fusion.1
  15.7 0.2 select_reduce_fusion.mate_ref
  15.9 74.4 %all-to-all-done.inc_ref = bf16[16,3,128,256]{3,2,1,0:T(8,128)(2,1)S(1)} async-done(((bf16[16,3,128,256]{3,2,1,0:T(8,128)(2,1)}), bf16[16,3,128,256]{3,2,1,0:T(8,128)(2,1)S(1)}, u32[]{:S(2)}, u32[]{:S(2)}) %all-to-all-start) | async-done | bytes 3145760 | tf_op jit(solution)/shard_map/all_to_all | solution.py:419
  90.3 0.1 broadcast_in_dim.18.target_ref
  90.4 0.0 copy-done.1
  90.4 0.0 copy-done.2
  90.4 0.0 copy-start
  90.4 1.4 copy-done
  91.8 6.1 %pair_forward.1 = (f32[16,128]{1,0:T(8,128)S(1)}, bf16[2,16,2,128,128]{4,3,2,1,0:T(8,128)(2,1)S(1)}, bf16[2,16,2,128,256]{4,3,2,1,0:T(8,128)(2,1)S(1)}) custom-call(s32[16]{0:T(128)S(1)} %get-tuple-element.38.first_ref, s32[16]{0:T(128)S(1)} %get-tuple-element.55.slot_ref, bf16[8,3,128,256]{3,2,1,0:T(8,128)(2,1)S(1)} %bitcast.9, ...), custom_call_target="tpu_custom_call" | custom-call | tf_op jit(solution)/shard_map/pair_forward/pallas_call | solution.py:133
  97.9 0.0 collective-permute-start
  97.9 1.2 collective-permute-done
  99.1 0.6 collective-permute-start.1
  99.7 2.9 %pair_backward.2 = (bf16[16,128,256]{2,1,0:T(8,128)(2,1)S(1)}, bf16[16,2,128,256]{3,2,1,0:T(8,128)(2,1)S(1)}) custom-call(s32[16]{0:T(128)S(1)} %get-tuple-element.38.first_ref, s32[16]{0:T(128)S(1)} %get-tuple-element.55.slot_ref, bf16[8,3,128,256]{3,2,1,0:T(8,128)(2,1)S(1)} %bitcast.10, bf16[16,3,128,256]{3,2,1,0:T(8,128)(2,1)S(1)} %all-to-all-done.inc_ref, ...), custom_call_target="tpu_custom_call" | custom-call | tf_op jit(solution)/shard_map/pair_backward/pallas_call | solution.py:184
  102.6 0.1 collective-permute-done.1
  102.7 0.4 collective-permute-start.4
  103.2 2.6 %collective-permute-start.3 = (f32[16,128]{1,0:T(8,128)S(1)}, f32[16,128]{1,0:T(8,128)S(1)}, u32[]{:S(2)}, u32[]{:S(2)}) collective-permute-start(f32[16,128]{1,0:T(8,128)S(1)} %add.25), channel_id=1, source_target_pairs={{0,8},{1,9},{2,10},{3,11},{4,12},{5,13},{6,14},{7,15},{8,0},{9,1},... | collective-permute-start | bytes 24584 | tf_op jit(solution)/shard_map/ppermute | solution.py:390
  105.8 1.9 collective-permute-start.2
  107.7 2.9 %pair_backward.3 = (bf16[16,128,256]{2,1,0:T(8,128)(2,1)S(1)}, bf16[16,2,128,256]{3,2,1,0:T(8,128)(2,1)S(1)}) custom-call(s32[16]{0:T(128)S(1)} %get-tuple-element.38.first_ref, s32[16]{0:T(128)S(1)} %get-tuple-element.55.slot_ref, bf16[8,3,128,256]{3,2,1,0:T(8,128)(2,1)S(1)} %bitcast.11, bf16[16,3,128,256]{3,2,1,0:T(8,128)(2,1)S(1)} %all-to-all-done.inc_ref, ...), custom_call_target="tpu_custom_call" | custom-call | tf_op jit(solution)/shard_map/pair_backward/pallas_call | solution.py:184
  110.6 0.0 collective-permute-done.4
  110.6 0.0 collective-permute-done.3
  110.6 0.0 collective-permute-done.2
  110.6 3.0 %scaled_terms.1 = (bf16[16,784,128]{2,1,0:T(8,128)(2,1)}, f32[8,3,128,256]{3,2,1,0:T(8,128)S(1)}) custom-call(s32[16]{0:T(128)S(1)} %get-tuple-element.38.first_ref, s32[16]{0:T(128)S(1)} %get-tuple-element.55.slot_ref, s32[16]{0:T(128)S(1)} %not_convert_fusion.lead_ref, s32[16]{0:T(128)S(1)} %select_reduce_fusion.mate_ref, ...), custom_call_target="tpu_custom_call" | custom-call | tf_op jit(solution)/shard_map/scaled_terms/pallas_call | solution.py:306
  113.6 4.5 %all-to-all-start.1 = ((bf16[16,784,128]{2,1,0:T(8,128)(2,1)}), bf16[16,784,128]{2,1,0:T(8,128)(2,1)}, u32[]{:S(2)}, u32[]{:S(2)}) async-start(bf16[16,784,128]{2,1,0:T(8,128)(2,1)} %get-tuple-element.50), calls=%async_computation.1 | async-start | bytes 6422528 | tf_op jit(solution)/shard_map/all_to_all | solution.py:419
  118.1 0.1 select_n.24
  118.2 0.1 reduce_max.18.code_ref
  118.3 0.6 slice_reduce_fusion
  119.0 74.6 %all-to-all-done.1.back_ref = bf16[16,784,128]{2,1,0:T(8,128)(2,1)} async-done(((bf16[16,784,128]{2,1,0:T(8,128)(2,1)}), bf16[16,784,128]{2,1,0:T(8,128)(2,1)}, u32[]{:S(2)}, u32[]{:S(2)}) %all-to-all-start.1) | async-done | bytes 3211296 | tf_op jit(solution)/shard_map/all_to_all | solution.py:419
  193.5 4.4 %finish_parts.1 = (bf16[8,3,128,256]{3,2,1,0:T(8,128)(2,1)}, f32[1,1]{1,0:T(1,128)}) custom-call(s32[16]{0:T(128)S(1)} %reduce_max.18.code_ref, f32[8,3,128,256]{3,2,1,0:T(8,128)S(1)} %get-tuple-element.49.own_ref, bf16[16,784,128]{2,1,0:T(8,128)(2,1)} %all-to-all-done.1.back_ref), custom_call_target="tpu_custom_call" | custom-call | tf_op jit(solution)/shard_map/finish_parts/pallas_call | solution.py:370
  (7 shorter events, 0.1 us)
Async XLA Ops:
  4.2 11.2 %copy-start.3 = (s32[256,3]{0,1:T(4,128)S(1)}, s32[256,3]{0,1:T(4,128)}, u32[]{:S(2)}) copy-start(s32[256,3]{0,1:T(4,128)} %param.6) | copy-start | bytes 9220
  4.2 11.3 %copy-start.4 = (s32[16]{0:T(128)S(1)}, s32[16]{0:T(128)}, u32[]{:S(2)}) copy-start(s32[16]{0:T(128)} %param.9) | copy-start | bytes 196
  4.2 86.2 %copy-start.1 = (bf16[2,128,256]{2,1,0:T(8,128)(2,1)S(1)}, bf16[2,128,256]{2,1,0:T(8,128)(2,1)}, u32[]{:S(2)}) copy-start(bf16[2,128,256]{2,1,0:T(8,128)(2,1)} %proj_ref.5) | copy-start | bytes 393220
  4.2 86.2 %copy-start.2 = (f32[2,256]{1,0:T(2,128)S(1)}, f32[2,256]{1,0:T(2,128)}, u32[]{:S(2)}) copy-start(f32[2,256]{1,0:T(2,128)} %readout_ref.1) | copy-start | bytes 6148
  4.2 86.1 %all-to-all-start = ((bf16[16,3,128,256]{3,2,1,0:T(8,128)(2,1)}), bf16[16,3,128,256]{3,2,1,0:T(8,128)(2,1)S(1)}, u32[]{:S(2)}, u32[]{:S(2)}) async-start(bf16[16,3,128,256]{3,2,1,0:T(8,128)(2,1)} %pick_rows.1), calls=%async_computation | async-start | bytes 6291456 | tf_op jit(solution)/shard_map/all_to_all | solution.py:419
  90.4 1.4 copy-start
  97.9 1.2 collective-permute-start
  99.1 3.7 %collective-permute-start.1 = (f32[16,128]{1,0:T(8,128)S(1)}, f32[16,128]{1,0:T(8,128)S(1)}, u32[]{:S(2)}, u32[]{:S(2)}) collective-permute-start(f32[16,128]{1,0:T(8,128)S(1)} %add.24), channel_id=1, source_target_pairs={{0,2},{1,3},{2,0},{3,1},{4,6},{5,7},{6,4},{7,5},{8,10},{9,11},{10,... | collective-permute-start | bytes 24584 | tf_op jit(solution)/shard_map/ppermute | solution.py:390
  102.7 7.8 %collective-permute-start.4 = (f32[16,128]{1,0:T(8,128)S(1)}, f32[16,128]{1,0:T(8,128)S(1)}, u32[]{:S(2)}, u32[]{:S(2)}) collective-permute-start(f32[16,128]{1,0:T(8,128)S(1)} %add.25), channel_id=1, source_target_pairs={{0,12},{1,13},{2,14},{3,15},{4,0},{5,1},{6,2},{7,3},{8,4},{9,5},{1... | collective-permute-start | bytes 24584 | tf_op jit(solution)/shard_map/ppermute | solution.py:390
  103.2 7.4 %collective-permute-start.3 = (f32[16,128]{1,0:T(8,128)S(1)}, f32[16,128]{1,0:T(8,128)S(1)}, u32[]{:S(2)}, u32[]{:S(2)}) collective-permute-start(f32[16,128]{1,0:T(8,128)S(1)} %add.25), channel_id=1, source_target_pairs={{0,8},{1,9},{2,10},{3,11},{4,12},{5,13},{6,14},{7,15},{8,0},{9,1},... | collective-permute-start | bytes 24584 | tf_op jit(solution)/shard_map/ppermute | solution.py:390
  105.8 4.8 %collective-permute-start.2 = (f32[16,128]{1,0:T(8,128)S(1)}, f32[16,128]{1,0:T(8,128)S(1)}, u32[]{:S(2)}, u32[]{:S(2)}) collective-permute-start(f32[16,128]{1,0:T(8,128)S(1)} %add.25), channel_id=1, source_target_pairs={{0,4},{1,5},{2,6},{3,7},{4,8},{5,9},{6,10},{7,11},{8,12},{9,13},{1... | collective-permute-start | bytes 24584 | tf_op jit(solution)/shard_map/ppermute | solution.py:390
  113.6 79.9 %all-to-all-start.1 = ((bf16[16,784,128]{2,1,0:T(8,128)(2,1)}), bf16[16,784,128]{2,1,0:T(8,128)(2,1)}, u32[]{:S(2)}, u32[]{:S(2)}) async-start(bf16[16,784,128]{2,1,0:T(8,128)(2,1)} %get-tuple-element.50), calls=%async_computation.1 | async-start | bytes 6422528 | tf_op jit(solution)/shard_map/all_to_all | solution.py:419
